TPU v7x, 512 devices: a whole 4x8x8 slice. The times are simulated.
512 devices in a mesh: mem: 16 (over z, y_lo), lon: 32 (over y_hi, x, core).
Axes of the slice: x: 4, y: 8 (y_hi: 4, y_lo: 2; y = y_hi * 2 + y_lo), z: 8, core: 2. Of those that a mesh axis runs over, the one named last changes fastest.
Arguments:
- fields: bfloat16 [80, 64, 256, 128], P('mem', None, 'lon'), may hold values from -8 to 8
- w_query: bfloat16 [24, 576], replicated, may hold values from -1 to 1
- w_key: bfloat16 [24, 576], replicated, may hold values from -1 to 1
- w_value: bfloat16 [24, 576], replicated, may hold values from -0.25 to 0.25
- w_out: bfloat16 [64, 216], replicated, may hold values from -1.25 to 1.25
Outputs:
- updated: bfloat16 [80, 64, 256, 128], P('mem', None, 'lon')
All inputs are finite; a program needn't handle non-finite values.
Results may differ from a plain program's by a relative error of at most 0.008.
Values may be sent and summed in bfloat16 or wider, within the bound.
No kernel may reach another device: no remote copies, remote signals or barrier semaphores. Data moves between devices by JAX's collectives and lax.ppermute only.
A program may use at most 64 MiB of HBM per device.

v0:
```python
import math

import jax
import jax.numpy as jnp
from jax import lax
from jax.sharding import PartitionSpec as P


def with_halo(block, sides, width):
    for axis, dim in sides:
        count = lax.axis_size(axis)
        forward = [(i, i + 1) for i in range(count - 1)]
        forward.append((count - 1, 0))
        backward = [(target, source) for source, target in forward]
        low = lax.ppermute(
            lax.slice_in_dim(block, block.shape[dim] - width, None, axis=dim), axis, forward
        )
        high = lax.ppermute(lax.slice_in_dim(block, 0, width, axis=dim), axis, backward)
        block = jnp.concatenate([low, block, high], axis=dim)
    return block


def tap_stack(extended):
    span_lon = extended.shape[2] - 2
    latitudes = extended.shape[3]
    padded = jnp.pad(extended, ((0, 0), (0, 0), (0, 0), (1, 1)))
    return jnp.concatenate(
        [
            padded[:, :, lon_step : lon_step + span_lon, lat_step : lat_step + latitudes]
            for lon_step in range(3)
            for lat_step in range(3)
        ],
        axis=1,
    )


def shards(fields, w_query, w_key, w_value, w_out):
    members = fields.shape[0]
    longitudes = fields.shape[2]
    latitudes = fields.shape[3]
    inner_width = w_query.shape[0]
    extended = with_halo(fields, (("lon", 2),), 1)
    w_inner = jnp.concatenate([w_query, w_key, w_value], axis=0)
    projected = jnp.einsum(
        "oc,mcwh->mowh", w_inner, tap_stack(extended), preferred_element_type=jnp.float32
    ).astype(jnp.bfloat16)
    queries = projected[:, :inner_width]
    keys_local = projected[:, inner_width : 2 * inner_width]
    values = projected[:, 2 * inner_width :]
    query_blocks, key_blocks = (
        lax.all_to_all(queries, "mem", split_axis=3, concat_axis=0, tiled=True),
        lax.all_to_all(keys_local, "mem", split_axis=3, concat_axis=0, tiled=True),
    )
    total_members = query_blocks.shape[0]
    partial_value = jnp.dot(
        query_blocks.reshape(total_members, -1),
        key_blocks.reshape(total_members, -1).T,
        preferred_element_type=jnp.float32,
    )
    score_scale = 1.0 / math.sqrt(inner_width * latitudes * longitudes * lax.axis_size("lon"))
    first_row = lax.axis_index("mem") * members
    gram_sums = lax.psum(partial_value, ("mem", "lon"))
    weights_all = jax.nn.softmax(gram_sums * score_scale, axis=1).astype(jnp.bfloat16)
    weights_own = lax.dynamic_slice_in_dim(weights_all, first_row, members, 0)
    mixed_values = jnp.einsum(
        "mn,ncwh->mcwh",
        weights_own,
        lax.all_gather(values, "mem", axis=0, tiled=True),
        preferred_element_type=jnp.float32,
    ).astype(jnp.bfloat16)
    mixed_ext = with_halo(mixed_values, (("lon", 2),), 1)
    branch = jnp.einsum(
        "oc,mcwh->mowh", w_out, tap_stack(mixed_ext), preferred_element_type=jnp.float32
    )
    return (fields.astype(jnp.float32) + branch).astype(jnp.bfloat16)


def solution(mesh):
    return jax.shard_map(
        shards,
        mesh=mesh,
        in_specs=(P("mem", None, "lon", None), P(), P(), P(), P()),
        out_specs=P("mem", None, "lon", None),
        check_vma=False,
    )
```

profile of v0, /device:TPU:23, one launch (start us, length us, event | category | flops | bytes accessed | tf_op | source)
XLA Modules:
  0.0 210.7 jit_solution(2268765919190541490)
XLA Ops:
  6.5 1.2 copy.30
  7.8 5.9 %collective-permute-start = (bf16[5,64,1,128]{3,1,2,0:T(8,128)(2,1)S(1)}, bf16[5,64,1,128]{3,1,2,0:T(8,128)(2,1)S(1)}, u32[]{:S(2)}, u32[]{:S(2)}) collective-permute-start(bf16[5,64,1,128]{3,1,2,0:T(8,128)(2,1)S(1)} %get-tuple-element.10), channel_id=1, source_target_pairs={{0,1},{1,2},{2,3},{3,4},{4,5},{5,6},{6,7},{7,8},{8,9},{9,10},{10,1... | collective-permute-start | bytes 245768 | tf_op jit(solution)/shard_map/ppermute | solution.py:15
  13.7 2.1 collective-permute-start.1
  15.8 8.9 %collective-permute-done.1 = bf16[5,64,1,128]{3,1,2,0:T(8,128)(2,1)S(1)} collective-permute-done((bf16[5,64,1,128]{3,1,2,0:T(8,128)(2,1)S(1)}, bf16[5,64,1,128]{3,1,2,0:T(8,128)(2,1)S(1)}, u32[]{:S(2)}, u32[]{:S(2)}) %collective-permute-start.1) | collective-permute-done | bytes 81952 | tf_op jit(solution)/shard_map/ppermute | solution.py:18
  24.7 0.9 fusion.10
  27.7 1.2 fusion.20
  30.4 2.4 %reshape.15 = bf16[16,2,3840]{2,1,0:T(2,128)(2,1)} reshape(bf16[128,5,8,24]{3,2,1,0:T(8,128)(2,1)S(1)} %bitcast.42) | data formatting | bytes 491520
  32.9 10.2 %all-to-all-start = ((bf16[16,2,3840]{2,1,0:T(2,128)(2,1)}), bf16[16,2,3840]{2,1,0:T(2,128)(2,1)S(1)}, u32[]{:S(2)}, u32[]{:S(2)}) async-start(bf16[16,2,3840]{2,1,0:T(2,128)(2,1)} %reshape.15), calls=%async_computation | async-start | bytes 491520 | tf_op jit(solution)/shard_map/all_to_all | solution.py:51
  43.7 2.5 %reshape.17 = bf16[16,2,3840]{2,1,0:T(2,128)(2,1)} reshape(bf16[128,5,8,24]{3,2,1,0:T(8,128)(2,1)S(1)} %bitcast.43) | data formatting | bytes 491520
  46.2 5.6 %all-to-all-done = bf16[16,2,3840]{2,1,0:T(2,128)(2,1)S(1)} async-done(((bf16[16,2,3840]{2,1,0:T(2,128)(2,1)}), bf16[16,2,3840]{2,1,0:T(2,128)(2,1)S(1)}, u32[]{:S(2)}, u32[]{:S(2)}) %all-to-all-start) | async-done | bytes 245792 | tf_op jit(solution)/shard_map/all_to_all | solution.py:51
  51.8 4.0 %all-to-all-start.1 = ((bf16[16,2,3840]{2,1,0:T(2,128)(2,1)}), bf16[16,2,3840]{2,1,0:T(2,128)(2,1)S(1)}, u32[]{:S(2)}, u32[]{:S(2)}) async-start(bf16[16,2,3840]{2,1,0:T(2,128)(2,1)} %reshape.17), calls=%async_computation.1 | async-start | bytes 491520 | tf_op jit(solution)/shard_map/all_to_all | solution.py:52
  55.8 1.8 reshape.16
  57.7 3.6 %copy.39 = bf16[16,5,24,8,8]{4,3,2,1,0:T(8,128)(2,1)} copy(bf16[16,5,24,8,8]{2,3,1,4,0:T(8,128)(2,1)S(1)} %bitcast.40) | data formatting | bytes 491520 | tf_op jit(solution)/shard_map/all_to_all | solution.py:51
  61.3 6.3 %reshape.10 = bf16[80,1536]{1,0:T(8,128)(2,1)S(1)} reshape(bf16[16,5,24,8,8]{4,3,2,1,0:T(8,128)(2,1)} %copy.39) | data formatting | bytes 491520 | tf_op jit(solution)/shard_map/reshape | solution.py:56
  67.6 1.8 reshape.18
  69.5 3.6 %copy.42 = bf16[16,5,24,8,8]{4,3,2,1,0:T(8,128)(2,1)} copy(bf16[16,5,24,8,8]{2,3,1,4,0:T(8,128)(2,1)S(1)} %bitcast.41) | data formatting | bytes 491520 | tf_op jit(solution)/shard_map/all_to_all | solution.py:52
  73.1 6.3 %reshape.11 = bf16[80,1536]{1,0:T(8,128)(2,1)S(1)} reshape(bf16[16,5,24,8,8]{4,3,2,1,0:T(8,128)(2,1)} %copy.42) | data formatting | bytes 491520 | tf_op jit(solution)/shard_map/reshape | solution.py:57
  79.6 96.1 %psum.7 = f32[80,80]{1,0:T(8,128)S(1)} all-reduce(f32[80,80]{1,0:T(8,128)S(1)} %fusion.47), channel_id=1, replica_groups=mesh['mem'=16,'lon'=32] {'mem','lon'}, use_global_device_ids=true, to_apply=%region_0.1 | all-reduce | flops 6400 | bytes 51200 | tf_op jit(solution)/shard_map/psum | solution.py:62
  176.1 4.3 %fusion.21 = bf16[5,24,8,128]{3,0,2,1:T(8,128)(2,1)S(1)} fusion(bf16[80,24,8,128]{3,2,1,0:T(8,128)(2,1)} %all-gather.2.cloned.1.call-done, f32[80,80]{1,0:T(8,128)S(1)} %get-tuple-element.6, s32[]{:T(128)S(6)} %select_n.3, f32[5]{0:T(128)S(1)} %dynamic-slice), kind=kOutput, calls=%fused_computation.20 | convolution fusion | flops 19784480 | bytes 4182532 | tf_op jit(solution)/shard_map/mn,ncwh->mcwh/dot_general | solution.py:65
  180.4 7.6 %collective-permute-start.2 = (bf16[5,24,1,128]{3,0,2,1:T(8,128)(2,1)S(1)}, bf16[5,24,1,128]{3,0,2,1:T(8,128)(2,1)S(1)}, u32[]{:S(2)}, u32[]{:S(2)}) collective-permute-start(bf16[5,24,1,128]{3,0,2,1:T(8,128)(2,1)S(1)} %get-tuple-element.12), channel_id=1, source_target_pairs={{0,1},{1,2},{2,3},{3,4},{4,5},{5,6},{6,7},{7,8},{8,9},{9,10},{10,1... | collective-permute-start | bytes 92168 | tf_op jit(solution)/shard_map/ppermute | solution.py:15
  188.0 2.1 %collective-permute-start.3 = (bf16[5,24,1,128]{3,0,2,1:T(8,128)(2,1)S(1)}, bf16[5,24,1,128]{3,0,2,1:T(8,128)(2,1)S(1)}, u32[]{:S(2)}, u32[]{:S(2)}) collective-permute-start(bf16[5,24,1,128]{3,0,2,1:T(8,128)(2,1)S(1)} %get-tuple-element.13), channel_id=1, source_target_pairs={{1,0},{2,1},{3,2},{4,3},{5,4},{6,5},{7,6},{8,7},{9,8},{10,9},{11,1... | collective-permute-start | bytes 92168 | tf_op jit(solution)/shard_map/ppermute | solution.py:18
  190.1 7.9 %collective-permute-done.3 = bf16[5,24,1,128]{3,0,2,1:T(8,128)(2,1)S(1)} collective-permute-done((bf16[5,24,1,128]{3,0,2,1:T(8,128)(2,1)S(1)}, bf16[5,24,1,128]{3,0,2,1:T(8,128)(2,1)S(1)}, u32[]{:S(2)}, u32[]{:S(2)}) %collective-permute-start.3) | collective-permute-done | bytes 30752 | tf_op jit(solution)/shard_map/ppermute | solution.py:18
  200.0 2.6 %fusion.17 = bf16[5,64,8,128]{3,1,2,0:T(8,128)(2,1)S(1)} fusion(bf16[5,216,8,128]{3,0,2,1:T(8,128)(2,1)S(1)} %slice_dynamic-update-slice_fusion.6, bf16[64,216]{1,0:T(8,128)(2,1)S(1)} %copy-done, bf16[5,64,8,128]{3,2,1,0:T(8,128)(2,1)S(1)} %copy-done.1), kind=kOutput, calls=%fused_computation.18 | convolution fusion | flops 142540800 | bytes 3550208 | tf_op jit(solution)/shard_map/oc,mcwh->mowh/dot_general | solution.py:72
  202.6 1.3 copy.46
  (45 shorter events, 6.6 us)
Async XLA Ops:
  6.5 193.4 %copy-start = (bf16[64,216]{1,0:T(8,128)(2,1)S(1)}, bf16[64,216]{1,0:T(8,128)(2,1)}, u32[]{:S(2)}) copy-start(bf16[64,216]{1,0:T(8,128)(2,1)} %param.9) | copy-start | bytes 82948
  6.5 169.5 %all-gather.2.cloned.1.call-start = ((), (), s32[]{:S(2)}) async-start(), calls=%async_computation.2 | async-start | bytes 4177920 | tf_op jit(solution)/shard_map/all_gather | solution.py:68
  7.8 8.0 %collective-permute-start = (bf16[5,64,1,128]{3,1,2,0:T(8,128)(2,1)S(1)}, bf16[5,64,1,128]{3,1,2,0:T(8,128)(2,1)S(1)}, u32[]{:S(2)}, u32[]{:S(2)}) collective-permute-start(bf16[5,64,1,128]{3,1,2,0:T(8,128)(2,1)S(1)} %get-tuple-element.10), channel_id=1, source_target_pairs={{0,1},{1,2},{2,3},{3,4},{4,5},{5,6},{6,7},{7,8},{8,9},{9,10},{10,1... | collective-permute-start | bytes 245768 | tf_op jit(solution)/shard_map/ppermute | solution.py:15
  13.7 12.7 %copy-start.1 = (bf16[5,64,8,128]{3,2,1,0:T(8,128)(2,1)S(1)}, bf16[5,64,8,128]{3,2,1,0:T(8,128)(2,1)}, u32[]{:S(2)}) copy-start(bf16[5,64,8,128]{3,2,1,0:T(8,128)(2,1)} %param.5) | copy-start | bytes 1966084
  13.7 11.0 %collective-permute-start.1 = (bf16[5,64,1,128]{3,1,2,0:T(8,128)(2,1)S(1)}, bf16[5,64,1,128]{3,1,2,0:T(8,128)(2,1)S(1)}, u32[]{:S(2)}, u32[]{:S(2)}) collective-permute-start(bf16[5,64,1,128]{3,1,2,0:T(8,128)(2,1)S(1)} %get-tuple-element.11), channel_id=1, source_target_pairs={{1,0},{2,1},{3,2},{4,3},{5,4},{6,5},{7,6},{8,7},{9,8},{10,9},{11,1... | collective-permute-start | bytes 245768 | tf_op jit(solution)/shard_map/ppermute | solution.py:18
  26.4 1.3 copy-start.2
  26.4 1.3 copy-start.3
  26.4 1.3 copy-start.4
  32.9 18.9 %all-to-all-start = ((bf16[16,2,3840]{2,1,0:T(2,128)(2,1)}), bf16[16,2,3840]{2,1,0:T(2,128)(2,1)S(1)}, u32[]{:S(2)}, u32[]{:S(2)}) async-start(bf16[16,2,3840]{2,1,0:T(2,128)(2,1)} %reshape.15), calls=%async_computation | async-start | bytes 491520 | tf_op jit(solution)/shard_map/all_to_all | solution.py:51
  51.8 15.8 %all-to-all-start.1 = ((bf16[16,2,3840]{2,1,0:T(2,128)(2,1)}), bf16[16,2,3840]{2,1,0:T(2,128)(2,1)S(1)}, u32[]{:S(2)}, u32[]{:S(2)}) async-start(bf16[16,2,3840]{2,1,0:T(2,128)(2,1)} %reshape.17), calls=%async_computation.1 | async-start | bytes 491520 | tf_op jit(solution)/shard_map/all_to_all | solution.py:52
  180.4 9.7 %collective-permute-start.2 = (bf16[5,24,1,128]{3,0,2,1:T(8,128)(2,1)S(1)}, bf16[5,24,1,128]{3,0,2,1:T(8,128)(2,1)S(1)}, u32[]{:S(2)}, u32[]{:S(2)}) collective-permute-start(bf16[5,24,1,128]{3,0,2,1:T(8,128)(2,1)S(1)} %get-tuple-element.12), channel_id=1, source_target_pairs={{0,1},{1,2},{2,3},{3,4},{4,5},{5,6},{6,7},{7,8},{8,9},{9,10},{10,1... | collective-permute-start | bytes 92168 | tf_op jit(solution)/shard_map/ppermute | solution.py:15
  188.0 10.1 %collective-permute-start.3 = (bf16[5,24,1,128]{3,0,2,1:T(8,128)(2,1)S(1)}, bf16[5,24,1,128]{3,0,2,1:T(8,128)(2,1)S(1)}, u32[]{:S(2)}, u32[]{:S(2)}) collective-permute-start(bf16[5,24,1,128]{3,0,2,1:T(8,128)(2,1)S(1)} %get-tuple-element.13), channel_id=1, source_target_pairs={{1,0},{2,1},{3,2},{4,3},{5,4},{6,5},{7,6},{8,7},{9,8},{10,9},{11,1... | collective-permute-start | bytes 92168 | tf_op jit(solution)/shard_map/ppermute | solution.py:18
Sparse Core Ops, SparseCore 0:
  29.9 102.4 all-gather.1
where the time goes:
time: 211 us
  blocking collectives  96.1 us (46%)
  local copies, waits for them, and re-layouts  36.1 us (17%)
  starting transfers between devices  31.8 us (15%)
  waiting for transfers between devices  22.5 us (11%)
  between operations  13.8 us (7%)
  matrix products  8.3 us (4%)
  other arithmetic  2.14 us (1%)
    psum x1, blocking collectives, shards(): gram_sums = lax.psum(partial_value, ('mem', 'lon'))  96.1 us
    ppermute x2, waiting for transfers between devices, with_halo(): lax.ppermute(lax.slice_in_dim(block, 0, width, axis=dim), axis, backward)  16.8 us
    ppermute x2, starting transfers between devices, with_halo(): lax.ppermute(lax.slice_in_dim(block, block.shape[dim] - width, None, axis...  13.5 us
    unnamed x27, local copies, waits for them, and re-layouts  12.1 us
    all_to_all x1, starting transfers between devices, shards(): lax.all_to_all(queries, 'mem', split_axis=3, concat_axis=0, tiled=True)  10.2 us
    reshape x1, local copies, waits for them, and re-layouts, shards(): query_blocks.reshape(total_members, -1)  6.3 us
    reshape x1, local copies, waits for them, and re-layouts, shards(): key_blocks.reshape(total_members, -1)  6.29 us
    all_to_all x1, waiting for transfers between devices, shards(): lax.all_to_all(queries, 'mem', split_axis=3, concat_axis=0, tiled=True)  5.63 us
  transfers between devices with their start and end apart: 7, of which 3 were waited for; matrix products, arithmetic and copies ran while one was open for 14% of the time, Pallas kernels for 0%

commit v1 on v0

v1 whole, which is shorter than its diff:
```python
import functools
import math

import jax
import jax.numpy as jnp
from jax import lax
from jax.experimental import pallas as pl
from jax.experimental.pallas import tpu as pltpu
from jax.sharding import PartitionSpec as P

CH, CQ, LAT = 64, 24, 128
HALF = CQ // 2
MEM, LON = 16, 32
OWN = 5
TOTAL = MEM * OWN
COLS = 8
EXT = COLS + 2
ROWS = 16
F32, BF16 = jnp.float32, jnp.bfloat16
VMEM = pl.BlockSpec(memory_space=pltpu.VMEM)


def call(body, outs, scratch, flops, nbytes, *args):
    many = isinstance(outs, tuple)
    return pl.pallas_call(
        body,
        out_shape=outs,
        in_specs=[VMEM] * len(args),
        out_specs=(VMEM,) * len(outs) if many else VMEM,
        scratch_shapes=scratch,
        compiler_params=pltpu.CompilerParams(vmem_limit_bytes=32 * 1024 * 1024),
        cost_estimate=pl.CostEstimate(flops=flops, bytes_accessed=nbytes, transcendentals=0),
    )(*args)


def lat_shifts(x):
    lane = lax.broadcasted_iota(jnp.int32, x.shape, 1)
    before = jnp.where(lane == 0, 0.0, pltpu.roll(x, 1, 1))
    after = jnp.where(lane == LAT - 1, 0.0, pltpu.roll(x, LAT - 1, 1))
    return before, after


def project_kernel(f_ref, lo_ref, hi_ref, w_ref, qk_ref, v_ref, xf, xt, vs):
    width = 3 * CQ
    lane = lax.broadcasted_iota(jnp.int32, (width, LAT), 1)
    for m in range(OWN):
        xf[...] = f_ref[m].astype(F32).reshape(CH * COLS, LAT)
        for s in range(2):
            xt[s * CH : (s + 1) * CH] = lo_ref[m, s]
            xt[(EXT + s) * CH : (EXT + s + 1) * CH] = hi_ref[m, s]
        for i in range(COLS):
            xt[(i + 2) * CH : (i + 3) * CH] = xf[pl.ds(i, CH, stride=COLS), :].astype(BF16)
        for p in range(EXT // 2):
            r = jnp.dot(w_ref[...], xt[2 * p * CH : (2 * p + 4) * CH], preferred_element_type=F32)
            for s in range(2):
                y = [r[(3 * s + b) * width : (3 * s + b + 1) * width] for b in range(3)]
                out = (
                    y[1]
                    + jnp.where(lane == 0, 0.0, pltpu.roll(y[0], 1, 1))
                    + jnp.where(lane == LAT - 1, 0.0, pltpu.roll(y[2], LAT - 1, 1))
                )
                col = 2 * p + s
                vs[col * CQ : (col + 1) * CQ] = out[2 * CQ :]
                if 1 <= col <= COLS:
                    for h in range(2):
                        qk_ref[2 * (col - 1) + h, m] = out[h * CQ : (h + 1) * CQ].astype(BF16)
        vs[EXT * CQ :] = jnp.zeros((MEM * ROWS - EXT * CQ, LAT), F32)
        for j in range(MEM):
            v_ref[j, m] = vs[j * ROWS : (j + 1) * ROWS].astype(BF16)


def gram_kernel(x_ref, g_ref, xs, gs):
    xs[...] = x_ref[...].astype(F32).reshape(TOTAL * CQ, LAT)
    pad = jnp.zeros((LAT - TOTAL, LAT), BF16)
    q, k = [], []
    for r in range(HALF):
        q.append(xs[pl.ds(r, TOTAL, stride=CQ), :].astype(BF16))
        k.append(jnp.concatenate([xs[pl.ds(HALF + r, TOTAL, stride=CQ), :].astype(BF16), pad], axis=0))
    gs[...] = lax.dot_general(
        jnp.concatenate(q, axis=1),
        jnp.concatenate(k, axis=1),
        (((1,), (1,)), ((), ())),
        preferred_element_type=F32,
    )
    g_ref[...] = jnp.zeros(g_ref.shape, F32)
    for s in range(MEM):
        g_ref[s, 0:OWN, :] = gs[s * OWN : (s + 1) * OWN, :]


def spread_kernel(x_ref, o_ref):
    o_ref[...] = jnp.broadcast_to(jnp.sum(x_ref[...], axis=0)[None], o_ref.shape)


def softmax_kernel(scale, x_ref, o_ref):
    s = jnp.sum(x_ref[...], axis=0) * scale
    lane = lax.broadcasted_iota(jnp.int32, s.shape, 1)
    s = jnp.where(lane < TOTAL, s, -jnp.inf)
    e = jnp.exp(s - jnp.max(s, axis=1, keepdims=True))
    w = e / jnp.sum(e, axis=1, keepdims=True)
    o_ref[...] = jnp.broadcast_to(w.astype(BF16).astype(F32)[None], o_ref.shape)


def mix_kernel(w_ref, v_ref, o_ref, ws, vs, ms):
    for s in range(MEM):
        ws[s * OWN : (s + 1) * OWN, :] = w_ref[s, 0:OWN, :]
    w = ws[...].astype(BF16)[:, :TOTAL]
    vs[...] = v_ref[...].astype(F32).reshape(TOTAL * ROWS, LAT)
    v = jnp.concatenate([vs[pl.ds(r, TOTAL, stride=ROWS), :].astype(BF16) for r in range(ROWS)], axis=1)
    mixed = jnp.dot(w, v, preferred_element_type=F32)
    for r in range(ROWS):
        ms[pl.ds(r, TOTAL, stride=ROWS), :] = mixed[:, r * LAT : (r + 1) * LAT]
    o_ref[...] = ms[...].astype(BF16).reshape(o_ref.shape)


def finish_kernel(x_ref, f_ref, w_ref, o_ref, mc, mb, ma, br):
    for m in range(OWN):
        for j in range(MEM):
            mc[j * ROWS : (j + 1) * ROWS] = x_ref[j, m].astype(F32)
        mb[...], ma[...] = lat_shifts(mc[...])
        for i in range(0, COLS, 2):
            patches = []
            for col in (i, i + 1):
                parts = [
                    t[(col + a) * CQ : (col + a + 1) * CQ, :] for a in range(3) for t in (mb, mc, ma)
                ]
                patches.append(jnp.concatenate(parts, axis=0).astype(BF16))
            r = jnp.dot(w_ref[...], jnp.concatenate(patches, axis=1), preferred_element_type=F32)
            for s in range(2):
                br[pl.ds(i + s, CH, stride=COLS), :] = r[:, s * LAT : (s + 1) * LAT]
        o_ref[m] = (f_ref[m].astype(F32) + br[...].reshape(CH, COLS, LAT)).astype(BF16)


def shards(fields, w_query, w_key, w_value, w_out):
    forward = [(i, (i + 1) % LON) for i in range(LON)]
    backward = [(target, source) for source, target in forward]
    lo = lax.ppermute(jnp.transpose(fields[:, :, COLS - 2 :], (0, 2, 1, 3)), "lon", forward)
    hi = lax.ppermute(jnp.transpose(fields[:, :, :2], (0, 2, 1, 3)), "lon", backward)

    w = jnp.concatenate([w_query[:HALF], w_key[:HALF], w_query[HALF:], w_key[HALF:], w_value], axis=0)
    w = jnp.transpose(w.reshape(3 * CQ, 3, 3, CH), (2, 0, 1, 3)).reshape(9 * CQ, 3 * CH)
    w_pair = jnp.concatenate(
        [jnp.pad(w, ((0, 0), (0, CH))), jnp.pad(w, ((0, 0), (CH, 0)))], axis=0
    )
    qk, v = call(
        project_kernel,
        (
            jax.ShapeDtypeStruct((MEM, OWN, CQ, LAT), BF16),
            jax.ShapeDtypeStruct((MEM, OWN, ROWS, LAT), BF16),
        ),
        [
            pltpu.VMEM((CH * COLS, LAT), F32),
            pltpu.VMEM((CH * (COLS + 4), LAT), BF16),
            pltpu.VMEM((MEM * ROWS, LAT), F32),
        ],
        700_000_000,
        2_000_000,
        fields,
        lo,
        hi,
        w_pair,
    )
    qk = lax.all_to_all(qk, "mem", 0, 0, tiled=True)
    v = lax.all_to_all(v, "mem", 0, 0, tiled=True)

    tile = (8, LAT)
    gram = call(
        gram_kernel,
        jax.ShapeDtypeStruct((MEM, *tile), F32),
        [pltpu.VMEM((TOTAL * CQ, LAT), F32), pltpu.VMEM((TOTAL, LAT), F32)],
        20_000_000,
        600_000,
        qk,
    )
    gram = lax.all_to_all(gram, "mem", 0, 0, tiled=True)
    gram = call(spread_kernel, jax.ShapeDtypeStruct((LON, *tile), F32), [], 20_000, 200_000, gram)
    gram = lax.all_to_all(gram, "lon", 0, 0, tiled=True)
    scale = 1.0 / math.sqrt(CQ * LAT * COLS * LON)
    weights = call(
        functools.partial(softmax_kernel, scale),
        jax.ShapeDtypeStruct((MEM, *tile), F32),
        [],
        40_000,
        200_000,
        gram,
    )
    weights = lax.all_to_all(weights, "mem", 0, 0, tiled=True)
    mixed = call(
        mix_kernel,
        jax.ShapeDtypeStruct((MEM, OWN, ROWS, LAT), BF16),
        [
            pltpu.VMEM((TOTAL, LAT), F32),
            pltpu.VMEM((TOTAL * ROWS, LAT), F32),
            pltpu.VMEM((TOTAL * ROWS, LAT), F32),
        ],
        30_000_000,
        700_000,
        weights,
        v,
    )
    mixed = lax.all_to_all(mixed, "mem", 0, 0, tiled=True)
    return call(
        finish_kernel,
        jax.ShapeDtypeStruct(fields.shape, BF16),
        [pltpu.VMEM((MEM * ROWS, LAT), F32)] * 3 + [pltpu.VMEM((CH * COLS, LAT), F32)],
        150_000_000,
        1_700_000,
        mixed,
        fields,
        w_out,
    )


def solution(mesh):
    return jax.shard_map(
        shards,
        mesh=mesh,
        in_specs=(P("mem", None, "lon", None), P(), P(), P(), P()),
        out_specs=P("mem", None, "lon", None),
        check_vma=False,
    )
```

time: 211 us -> 119 us (0.56)
  the two profiles are of different devices: /device:TPU:23 before, /device:TPU:8 now
where the time goes in v1:
time: 119 us
  blocking collectives  80.9 us (68%)
  waiting for transfers between devices  14.6 us (12%)
  starting transfers between devices  14 us (12%)
  Pallas kernels  5.03 us (4%)
  local copies, waits for them, and re-layouts  3.67 us (3%)
    all_to_all x1, blocking collectives, shards(): qk = lax.all_to_all(qk, 'mem', 0, 0, tiled=True)  24.4 us
    all_to_all x1, blocking collectives, shards(): gram = lax.all_to_all(gram, 'lon', 0, 0, tiled=True)  19.2 us
    all_to_all x1, blocking collectives, shards(): mixed = lax.all_to_all(mixed, 'mem', 0, 0, tiled=True)  15.3 us
    all_to_all x1, waiting for transfers between devices, shards(): v = lax.all_to_all(v, 'mem', 0, 0, tiled=True)  13.1 us
    all_to_all x1, blocking collectives, shards(): gram = lax.all_to_all(gram, 'mem', 0, 0, tiled=True)  11.2 us
    all_to_all x1, blocking collectives, shards(): weights = lax.all_to_all(weights, 'mem', 0, 0, tiled=True)  10.9 us
    ppermute x1, starting transfers between devices, shards(): lax.ppermute(jnp.transpose(fields[:, :, :2], (0, 2, 1, 3)), 'lon', backward)  7.86 us
    pallas_call x6, Pallas kernels, call(): pl.pallas_call(body, out_shape=outs, in_specs=[VMEM] * len(args), out_spe...  5.03 us
  transfers between devices with their start and end apart: 3, of which 2 were waited for; matrix products, arithmetic and copies ran while one was open for 1% of the time, Pallas kernels for 0%

profile of v1, /device:TPU:8, one launch (start us, length us, event | category | flops | bytes accessed | tf_op | source)
XLA Modules:
  0.0 118.5 jit_solution(14641321692814303437)
XLA Ops:
  0.0 1.6 %fusion.3 = (bf16[5,64,2,128]{3,2,1,0:T(2,128)(2,1)S(1)}, bf16[5,64,2,128]{3,2,1,0:T(2,128)(2,1)S(1)}) fusion(bf16[5,64,8,128]{3,2,1,0:T(8,128)(2,1)} %f_ref.3), kind=kLoop, calls=%fused_computation.7 | loop fusion | bytes 655360 | tf_op jit(solution)/shard_map/slice | solution.py:137
  1.6 1.9 %collective-permute-start = (bf16[5,2,64,128]{3,2,1,0:T(8,128)(2,1)S(1)}, bf16[5,2,64,128]{3,2,1,0:T(8,128)(2,1)S(1)}, u32[]{:S(2)}, u32[]{:S(2)}) collective-permute-start(bf16[5,2,64,128]{3,2,1,0:T(8,128)(2,1)S(1)} %bitcast.10), channel_id=1, source_target_pairs={{0,1},{1,2},{2,3},{3,4},{4,5},{5,6},{6,7},{7,8},{8,9},{9,10},{10,1... | collective-permute-start | bytes 491528 | tf_op jit(solution)/shard_map/ppermute | solution.py:136
  3.6 7.9 %collective-permute-start.1 = (bf16[5,2,64,128]{3,2,1,0:T(8,128)(2,1)S(1)}, bf16[5,2,64,128]{3,2,1,0:T(8,128)(2,1)S(1)}, u32[]{:S(2)}, u32[]{:S(2)}) collective-permute-start(bf16[5,2,64,128]{3,2,1,0:T(8,128)(2,1)S(1)} %bitcast.11), channel_id=1, source_target_pairs={{1,0},{2,1},{3,2},{4,3},{5,4},{6,5},{7,6},{8,7},{9,8},{10,9},{11,1... | collective-permute-start | bytes 491528 | tf_op jit(solution)/shard_map/ppermute | solution.py:137
  11.5 0.2 copy.14
  11.7 0.2 copy.13
  11.8 0.2 copy.12
  12.0 0.2 copy.11
  12.2 0.6 copy-done.4
  12.9 0.3 concatenate.6
  13.2 0.2 copy.19
  13.4 0.2 reshape.8
  13.7 1.5 %collective-permute-done.1.hi_ref = bf16[5,2,64,128]{3,2,1,0:T(8,128)(2,1)S(1)} collective-permute-done((bf16[5,2,64,128]{3,2,1,0:T(8,128)(2,1)S(1)}, bf16[5,2,64,128]{3,2,1,0:T(8,128)(2,1)S(1)}, u32[]{:S(2)}, u32[]{:S(2)}) %collective-permute-start.1) | collective-permute-done | bytes 163872 | tf_op jit(solution)/shard_map/ppermute | solution.py:137
  15.2 2.5 %shard_map.55 = (bf16[16,5,24,128]{3,2,1,0:T(8,128)(2,1)S(1)}, bf16[16,5,16,128]{3,2,1,0:T(8,128)(2,1)}) custom-call(bf16[5,64,8,128]{3,2,1,0:T(8,128)(2,1)S(1)} %copy-done, bf16[5,2,64,128]{3,2,1,0:T(8,128)(2,1)S(1)} %collective-permute-done.lo_ref, bf16[5,2,64,128]{3,2,1,0:T(8,128)(2,1)S(1)} %collective-permute-done.1.hi_ref, bf16[432,256]{1,0:T(8,128)(2,1)S(1)} %fusion.2.w_ref), custom_call_target="tpu_custom_call" | custom-call | flops 700000000 | bytes 2000000 | tf_op jit(solution)/shard_map/pallas_call | solution.py:25
  17.7 24.4 %all_to_all.30.x_ref = bf16[16,5,24,128]{3,2,1,0:T(8,128)(2,1)S(1)} all-to-all(bf16[16,5,24,128]{3,2,1,0:T(8,128)(2,1)S(1)} %get-tuple-element.7), channel_id=1, replica_groups=mesh['mem'=16,'lon'=32] {'mem'}, dimensions={0} | all-to-all | bytes 983040 | tf_op jit(solution)/shard_map/all_to_all | solution.py:162
  42.1 0.3 shard_map.56
  42.4 11.2 %all_to_all.31.x_ref = f32[16,8,128]{2,1,0:T(8,128)S(1)} all-to-all(f32[16,8,128]{2,1,0:T(8,128)S(1)} %shard_map.56), channel_id=1, replica_groups=mesh['mem'=16,'lon'=32] {'mem'}, dimensions={0} | all-to-all | bytes 131072 | tf_op jit(solution)/shard_map/all_to_all | solution.py:174
  53.6 19.2 %all_to_all.32.x_ref = f32[32,8,128]{2,1,0:T(8,128)S(1)} all-to-all(f32[32,8,128]{2,1,0:T(8,128)S(1)} %shard_map.57), channel_id=1, replica_groups=mesh['mem'=16,'lon'=32] {'lon'}, dimensions={0} | all-to-all | bytes 262144 | tf_op jit(solution)/shard_map/all_to_all | solution.py:176
  72.7 4.2 %all-to-all-start.4 = ((bf16[16,5,16,128]{3,2,1,0:T(8,128)(2,1)}), bf16[16,5,16,128]{3,2,1,0:T(8,128)(2,1)S(1)}, u32[]{:S(2)}, u32[]{:S(2)}) async-start(bf16[16,5,16,128]{3,2,1,0:T(8,128)(2,1)} %get-tuple-element.8), calls=%async_computation.4 | async-start | bytes 655360 | tf_op jit(solution)/shard_map/all_to_all | solution.py:163
  77.0 0.2 shard_map.58
  77.2 13.1 %all-to-all-done.4.v_ref = bf16[16,5,16,128]{3,2,1,0:T(8,128)(2,1)S(1)} async-done(((bf16[16,5,16,128]{3,2,1,0:T(8,128)(2,1)}), bf16[16,5,16,128]{3,2,1,0:T(8,128)(2,1)S(1)}, u32[]{:S(2)}, u32[]{:S(2)}) %all-to-all-start.4) | async-done | bytes 327712 | tf_op jit(solution)/shard_map/all_to_all | solution.py:163
  90.3 10.9 %all_to_all.33.w_ref = f32[16,8,128]{2,1,0:T(8,128)S(1)} all-to-all(f32[16,8,128]{2,1,0:T(8,128)S(1)} %shard_map.58), channel_id=1, replica_groups=mesh['mem'=16,'lon'=32] {'mem'}, dimensions={0} | all-to-all | bytes 131072 | tf_op jit(solution)/shard_map/all_to_all | solution.py:186
  101.2 0.5 shard_map.59
  101.7 15.3 %all_to_all.34.x_ref = bf16[16,5,16,128]{3,2,1,0:T(8,128)(2,1)S(1)} all-to-all(bf16[16,5,16,128]{3,2,1,0:T(8,128)(2,1)S(1)} %shard_map.59), channel_id=1, replica_groups=mesh['mem'=16,'lon'=32] {'mem'}, dimensions={0} | all-to-all | bytes 655360 | tf_op jit(solution)/shard_map/all_to_all | solution.py:200
  117.0 1.5 %shard_map.60 = bf16[5,64,8,128]{3,2,1,0:T(8,128)(2,1)} custom-call(bf16[16,5,16,128]{3,2,1,0:T(8,128)(2,1)S(1)} %all_to_all.34.x_ref, bf16[5,64,8,128]{3,2,1,0:T(8,128)(2,1)S(1)} %copy-done, bf16[64,216]{1,0:T(8,128)(2,1)S(1)} %copy-done.1), custom_call_target="tpu_custom_call" | custom-call | flops 150000000 | bytes 1700000 | tf_op jit(solution)/shard_map/pallas_call | solution.py:25
  (17 shorter events, 0.4 us)
Async XLA Ops:
  1.6 12.1 %collective-permute-start = (bf16[5,2,64,128]{3,2,1,0:T(8,128)(2,1)S(1)}, bf16[5,2,64,128]{3,2,1,0:T(8,128)(2,1)S(1)}, u32[]{:S(2)}, u32[]{:S(2)}) collective-permute-start(bf16[5,2,64,128]{3,2,1,0:T(8,128)(2,1)S(1)} %bitcast.10), channel_id=1, source_target_pairs={{0,1},{1,2},{2,3},{3,4},{4,5},{5,6},{6,7},{7,8},{8,9},{9,10},{10,1... | collective-permute-start | bytes 491528 | tf_op jit(solution)/shard_map/ppermute | solution.py:136
  3.5 7.9 %copy-start.2 = (bf16[24,576]{1,0:T(8,128)(2,1)S(1)}, bf16[24,576]{1,0:T(8,128)(2,1)}, u32[]{:S(2)}) copy-start(bf16[24,576]{1,0:T(8,128)(2,1)} %param.6) | copy-start | bytes 82948
  3.6 7.9 %copy-start.3 = (bf16[24,576]{1,0:T(8,128)(2,1)S(1)}, bf16[24,576]{1,0:T(8,128)(2,1)}, u32[]{:S(2)}) copy-start(bf16[24,576]{1,0:T(8,128)(2,1)} %param.7) | copy-start | bytes 82948
  3.6 11.6 %collective-permute-start.1 = (bf16[5,2,64,128]{3,2,1,0:T(8,128)(2,1)S(1)}, bf16[5,2,64,128]{3,2,1,0:T(8,128)(2,1)S(1)}, u32[]{:S(2)}, u32[]{:S(2)}) collective-permute-start(bf16[5,2,64,128]{3,2,1,0:T(8,128)(2,1)S(1)} %bitcast.11), channel_id=1, source_target_pairs={{1,0},{2,1},{3,2},{4,3},{5,4},{6,5},{7,6},{8,7},{9,8},{10,9},{11,1... | collective-permute-start | bytes 491528 | tf_op jit(solution)/shard_map/ppermute | solution.py:137
  12.0 0.8 copy-start.4
  13.2 2.0 %copy-start = (bf16[5,64,8,128]{3,2,1,0:T(8,128)(2,1)S(1)}, bf16[5,64,8,128]{3,2,1,0:T(8,128)(2,1)}, u32[]{:S(2)}) copy-start(bf16[5,64,8,128]{3,2,1,0:T(8,128)(2,1)} %f_ref.3) | copy-start | bytes 1966084
  72.7 17.6 %all-to-all-start.4 = ((bf16[16,5,16,128]{3,2,1,0:T(8,128)(2,1)}), bf16[16,5,16,128]{3,2,1,0:T(8,128)(2,1)S(1)}, u32[]{:S(2)}, u32[]{:S(2)}) async-start(bf16[16,5,16,128]{3,2,1,0:T(8,128)(2,1)} %get-tuple-element.8), calls=%async_computation.4 | async-start | bytes 655360 | tf_op jit(solution)/shard_map/all_to_all | solution.py:163
  101.7 15.3 %copy-start.1 = (bf16[64,216]{1,0:T(8,128)(2,1)S(1)}, bf16[64,216]{1,0:T(8,128)(2,1)}, u32[]{:S(2)}) copy-start(bf16[64,216]{1,0:T(8,128)(2,1)} %w_ref.1) | copy-start | bytes 82948

commit v2 on v1

--- a/solution.py
+++ b/solution.py
@@ -6,6 +6,7 @@
 from jax import lax
 from jax.experimental import pallas as pl
 from jax.experimental.pallas import tpu as pltpu
+from jax.sharding import Mesh
 from jax.sharding import PartitionSpec as P
 
 CH, CQ, LAT = 64, 24, 128
@@ -20,7 +21,7 @@
 VMEM = pl.BlockSpec(memory_space=pltpu.VMEM)
 
 
-def call(body, outs, scratch, flops, nbytes, *args):
+def call(body, outs, scratch, flops, nbytes, *args, alias=None):
     many = isinstance(outs, tuple)
     return pl.pallas_call(
         body,
@@ -28,6 +29,7 @@
         in_specs=[VMEM] * len(args),
         out_specs=(VMEM,) * len(outs) if many else VMEM,
         scratch_shapes=scratch,
+        input_output_aliases=alias or {},
         compiler_params=pltpu.CompilerParams(vmem_limit_bytes=32 * 1024 * 1024),
         cost_estimate=pl.CostEstimate(flops=flops, bytes_accessed=nbytes, transcendentals=0),
     )(*args)
@@ -40,37 +42,91 @@
     return before, after
 
 
-def project_kernel(f_ref, lo_ref, hi_ref, w_ref, qk_ref, v_ref, xf, xt, vs):
+def edges_kernel(f_ref, sib_ref, nb_ref, xf):
+    even = lax.axis_index("core") == 0
+    for m in range(OWN):
+        xf[...] = f_ref[m].astype(F32).reshape(CH * COLS, LAT)
+        for s in range(2):
+            left = xf[pl.ds(s, CH, stride=COLS), :]
+            right = xf[pl.ds(COLS - 2 + s, CH, stride=COLS), :]
+            sib_ref[m, s * CH : (s + 1) * CH] = jnp.where(even, right, left).astype(BF16)
+            nb_ref[m, s * CH : (s + 1) * CH] = jnp.where(even, left, right).astype(BF16)
+
+
+def conv_pair(w, x):
     width = 3 * CQ
     lane = lax.broadcasted_iota(jnp.int32, (width, LAT), 1)
+    r = jnp.dot(w, x, preferred_element_type=F32)
+    outs = []
+    for s in range(2):
+        y = [r[(3 * s + b) * width : (3 * s + b + 1) * width] for b in range(3)]
+        outs.append(
+            y[1]
+            + jnp.where(lane == 0, 0.0, pltpu.roll(y[0], 1, 1))
+            + jnp.where(lane == LAT - 1, 0.0, pltpu.roll(y[2], LAT - 1, 1))
+        )
+    return outs
+
+
+def put_pair(o_ref, vs, m, p, outs):
+    for s in range(2):
+        col = 2 * p + s
+        vs[s * CQ : (s + 1) * CQ] = outs[s][2 * CQ :]
+        if 1 <= col <= COLS:
+            for h in range(2):
+                o_ref[2 * (col - 1) + h, m, 0:CQ] = outs[s][h * CQ : (h + 1) * CQ].astype(BF16)
+    for j in range(3):
+        o_ref[3 * p + j, m, CQ:] = vs[j * ROWS : (j + 1) * ROWS].astype(BF16)
+
+
+def inner_kernel(f_ref, wq_ref, wk_ref, wv_ref, o_ref, wp_ref, ws, xf, xt, vs):
+    ws[0:HALF] = wq_ref[...].astype(F32)[:HALF]
+    ws[HALF : 2 * HALF] = wk_ref[...].astype(F32)[:HALF]
+    ws[2 * HALF : 3 * HALF] = wq_ref[...].astype(F32)[HALF:]
+    ws[3 * HALF : 4 * HALF] = wk_ref[...].astype(F32)[HALF:]
+    ws[2 * CQ :] = wv_ref[...].astype(F32)
+    zero = jnp.zeros((3 * CQ, CH), F32)
+    for b in range(3):
+        taps = [ws[:, (3 * a + b) * CH : (3 * a + b + 1) * CH] for a in range(3)]
+        for s in range(2):
+            row = (3 * s + b) * 3 * CQ
+            full = [zero] + taps if s else taps + [zero]
+            wp_ref[row : row + 3 * CQ] = jnp.concatenate(full, axis=1).astype(BF16)
     for m in range(OWN):
         xf[...] = f_ref[m].astype(F32).reshape(CH * COLS, LAT)
-        for s in range(2):
-            xt[s * CH : (s + 1) * CH] = lo_ref[m, s]
-            xt[(EXT + s) * CH : (EXT + s + 1) * CH] = hi_ref[m, s]
         for i in range(COLS):
-            xt[(i + 2) * CH : (i + 3) * CH] = xf[pl.ds(i, CH, stride=COLS), :].astype(BF16)
-        for p in range(EXT // 2):
-            r = jnp.dot(w_ref[...], xt[2 * p * CH : (2 * p + 4) * CH], preferred_element_type=F32)
-            for s in range(2):
-                y = [r[(3 * s + b) * width : (3 * s + b + 1) * width] for b in range(3)]
-                out = (
-                    y[1]
-                    + jnp.where(lane == 0, 0.0, pltpu.roll(y[0], 1, 1))
-                    + jnp.where(lane == LAT - 1, 0.0, pltpu.roll(y[2], LAT - 1, 1))
-                )
-                col = 2 * p + s
-                vs[col * CQ : (col + 1) * CQ] = out[2 * CQ :]
-                if 1 <= col <= COLS:
-                    for h in range(2):
-                        qk_ref[2 * (col - 1) + h, m] = out[h * CQ : (h + 1) * CQ].astype(BF16)
-        vs[EXT * CQ :] = jnp.zeros((MEM * ROWS - EXT * CQ, LAT), F32)
-        for j in range(MEM):
-            v_ref[j, m] = vs[j * ROWS : (j + 1) * ROWS].astype(BF16)
+            xt[i * CH : (i + 1) * CH] = xf[pl.ds(i, CH, stride=COLS), :].astype(BF16)
+        for p in range(1, EXT // 2 - 1):
+            x = xt[2 * (p - 1) * CH : 2 * (p + 1) * CH]
+            put_pair(o_ref, vs, m, p, conv_pair(wp_ref[...], x))
+
+
+def outer_kernel(i_ref, wp_ref, sib_ref, nb_ref, gs_ref, gn_ref, o_ref, xl, xr, vs):
+    core = lax.axis_index("core")
+    near = 2 * CH
+
+    @pl.when(core == 0)
+    def _():
+        xl[:, :near] = gn_ref[...]
+        xl[:, near:] = nb_ref[...]
+        xr[:, :near] = sib_ref[...]
+        xr[:, near:] = gs_ref[1]
+
+    @pl.when(core == 1)
+    def _():
+        xl[:, :near] = gs_ref[0]
+        xl[:, near:] = sib_ref[...]
+        xr[:, :near] = nb_ref[...]
+        xr[:, near:] = gn_ref[...]
+
+    for m in range(OWN):
+        put_pair(o_ref, vs, m, 0, conv_pair(wp_ref[...], xl[m]))
+        put_pair(o_ref, vs, m, EXT // 2 - 1, conv_pair(wp_ref[...], xr[m]))
+        o_ref[MEM - 1, m, CQ:] = jnp.zeros((ROWS, LAT), BF16)
 
 
 def gram_kernel(x_ref, g_ref, xs, gs):
-    xs[...] = x_ref[...].astype(F32).reshape(TOTAL * CQ, LAT)
+    xs[...] = x_ref[:, :, 0:CQ, :].astype(F32).reshape(TOTAL * CQ, LAT)
     pad = jnp.zeros((LAT - TOTAL, LAT), BF16)
     q, k = [], []
     for r in range(HALF):
@@ -104,7 +160,7 @@
     for s in range(MEM):
         ws[s * OWN : (s + 1) * OWN, :] = w_ref[s, 0:OWN, :]
     w = ws[...].astype(BF16)[:, :TOTAL]
-    vs[...] = v_ref[...].astype(F32).reshape(TOTAL * ROWS, LAT)
+    vs[...] = v_ref[:, :, CQ:, :].astype(F32).reshape(TOTAL * ROWS, LAT)
     v = jnp.concatenate([vs[pl.ds(r, TOTAL, stride=ROWS), :].astype(BF16) for r in range(ROWS)], axis=1)
     mixed = jnp.dot(w, v, preferred_element_type=F32)
     for r in range(ROWS):
@@ -131,36 +187,45 @@
 
 
 def shards(fields, w_query, w_key, w_value, w_out):
-    forward = [(i, (i + 1) % LON) for i in range(LON)]
-    backward = [(target, source) for source, target in forward]
-    lo = lax.ppermute(jnp.transpose(fields[:, :, COLS - 2 :], (0, 2, 1, 3)), "lon", forward)
-    hi = lax.ppermute(jnp.transpose(fields[:, :, :2], (0, 2, 1, 3)), "lon", backward)
-
-    w = jnp.concatenate([w_query[:HALF], w_key[:HALF], w_query[HALF:], w_key[HALF:], w_value], axis=0)
-    w = jnp.transpose(w.reshape(3 * CQ, 3, 3, CH), (2, 0, 1, 3)).reshape(9 * CQ, 3 * CH)
-    w_pair = jnp.concatenate(
-        [jnp.pad(w, ((0, 0), (0, CH))), jnp.pad(w, ((0, 0), (CH, 0)))], axis=0
-    )
-    qk, v = call(
-        project_kernel,
-        (
-            jax.ShapeDtypeStruct((MEM, OWN, CQ, LAT), BF16),
-            jax.ShapeDtypeStruct((MEM, OWN, ROWS, LAT), BF16),
-        ),
+    edge = jax.ShapeDtypeStruct((OWN, 2 * CH, LAT), BF16)
+    plane = pltpu.VMEM((CH * COLS, LAT), F32)
+    sib, nb = call(edges_kernel, (edge, edge), [plane], 0, 1_000_000, fields)
+    swaps = [(i, (i - 1 if i % 2 == 0 else i + 1) % LON) for i in range(LON)]
+    got_nb = lax.ppermute(nb, ("chip", "core"), swaps)
+    got_sib = lax.all_gather(sib, "core", axis=0, tiled=False)
+    packed = jax.ShapeDtypeStruct((MEM, OWN, CQ + ROWS, LAT), BF16)
+    pair = jax.ShapeDtypeStruct((18 * CQ, 4 * CH), BF16)
+    part, w_pair = call(
+        inner_kernel,
+        (packed, pair),
         [
-            pltpu.VMEM((CH * COLS, LAT), F32),
-            pltpu.VMEM((CH * (COLS + 4), LAT), BF16),
-            pltpu.VMEM((MEM * ROWS, LAT), F32),
+            pltpu.VMEM((3 * CQ, 9 * CH), F32),
+            plane,
+            pltpu.VMEM((CH * COLS, LAT), BF16),
+            pltpu.VMEM((2 * CQ, LAT), F32),
         ],
-        700_000_000,
+        450_000_000,
         2_000_000,
         fields,
-        lo,
-        hi,
+        w_query,
+        w_key,
+        w_value,
+    )
+    qkv = call(
+        outer_kernel,
+        packed,
+        [pltpu.VMEM((OWN, 4 * CH, LAT), BF16)] * 2 + [pltpu.VMEM((2 * CQ, LAT), F32)],
+        300_000_000,
+        1_500_000,
+        part,
         w_pair,
-    )
-    qk = lax.all_to_all(qk, "mem", 0, 0, tiled=True)
-    v = lax.all_to_all(v, "mem", 0, 0, tiled=True)
+        sib,
+        nb,
+        got_sib,
+        got_nb,
+        alias={0: 0},
+    )
+    qkv = lax.all_to_all(qkv, "mem", 0, 0, tiled=True)
 
     tile = (8, LAT)
     gram = call(
@@ -169,11 +234,11 @@
         [pltpu.VMEM((TOTAL * CQ, LAT), F32), pltpu.VMEM((TOTAL, LAT), F32)],
         20_000_000,
         600_000,
-        qk,
+        qkv,
     )
     gram = lax.all_to_all(gram, "mem", 0, 0, tiled=True)
     gram = call(spread_kernel, jax.ShapeDtypeStruct((LON, *tile), F32), [], 20_000, 200_000, gram)
-    gram = lax.all_to_all(gram, "lon", 0, 0, tiled=True)
+    gram = lax.all_to_all(gram, ("chip", "core"), 0, 0, tiled=True)
     scale = 1.0 / math.sqrt(CQ * LAT * COLS * LON)
     weights = call(
         functools.partial(softmax_kernel, scale),
@@ -195,7 +260,7 @@
         30_000_000,
         700_000,
         weights,
-        v,
+        qkv,
     )
     mixed = lax.all_to_all(mixed, "mem", 0, 0, tiled=True)
     return call(
@@ -211,10 +276,12 @@
 
 
 def solution(mesh):
+    fine = Mesh(mesh.devices.reshape(MEM, LON // 2, 2), ("mem", "chip", "core"))
+    spec = P("mem", None, ("chip", "core"), None)
     return jax.shard_map(
         shards,
-        mesh=mesh,
-        in_specs=(P("mem", None, "lon", None), P(), P(), P(), P()),
-        out_specs=P("mem", None, "lon", None),
+        mesh=fine,
+        in_specs=(spec, P(), P(), P(), P()),
+        out_specs=spec,
         check_vma=False,
     )

time: 119 us -> 104 us (0.87)
  waiting for transfers between devices: 14.6 us -> 0.65 us
  blocking collectives: 80.9 us -> 90.3 us
  starting transfers between devices: 14 us -> 6.9 us
  local copies, waits for them, and re-layouts: 3.67 us -> 1.11 us
    all_to_all x1 -> x0, waiting for transfers between devices: 13.1 us -> none  [shards(): v = lax.all_to_all(v, 'mem', 0, 0, tiled=True)]
    all_to_all x2, blocking collectives: 43.5 us -> 51.2 us  [the longest x1 34.2 us: shards(): qkv = lax.all_to_all(qkv, 'mem', 0, 0, tiled=True)]
    all_to_all x1 -> x0, starting transfers between devices: 4.25 us -> none  [shards(): v = lax.all_to_all(v, 'mem', 0, 0, tiled=True)]
    ppermute x2 -> x1, starting transfers between devices: 9.78 us -> 6.9 us  [shards(): got_nb = lax.ppermute(nb, ('chip', 'core'), swaps)]
    slice x7 -> x0, local copies, waits for them, and re-layouts: 2.22 us -> none  [the longest x1 1.55 us: shards(): fields[:, :, :2]]
    all_gather x0 -> x1, blocking collectives: none -> 2.04 us  [shards(): got_sib = lax.all_gather(sib, 'core', axis=0, tiled=False)]
    pallas_call x6 -> x8, Pallas kernels: 5.03 us -> 4.9 us  [call(): pl.pallas_call(body, out_shape=outs, in_specs=[VMEM] * len(args), out_spe...]
  transfers between devices with their start and end apart: 3 -> 1, of which waited for: 2 -> 1; matrix products, arithmetic and copies ran while one was open for 1% -> 0% of each run, Pallas kernels for 0% -> 1%
where the time goes in v2:
time: 104 us
  blocking collectives  90.3 us (87%)
  starting transfers between devices  6.9 us (7%)
  Pallas kernels  4.9 us (5%)
  local copies, waits for them, and re-layouts  1.11 us (1%)
    all_to_all x1, blocking collectives, shards(): qkv = lax.all_to_all(qkv, 'mem', 0, 0, tiled=True)  34.2 us
    all_to_all x1, blocking collectives, shards(): gram = lax.all_to_all(gram, ('chip', 'core'), 0, 0, tiled=True)  17.1 us
    all_to_all x1, blocking collectives, shards(): mixed = lax.all_to_all(mixed, 'mem', 0, 0, tiled=True)  14.9 us
    all_to_all x1, blocking collectives, shards(): weights = lax.all_to_all(weights, 'mem', 0, 0, tiled=True)  11.2 us
    all_to_all x1, blocking collectives, shards(): gram = lax.all_to_all(gram, 'mem', 0, 0, tiled=True)  11 us
    ppermute x1, starting transfers between devices, shards(): got_nb = lax.ppermute(nb, ('chip', 'core'), swaps)  6.9 us
    pallas_call x8, Pallas kernels, call(): pl.pallas_call(body, out_shape=outs, in_specs=[VMEM] * len(args), out_spe...  4.9 us
  transfers between devices with their start and end apart: 1, of which 1 were waited for; matrix products, arithmetic and copies ran while one was open for 0% of the time, Pallas kernels for 1%

profile of v2, /device:TPU:8, one launch (start us, length us, event | category | flops | bytes accessed | tf_op | source)
XLA Modules:
  0.0 104.0 jit_solution(11628555389035182891)
XLA Ops:
  0.0 0.0 copy-start
  0.0 1.1 %copy-done = bf16[5,64,8,128]{3,2,1,0:T(8,128)(2,1)S(1)} copy-done((bf16[5,64,8,128]{3,2,1,0:T(8,128)(2,1)S(1)}, bf16[5,64,8,128]{3,2,1,0:T(8,128)(2,1)}, u32[]{:S(2)}) %copy-start) | copy-done | bytes 655384
  1.1 0.0 copy-start.3
  1.1 0.2 shard_map.56
  1.3 6.9 %collective-permute-start = (bf16[5,128,128]{2,1,0:T(8,128)(2,1)S(1)}, bf16[5,128,128]{2,1,0:T(8,128)(2,1)S(1)}, u32[]{:S(2)}, u32[]{:S(2)}) collective-permute-start(bf16[5,128,128]{2,1,0:T(8,128)(2,1)S(1)} %get-tuple-element.12.nb_ref), channel_id=1, source_target_pairs={{0,31},{1,2},{2,1},{3,4},{4,3},{5,6},{6,5},{7,8},{8,7},{9,10},{10,... | collective-permute-start | bytes 491528 | tf_op jit(solution)/shard_map/ppermute | solution.py:194
  8.2 0.0 copy-done.3
  8.2 0.0 copy-done.4
  8.2 0.0 copy-done.5
  8.2 1.3 %shard_map.55 = (bf16[16,5,40,128]{3,2,1,0:T(8,128)(2,1)S(1)}, bf16[432,256]{1,0:T(8,128)(2,1)S(1)}) custom-call(bf16[5,64,8,128]{3,2,1,0:T(8,128)(2,1)S(1)} %copy-done, bf16[24,576]{1,0:T(8,128)(2,1)S(1)} %copy-done.3, bf16[24,576]{1,0:T(8,128)(2,1)S(1)} %copy-done.4, bf16[24,576]{1,0:T(8,128)(2,1)S(1)} %copy-done.5), custom_call_target="tpu_custom_call" | custom-call | flops 450000000 | bytes 2000000 | tf_op jit(solution)/shard_map/pallas_call | solution.py:26
  9.6 2.0 %all-gather = bf16[10,128,128]{2,1,0:T(8,128)(2,1)S(1)} all-gather(bf16[5,128,128]{2,1,0:T(8,128)(2,1)S(1)} %get-tuple-element.11.sib_ref), channel_id=2, replica_groups=mesh['mem'=16,'chip'=16,'core'=2] {'core'}, dimensions={0}, use_global_device_ids=true | all-gather | bytes 491520 | tf_op jit(solution)/shard_map/all_gather | solution.py:195
  11.6 0.6 collective-permute-done.gn_ref
  12.2 0.9 shard_map.57
  13.1 34.2 %all_to_all.25.x_ref.v_ref = bf16[16,5,40,128]{3,2,1,0:T(8,128)(2,1)S(1)} all-to-all(bf16[16,5,40,128]{3,2,1,0:T(8,128)(2,1)S(1)} %shard_map.57), channel_id=1, replica_groups=mesh['mem'=16,'chip'=16,'core'=2] {'mem'}, dimensions={0} | all-to-all | bytes 1638400 | tf_op jit(solution)/shard_map/all_to_all | solution.py:228
  47.3 0.3 shard_map.58
  47.6 11.0 %all_to_all.26.x_ref = f32[16,8,128]{2,1,0:T(8,128)S(1)} all-to-all(f32[16,8,128]{2,1,0:T(8,128)S(1)} %shard_map.58), channel_id=1, replica_groups=mesh['mem'=16,'chip'=16,'core'=2] {'mem'}, dimensions={0} | all-to-all | bytes 131072 | tf_op jit(solution)/shard_map/all_to_all | solution.py:239
  58.6 17.1 %all_to_all.27.x_ref = f32[32,8,128]{2,1,0:T(8,128)S(1)} all-to-all(f32[32,8,128]{2,1,0:T(8,128)S(1)} %shard_map.59), channel_id=1, replica_groups=mesh['mem'=16,'chip'=16,'core'=2] {'chip','core'}, dimensions={0} | all-to-all | bytes 262144 | tf_op jit(solution)/shard_map/all_to_all | solution.py:241
  75.7 0.2 shard_map.60
  75.9 11.2 %all_to_all.28.w_ref = f32[16,8,128]{2,1,0:T(8,128)S(1)} all-to-all(f32[16,8,128]{2,1,0:T(8,128)S(1)} %shard_map.60), channel_id=1, replica_groups=mesh['mem'=16,'chip'=16,'core'=2] {'mem'}, dimensions={0} | all-to-all | bytes 131072 | tf_op jit(solution)/shard_map/all_to_all | solution.py:251
  87.1 0.5 shard_map.61
  87.6 0.0 copy-start.2
  87.6 14.9 %all_to_all.29.x_ref = bf16[16,5,16,128]{3,2,1,0:T(8,128)(2,1)S(1)} all-to-all(bf16[16,5,16,128]{3,2,1,0:T(8,128)(2,1)S(1)} %shard_map.61), channel_id=1, replica_groups=mesh['mem'=16,'chip'=16,'core'=2] {'mem'}, dimensions={0} | all-to-all | bytes 655360 | tf_op jit(solution)/shard_map/all_to_all | solution.py:265
  102.4 0.0 copy-done.1
  102.4 0.0 copy-done.2
  102.4 1.5 %shard_map.62 = bf16[5,64,8,128]{3,2,1,0:T(8,128)(2,1)} custom-call(bf16[16,5,16,128]{3,2,1,0:T(8,128)(2,1)S(1)} %all_to_all.29.x_ref, bf16[5,64,8,128]{3,2,1,0:T(8,128)(2,1)S(1)} %copy-done.1, bf16[64,216]{1,0:T(8,128)(2,1)S(1)} %copy-done.2), custom_call_target="tpu_custom_call" | custom-call | flops 150000000 | bytes 1700000 | tf_op jit(solution)/shard_map/pallas_call | solution.py:26
  (4 shorter events, 0.0 us)
Async XLA Ops:
  0.0 1.1 %copy-start = (bf16[5,64,8,128]{3,2,1,0:T(8,128)(2,1)S(1)}, bf16[5,64,8,128]{3,2,1,0:T(8,128)(2,1)}, u32[]{:S(2)}) copy-start(bf16[5,64,8,128]{3,2,1,0:T(8,128)(2,1)} %f_ref.5) | copy-start | bytes 1966084
  1.1 7.1 %copy-start.3 = (bf16[24,576]{1,0:T(8,128)(2,1)S(1)}, bf16[24,576]{1,0:T(8,128)(2,1)}, u32[]{:S(2)}) copy-start(bf16[24,576]{1,0:T(8,128)(2,1)} %wq_ref.1) | copy-start | bytes 82948
  1.1 7.1 %copy-start.4 = (bf16[24,576]{1,0:T(8,128)(2,1)S(1)}, bf16[24,576]{1,0:T(8,128)(2,1)}, u32[]{:S(2)}) copy-start(bf16[24,576]{1,0:T(8,128)(2,1)} %wk_ref.1) | copy-start | bytes 82948
  1.1 7.1 %copy-start.5 = (bf16[24,576]{1,0:T(8,128)(2,1)S(1)}, bf16[24,576]{1,0:T(8,128)(2,1)}, u32[]{:S(2)}) copy-start(bf16[24,576]{1,0:T(8,128)(2,1)} %wv_ref.1) | copy-start | bytes 82948
  1.3 11.0 %collective-permute-start = (bf16[5,128,128]{2,1,0:T(8,128)(2,1)S(1)}, bf16[5,128,128]{2,1,0:T(8,128)(2,1)S(1)}, u32[]{:S(2)}, u32[]{:S(2)}) collective-permute-start(bf16[5,128,128]{2,1,0:T(8,128)(2,1)S(1)} %get-tuple-element.12.nb_ref), channel_id=1, source_target_pairs={{0,31},{1,2},{2,1},{3,4},{4,3},{5,6},{6,5},{7,8},{8,7},{9,10},{10,... | collective-permute-start | bytes 491528 | tf_op jit(solution)/shard_map/ppermute | solution.py:194
  87.1 15.4 %copy-start.1 = (bf16[5,64,8,128]{3,2,1,0:T(8,128)(2,1)S(1)}, bf16[5,64,8,128]{3,2,1,0:T(8,128)(2,1)}, u32[]{:S(2)}) copy-start(bf16[5,64,8,128]{3,2,1,0:T(8,128)(2,1)} %f_ref.5) | copy-start | bytes 1966084
  87.6 14.9 %copy-start.2 = (bf16[64,216]{1,0:T(8,128)(2,1)S(1)}, bf16[64,216]{1,0:T(8,128)(2,1)}, u32[]{:S(2)}) copy-start(bf16[64,216]{1,0:T(8,128)(2,1)} %w_ref.1) | copy-start | bytes 82948

commit v3 on v2

--- a/solution.py
+++ b/solution.py
@@ -14,6 +14,7 @@
 MEM, LON = 16, 32
 OWN = 5
 TOTAL = MEM * OWN
+PART = TOTAL // 2
 COLS = 8
 EXT = COLS + 2
 ROWS = 16
@@ -125,22 +126,24 @@
         o_ref[MEM - 1, m, CQ:] = jnp.zeros((ROWS, LAT), BF16)
 
 
-def gram_kernel(x_ref, g_ref, xs, gs):
+def gram_kernel(x_ref, g_ref, xs):
     xs[...] = x_ref[:, :, 0:CQ, :].astype(F32).reshape(TOTAL * CQ, LAT)
     pad = jnp.zeros((LAT - TOTAL, LAT), BF16)
     q, k = [], []
     for r in range(HALF):
         q.append(xs[pl.ds(r, TOTAL, stride=CQ), :].astype(BF16))
         k.append(jnp.concatenate([xs[pl.ds(HALF + r, TOTAL, stride=CQ), :].astype(BF16), pad], axis=0))
-    gs[...] = lax.dot_general(
+    g_ref[...] = lax.dot_general(
         jnp.concatenate(q, axis=1),
         jnp.concatenate(k, axis=1),
         (((1,), (1,)), ((), ())),
         preferred_element_type=F32,
     )
-    g_ref[...] = jnp.zeros(g_ref.shape, F32)
-    for s in range(MEM):
-        g_ref[s, 0:OWN, :] = gs[s * OWN : (s + 1) * OWN, :]
+
+
+def halve_kernel(x_ref, o_ref):
+    rows = pl.ds(pl.multiple_of(lax.axis_index("core") * PART, 8), PART)
+    o_ref[...] = jnp.broadcast_to((x_ref[0, rows, :] + x_ref[1, rows, :])[None], o_ref.shape)
 
 
 def spread_kernel(x_ref, o_ref):
@@ -153,13 +156,11 @@
     s = jnp.where(lane < TOTAL, s, -jnp.inf)
     e = jnp.exp(s - jnp.max(s, axis=1, keepdims=True))
     w = e / jnp.sum(e, axis=1, keepdims=True)
-    o_ref[...] = jnp.broadcast_to(w.astype(BF16).astype(F32)[None], o_ref.shape)
-
-
-def mix_kernel(w_ref, v_ref, o_ref, ws, vs, ms):
-    for s in range(MEM):
-        ws[s * OWN : (s + 1) * OWN, :] = w_ref[s, 0:OWN, :]
-    w = ws[...].astype(BF16)[:, :TOTAL]
+    o_ref[...] = w.astype(BF16)
+
+
+def mix_kernel(w_ref, v_ref, o_ref, vs, ms):
+    w = w_ref[...].astype(F32).reshape(TOTAL, LAT).astype(BF16)[:, :TOTAL]
     vs[...] = v_ref[:, :, CQ:, :].astype(F32).reshape(TOTAL * ROWS, LAT)
     v = jnp.concatenate([vs[pl.ds(r, TOTAL, stride=ROWS), :].astype(BF16) for r in range(ROWS)], axis=1)
     mixed = jnp.dot(w, v, preferred_element_type=F32)
@@ -227,33 +228,34 @@
     )
     qkv = lax.all_to_all(qkv, "mem", 0, 0, tiled=True)
 
-    tile = (8, LAT)
     gram = call(
         gram_kernel,
-        jax.ShapeDtypeStruct((MEM, *tile), F32),
-        [pltpu.VMEM((TOTAL * CQ, LAT), F32), pltpu.VMEM((TOTAL, LAT), F32)],
+        jax.ShapeDtypeStruct((TOTAL, LAT), F32),
+        [pltpu.VMEM((TOTAL * CQ, LAT), F32)],
         20_000_000,
         600_000,
         qkv,
     )
+    gram = lax.all_gather(gram, "core", axis=0, tiled=False)
+    copies = jax.ShapeDtypeStruct((MEM, PART, LAT), F32)
+    gram = call(halve_kernel, copies, [], 20_000, 200_000, gram)
+    gram = lax.all_to_all(gram, "chip", 0, 0, tiled=True)
+    gram = call(spread_kernel, copies, [], 80_000, 400_000, gram)
     gram = lax.all_to_all(gram, "mem", 0, 0, tiled=True)
-    gram = call(spread_kernel, jax.ShapeDtypeStruct((LON, *tile), F32), [], 20_000, 200_000, gram)
-    gram = lax.all_to_all(gram, ("chip", "core"), 0, 0, tiled=True)
     scale = 1.0 / math.sqrt(CQ * LAT * COLS * LON)
     weights = call(
         functools.partial(softmax_kernel, scale),
-        jax.ShapeDtypeStruct((MEM, *tile), F32),
+        jax.ShapeDtypeStruct((PART, LAT), BF16),
         [],
-        40_000,
+        100_000,
         200_000,
         gram,
     )
-    weights = lax.all_to_all(weights, "mem", 0, 0, tiled=True)
+    weights = lax.all_gather(weights, "core", axis=0, tiled=False)
     mixed = call(
         mix_kernel,
         jax.ShapeDtypeStruct((MEM, OWN, ROWS, LAT), BF16),
         [
-            pltpu.VMEM((TOTAL, LAT), F32),
             pltpu.VMEM((TOTAL * ROWS, LAT), F32),
             pltpu.VMEM((TOTAL * ROWS, LAT), F32),
         ],

time: 104 us -> 105 us (level)
    all_to_all x2 -> x1, blocking collectives: 28.2 us -> 18.7 us  [shards(): gram = lax.all_to_all(gram, 'chip', 0, 0, tiled=True)]
    all_to_all x1, blocking collectives: 11 us -> 15.8 us  [shards(): gram = lax.all_to_all(gram, 'mem', 0, 0, tiled=True)]
    all_gather x0 -> x2, blocking collectives: none -> 3.69 us  [the longest x1 1.87 us: shards(): gram = lax.all_gather(gram, 'core', axis=0, tiled=False)]
    all_to_all x1, blocking collectives: 14.9 us -> 16.1 us  [shards(): mixed = lax.all_to_all(mixed, 'mem', 0, 0, tiled=True)]
    pallas_call x8 -> x9, Pallas kernels: 4.9 us -> 4.93 us  [call(): pl.pallas_call(body, out_shape=outs, in_specs=[VMEM] * len(args), out_spe...]
where the time goes in v3:
time: 105 us; the launch traced here: 104 us
  blocking collectives  90.6 us (86%)
  starting transfers between devices  6.9 us (7%)
  Pallas kernels  4.93 us (5%)
  local copies, waits for them, and re-layouts  1.11 us (1%)
    all_to_all x1, blocking collectives, shards(): qkv = lax.all_to_all(qkv, 'mem', 0, 0, tiled=True)  34.2 us
    all_to_all x1, blocking collectives, shards(): gram = lax.all_to_all(gram, 'chip', 0, 0, tiled=True)  18.7 us
    all_to_all x1, blocking collectives, shards(): mixed = lax.all_to_all(mixed, 'mem', 0, 0, tiled=True)  16.1 us
    all_to_all x1, blocking collectives, shards(): gram = lax.all_to_all(gram, 'mem', 0, 0, tiled=True)  15.8 us
    ppermute x1, starting transfers between devices, shards(): got_nb = lax.ppermute(nb, ('chip', 'core'), swaps)  6.9 us
    pallas_call x9, Pallas kernels, call(): pl.pallas_call(body, out_shape=outs, in_specs=[VMEM] * len(args), out_spe...  4.93 us
  transfers between devices with their start and end apart: 1, of which 1 were waited for; matrix products, arithmetic and copies ran while one was open for 0% of the time, Pallas kernels for 1%

profile of v3, /device:TPU:8, one launch (start us, length us, event | category | flops | bytes accessed | tf_op | source)
XLA Modules:
  0.0 104.2 jit_solution(11944978556689095317)
XLA Ops:
  0.0 0.0 copy-start
  0.0 1.1 %copy-done = bf16[5,64,8,128]{3,2,1,0:T(8,128)(2,1)S(1)} copy-done((bf16[5,64,8,128]{3,2,1,0:T(8,128)(2,1)S(1)}, bf16[5,64,8,128]{3,2,1,0:T(8,128)(2,1)}, u32[]{:S(2)}) %copy-start) | copy-done | bytes 655384
  1.1 0.2 shard_map.56
  1.3 6.9 %collective-permute-start = (bf16[5,128,128]{2,1,0:T(8,128)(2,1)S(1)}, bf16[5,128,128]{2,1,0:T(8,128)(2,1)S(1)}, u32[]{:S(2)}, u32[]{:S(2)}) collective-permute-start(bf16[5,128,128]{2,1,0:T(8,128)(2,1)S(1)} %get-tuple-element.12.nb_ref), channel_id=1, source_target_pairs={{0,31},{1,2},{2,1},{3,4},{4,3},{5,6},{6,5},{7,8},{8,7},{9,10},{10,... | collective-permute-start | bytes 491528 | tf_op jit(solution)/shard_map/ppermute | solution.py:195
  8.2 0.0 copy-done.3
  8.2 0.0 copy-done.4
  8.2 0.0 copy-done.5
  8.2 1.3 %shard_map.55 = (bf16[16,5,40,128]{3,2,1,0:T(8,128)(2,1)S(1)}, bf16[432,256]{1,0:T(8,128)(2,1)S(1)}) custom-call(bf16[5,64,8,128]{3,2,1,0:T(8,128)(2,1)S(1)} %copy-done, bf16[24,576]{1,0:T(8,128)(2,1)S(1)} %copy-done.3, bf16[24,576]{1,0:T(8,128)(2,1)S(1)} %copy-done.4, bf16[24,576]{1,0:T(8,128)(2,1)S(1)} %copy-done.5), custom_call_target="tpu_custom_call" | custom-call | flops 450000000 | bytes 2000000 | tf_op jit(solution)/shard_map/pallas_call | solution.py:27
  9.6 2.0 %all-gather = bf16[10,128,128]{2,1,0:T(8,128)(2,1)S(1)} all-gather(bf16[5,128,128]{2,1,0:T(8,128)(2,1)S(1)} %get-tuple-element.11.sib_ref), channel_id=2, replica_groups=mesh['mem'=16,'chip'=16,'core'=2] {'core'}, dimensions={0}, use_global_device_ids=true | all-gather | bytes 491520 | tf_op jit(solution)/shard_map/all_gather | solution.py:196
  11.6 0.6 collective-permute-done.gn_ref
  12.2 0.9 shard_map.57
  13.1 34.2 %all_to_all.20.x_ref.v_ref = bf16[16,5,40,128]{3,2,1,0:T(8,128)(2,1)S(1)} all-to-all(bf16[16,5,40,128]{3,2,1,0:T(8,128)(2,1)S(1)} %shard_map.57), channel_id=1, replica_groups=mesh['mem'=16,'chip'=16,'core'=2] {'mem'}, dimensions={0} | all-to-all | bytes 1638400 | tf_op jit(solution)/shard_map/all_to_all | solution.py:229
  47.3 0.3 shard_map.58
  47.6 1.9 %all-gather.1 = f32[160,128]{1,0:T(8,128)S(1)} all-gather(f32[80,128]{1,0:T(8,128)S(1)} %shard_map.58), channel_id=3, replica_groups=mesh['mem'=16,'chip'=16,'core'=2] {'core'}, dimensions={0}, use_global_device_ids=true | all-gather | bytes 122880 | tf_op jit(solution)/shard_map/all_gather | solution.py:239
  49.5 18.7 %all_to_all.21.x_ref = f32[16,40,128]{2,1,0:T(8,128)S(1)} all-to-all(f32[16,40,128]{2,1,0:T(8,128)S(1)} %shard_map.59), channel_id=1, replica_groups=mesh['mem'=16,'chip'=16,'core'=2] {'chip'}, dimensions={0} | all-to-all | bytes 655360 | tf_op jit(solution)/shard_map/all_to_all | solution.py:242
  68.3 15.8 %all_to_all.22.x_ref = f32[16,40,128]{2,1,0:T(8,128)S(1)} all-to-all(f32[16,40,128]{2,1,0:T(8,128)S(1)} %shard_map.60), channel_id=1, replica_groups=mesh['mem'=16,'chip'=16,'core'=2] {'mem'}, dimensions={0} | all-to-all | bytes 655360 | tf_op jit(solution)/shard_map/all_to_all | solution.py:244
  84.1 0.2 shard_map.61
  84.3 1.8 %all-gather.2 = bf16[80,128]{1,0:T(8,128)(2,1)S(1)} all-gather(bf16[40,128]{1,0:T(8,128)(2,1)S(1)} %shard_map.61), channel_id=4, replica_groups=mesh['mem'=16,'chip'=16,'core'=2] {'core'}, dimensions={0}, use_global_device_ids=true | all-gather | bytes 30720 | tf_op jit(solution)/shard_map/all_gather | solution.py:254
  86.1 0.5 shard_map.62
  86.6 0.0 copy-start.2
  86.6 16.1 %all_to_all.23.x_ref = bf16[16,5,16,128]{3,2,1,0:T(8,128)(2,1)S(1)} all-to-all(bf16[16,5,16,128]{3,2,1,0:T(8,128)(2,1)S(1)} %shard_map.62), channel_id=1, replica_groups=mesh['mem'=16,'chip'=16,'core'=2] {'mem'}, dimensions={0} | all-to-all | bytes 655360 | tf_op jit(solution)/shard_map/all_to_all | solution.py:267
  102.7 0.0 copy-done.1
  102.7 0.0 copy-done.2
  102.7 1.5 %shard_map.63 = bf16[5,64,8,128]{3,2,1,0:T(8,128)(2,1)} custom-call(bf16[16,5,16,128]{3,2,1,0:T(8,128)(2,1)S(1)} %all_to_all.23.x_ref, bf16[5,64,8,128]{3,2,1,0:T(8,128)(2,1)S(1)} %copy-done.1, bf16[64,216]{1,0:T(8,128)(2,1)S(1)} %copy-done.2), custom_call_target="tpu_custom_call" | custom-call | flops 150000000 | bytes 1700000 | tf_op jit(solution)/shard_map/pallas_call | solution.py:27
  (6 shorter events, 0.1 us)
Async XLA Ops:
  0.0 1.1 %copy-start = (bf16[5,64,8,128]{3,2,1,0:T(8,128)(2,1)S(1)}, bf16[5,64,8,128]{3,2,1,0:T(8,128)(2,1)}, u32[]{:S(2)}) copy-start(bf16[5,64,8,128]{3,2,1,0:T(8,128)(2,1)} %f_ref.5) | copy-start | bytes 1966084
  1.1 7.1 %copy-start.3 = (bf16[24,576]{1,0:T(8,128)(2,1)S(1)}, bf16[24,576]{1,0:T(8,128)(2,1)}, u32[]{:S(2)}) copy-start(bf16[24,576]{1,0:T(8,128)(2,1)} %wq_ref.1) | copy-start | bytes 82948
  1.1 7.1 %copy-start.4 = (bf16[24,576]{1,0:T(8,128)(2,1)S(1)}, bf16[24,576]{1,0:T(8,128)(2,1)}, u32[]{:S(2)}) copy-start(bf16[24,576]{1,0:T(8,128)(2,1)} %wk_ref.1) | copy-start | bytes 82948
  1.1 7.1 %copy-start.5 = (bf16[24,576]{1,0:T(8,128)(2,1)S(1)}, bf16[24,576]{1,0:T(8,128)(2,1)}, u32[]{:S(2)}) copy-start(bf16[24,576]{1,0:T(8,128)(2,1)} %wv_ref.1) | copy-start | bytes 82948
  1.3 11.0 %collective-permute-start = (bf16[5,128,128]{2,1,0:T(8,128)(2,1)S(1)}, bf16[5,128,128]{2,1,0:T(8,128)(2,1)S(1)}, u32[]{:S(2)}, u32[]{:S(2)}) collective-permute-start(bf16[5,128,128]{2,1,0:T(8,128)(2,1)S(1)} %get-tuple-element.12.nb_ref), channel_id=1, source_target_pairs={{0,31},{1,2},{2,1},{3,4},{4,3},{5,6},{6,5},{7,8},{8,7},{9,10},{10,... | collective-permute-start | bytes 491528 | tf_op jit(solution)/shard_map/ppermute | solution.py:195
  86.1 16.6 %copy-start.1 = (bf16[5,64,8,128]{3,2,1,0:T(8,128)(2,1)S(1)}, bf16[5,64,8,128]{3,2,1,0:T(8,128)(2,1)}, u32[]{:S(2)}) copy-start(bf16[5,64,8,128]{3,2,1,0:T(8,128)(2,1)} %f_ref.5) | copy-start | bytes 1966084
  86.6 16.1 %copy-start.2 = (bf16[64,216]{1,0:T(8,128)(2,1)S(1)}, bf16[64,216]{1,0:T(8,128)(2,1)}, u32[]{:S(2)}) copy-start(bf16[64,216]{1,0:T(8,128)(2,1)} %w_ref.1) | copy-start | bytes 82948

commit v4 on v2

--- a/solution.py
+++ b/solution.py
@@ -14,6 +14,9 @@
 MEM, LON = 16, 32
 OWN = 5
 TOTAL = MEM * OWN
+NEAR = 8
+BAND = TOTAL // NEAR
+CUT = LAT - TOTAL
 COLS = 8
 EXT = COLS + 2
 ROWS = 16
@@ -132,34 +135,40 @@
     for r in range(HALF):
         q.append(xs[pl.ds(r, TOTAL, stride=CQ), :].astype(BF16))
         k.append(jnp.concatenate([xs[pl.ds(HALF + r, TOTAL, stride=CQ), :].astype(BF16), pad], axis=0))
-    gs[...] = lax.dot_general(
+    gram = lax.dot_general(
         jnp.concatenate(q, axis=1),
         jnp.concatenate(k, axis=1),
         (((1,), (1,)), ((), ())),
         preferred_element_type=F32,
     )
-    g_ref[...] = jnp.zeros(g_ref.shape, F32)
-    for s in range(MEM):
-        g_ref[s, 0:OWN, :] = gs[s * OWN : (s + 1) * OWN, :]
+    lane = lax.broadcasted_iota(jnp.int32, gram.shape, 1)
+    gs[0] = gram
+    gs[1] = jnp.where(lane < TOTAL, 0.0, pltpu.roll(gram, TOTAL, 1))
+    gs[2] = jnp.where(lane < TOTAL, 0.0, pltpu.roll(gram, TOTAL - CUT, 1))
+    rest = jnp.zeros((4, LAT), F32)
+    for s in range(NEAR):
+        row = s * BAND
+        free = [gs[1 + h, row + 8 + e : row + 9 + e, :] for e in range(2) for h in range(2)]
+        g_ref[s] = gs[0, row : row + 8, :] + jnp.concatenate(free + [rest], axis=0)
 
 
 def spread_kernel(x_ref, o_ref):
     o_ref[...] = jnp.broadcast_to(jnp.sum(x_ref[...], axis=0)[None], o_ref.shape)
 
 
-def softmax_kernel(scale, x_ref, o_ref):
-    s = jnp.sum(x_ref[...], axis=0) * scale
-    lane = lax.broadcasted_iota(jnp.int32, s.shape, 1)
-    s = jnp.where(lane < TOTAL, s, -jnp.inf)
+def mix_kernel(scale, g_ref, v_ref, o_ref, ws, vs, ms):
+    lane = lax.broadcasted_iota(jnp.int32, (8, LAT), 1)
+    for s in range(NEAR):
+        tile = g_ref[s]
+        head, tail = pltpu.roll(tile, LAT - TOTAL, 1), pltpu.roll(tile, LAT - TOTAL + CUT, 1)
+        ws[s * BAND : s * BAND + 8] = tile
+        for e in range(2):
+            row = jnp.where(lane[:1] < CUT, head[2 * e : 2 * e + 1], tail[2 * e + 1 : 2 * e + 2])
+            ws[s * BAND + 8 + e : s * BAND + 9 + e] = row
+    lane = lax.broadcasted_iota(jnp.int32, (TOTAL, LAT), 1)
+    s = jnp.where(lane < TOTAL, ws[...] * scale, -jnp.inf)
     e = jnp.exp(s - jnp.max(s, axis=1, keepdims=True))
-    w = e / jnp.sum(e, axis=1, keepdims=True)
-    o_ref[...] = jnp.broadcast_to(w.astype(BF16).astype(F32)[None], o_ref.shape)
-
-
-def mix_kernel(w_ref, v_ref, o_ref, ws, vs, ms):
-    for s in range(MEM):
-        ws[s * OWN : (s + 1) * OWN, :] = w_ref[s, 0:OWN, :]
-    w = ws[...].astype(BF16)[:, :TOTAL]
+    w = (e / jnp.sum(e, axis=1, keepdims=True)).astype(BF16)[:, :TOTAL]
     vs[...] = v_ref[:, :, CQ:, :].astype(F32).reshape(TOTAL * ROWS, LAT)
     v = jnp.concatenate([vs[pl.ds(r, TOTAL, stride=ROWS), :].astype(BF16) for r in range(ROWS)], axis=1)
     mixed = jnp.dot(w, v, preferred_element_type=F32)
@@ -191,7 +200,7 @@
     plane = pltpu.VMEM((CH * COLS, LAT), F32)
     sib, nb = call(edges_kernel, (edge, edge), [plane], 0, 1_000_000, fields)
     swaps = [(i, (i - 1 if i % 2 == 0 else i + 1) % LON) for i in range(LON)]
-    got_nb = lax.ppermute(nb, ("chip", "core"), swaps)
+    got_nb = lax.ppermute(nb, ("yhi", "x", "core"), swaps)
     got_sib = lax.all_gather(sib, "core", axis=0, tiled=False)
     packed = jax.ShapeDtypeStruct((MEM, OWN, CQ + ROWS, LAT), BF16)
     pair = jax.ShapeDtypeStruct((18 * CQ, 4 * CH), BF16)
@@ -227,30 +236,25 @@
     )
     qkv = lax.all_to_all(qkv, "mem", 0, 0, tiled=True)
 
-    tile = (8, LAT)
+    near, far = ("x", "core"), ("mem", "yhi")
+    tiles = jax.ShapeDtypeStruct((NEAR, 8, LAT), F32)
+    copies = jax.ShapeDtypeStruct((MEM * LON // NEAR, 8, LAT), F32)
     gram = call(
         gram_kernel,
-        jax.ShapeDtypeStruct((MEM, *tile), F32),
-        [pltpu.VMEM((TOTAL * CQ, LAT), F32), pltpu.VMEM((TOTAL, LAT), F32)],
+        tiles,
+        [pltpu.VMEM((TOTAL * CQ, LAT), F32), pltpu.VMEM((3, TOTAL, LAT), F32)],
         20_000_000,
         600_000,
         qkv,
     )
-    gram = lax.all_to_all(gram, "mem", 0, 0, tiled=True)
-    gram = call(spread_kernel, jax.ShapeDtypeStruct((LON, *tile), F32), [], 20_000, 200_000, gram)
-    gram = lax.all_to_all(gram, ("chip", "core"), 0, 0, tiled=True)
+    gram = lax.all_to_all(gram, near, 0, 0, tiled=True)
+    gram = call(spread_kernel, copies, [], 20_000, 300_000, gram)
+    gram = lax.all_to_all(gram, far, 0, 0, tiled=True)
+    gram = call(spread_kernel, tiles, [], 80_000, 300_000, gram)
+    gram = lax.all_to_all(gram, near, 0, 0, tiled=True)
     scale = 1.0 / math.sqrt(CQ * LAT * COLS * LON)
-    weights = call(
-        functools.partial(softmax_kernel, scale),
-        jax.ShapeDtypeStruct((MEM, *tile), F32),
-        [],
-        40_000,
-        200_000,
-        gram,
-    )
-    weights = lax.all_to_all(weights, "mem", 0, 0, tiled=True)
     mixed = call(
-        mix_kernel,
+        functools.partial(mix_kernel, scale),
         jax.ShapeDtypeStruct((MEM, OWN, ROWS, LAT), BF16),
         [
             pltpu.VMEM((TOTAL, LAT), F32),
@@ -259,7 +263,7 @@
         ],
         30_000_000,
         700_000,
-        weights,
+        gram,
         qkv,
     )
     mixed = lax.all_to_all(mixed, "mem", 0, 0, tiled=True)
@@ -276,8 +280,8 @@
 
 
 def solution(mesh):
-    fine = Mesh(mesh.devices.reshape(MEM, LON // 2, 2), ("mem", "chip", "core"))
-    spec = P("mem", None, ("chip", "core"), None)
+    fine = Mesh(mesh.devices.reshape(MEM, LON // NEAR, NEAR // 2, 2), ("mem", "yhi", "x", "core"))
+    spec = P("mem", None, ("yhi", "x", "core"), None)
     return jax.shard_map(
         shards,
         mesh=fine,

time: 104 us -> 103 us (level)
  blocking collectives: 90.3 us -> 89 us
    all_to_all x3, blocking collectives: 39.2 us -> 36.5 us  [the longest x1 20.8 us: shards(): gram = lax.all_to_all(gram, far, 0, 0, tiled=True)]
    all_to_all x1, blocking collectives: 14.9 us -> 16.4 us  [shards(): mixed = lax.all_to_all(mixed, 'mem', 0, 0, tiled=True)]
where the time goes in v4:
time: 103 us
  blocking collectives  89 us (86%)
  starting transfers between devices  6.9 us (7%)
  Pallas kernels  5 us (5%)
  local copies, waits for them, and re-layouts  1.11 us (1%)
    all_to_all x1, blocking collectives, shards(): qkv = lax.all_to_all(qkv, 'mem', 0, 0, tiled=True)  34.2 us
    all_to_all x1, blocking collectives, shards(): gram = lax.all_to_all(gram, far, 0, 0, tiled=True)  20.8 us
    all_to_all x1, blocking collectives, shards(): mixed = lax.all_to_all(mixed, 'mem', 0, 0, tiled=True)  16.4 us
    all_to_all x2, blocking collectives, shards(): gram = lax.all_to_all(gram, near, 0, 0, tiled=True)  15.6 us
    ppermute x1, starting transfers between devices, shards(): got_nb = lax.ppermute(nb, ('yhi', 'x', 'core'), swaps)  6.9 us
    pallas_call x8, Pallas kernels, call(): pl.pallas_call(body, out_shape=outs, in_specs=[VMEM] * len(args), out_spe...  5 us
  transfers between devices with their start and end apart: 1, of which 1 were waited for; matrix products, arithmetic and copies ran while one was open for 0% of the time, Pallas kernels for 1%

profile of v4, /device:TPU:8, one launch (start us, length us, event | category | flops | bytes accessed | tf_op | source)
XLA Modules:
  0.0 102.8 jit_solution(9511668720833532006)
XLA Ops:
  0.0 0.0 copy-start
  0.0 1.1 %copy-done = bf16[5,64,8,128]{3,2,1,0:T(8,128)(2,1)S(1)} copy-done((bf16[5,64,8,128]{3,2,1,0:T(8,128)(2,1)S(1)}, bf16[5,64,8,128]{3,2,1,0:T(8,128)(2,1)}, u32[]{:S(2)}) %copy-start) | copy-done | bytes 655384
  1.1 0.0 copy-start.3
  1.1 0.2 shard_map.56
  1.3 6.9 %collective-permute-start = (bf16[5,128,128]{2,1,0:T(8,128)(2,1)S(1)}, bf16[5,128,128]{2,1,0:T(8,128)(2,1)S(1)}, u32[]{:S(2)}, u32[]{:S(2)}) collective-permute-start(bf16[5,128,128]{2,1,0:T(8,128)(2,1)S(1)} %get-tuple-element.12.nb_ref), channel_id=1, source_target_pairs={{0,31},{1,2},{2,1},{3,4},{4,3},{5,6},{6,5},{7,8},{8,7},{9,10},{10,... | collective-permute-start | bytes 491528 | tf_op jit(solution)/shard_map/ppermute | solution.py:203
  8.2 0.0 copy-done.3
  8.2 0.0 copy-done.4
  8.2 0.0 copy-done.5
  8.2 1.3 %shard_map.55 = (bf16[16,5,40,128]{3,2,1,0:T(8,128)(2,1)S(1)}, bf16[432,256]{1,0:T(8,128)(2,1)S(1)}) custom-call(bf16[5,64,8,128]{3,2,1,0:T(8,128)(2,1)S(1)} %copy-done, bf16[24,576]{1,0:T(8,128)(2,1)S(1)} %copy-done.3, bf16[24,576]{1,0:T(8,128)(2,1)S(1)} %copy-done.4, bf16[24,576]{1,0:T(8,128)(2,1)S(1)} %copy-done.5), custom_call_target="tpu_custom_call" | custom-call | flops 450000000 | bytes 2000000 | tf_op jit(solution)/shard_map/pallas_call | solution.py:29
  9.6 2.0 %all-gather = bf16[10,128,128]{2,1,0:T(8,128)(2,1)S(1)} all-gather(bf16[5,128,128]{2,1,0:T(8,128)(2,1)S(1)} %get-tuple-element.11.sib_ref), channel_id=2, replica_groups=mesh['mem'=16,'yhi'=4,'x'=4,'core'=2] {'core'}, dimensions={0}, use_global_device_ids=true | all-gather | bytes 491520 | tf_op jit(solution)/shard_map/all_gather | solution.py:204
  11.6 0.6 collective-permute-done.gn_ref
  12.2 0.9 shard_map.57
  13.1 34.2 %all_to_all.25.x_ref.v_ref = bf16[16,5,40,128]{3,2,1,0:T(8,128)(2,1)S(1)} all-to-all(bf16[16,5,40,128]{3,2,1,0:T(8,128)(2,1)S(1)} %shard_map.57), channel_id=1, replica_groups=mesh['mem'=16,'yhi'=4,'x'=4,'core'=2] {'mem'}, dimensions={0} | all-to-all | bytes 1638400 | tf_op jit(solution)/shard_map/all_to_all | solution.py:237
  47.3 0.4 shard_map.58
  47.7 7.8 %all_to_all.26.x_ref = f32[8,8,128]{2,1,0:T(8,128)S(1)} all-to-all(f32[8,8,128]{2,1,0:T(8,128)S(1)} %shard_map.58), channel_id=1, replica_groups=mesh['mem'=16,'yhi'=4,'x'=4,'core'=2] {'x','core'}, dimensions={0} | all-to-all | bytes 65536 | tf_op jit(solution)/shard_map/all_to_all | solution.py:250
  55.5 20.8 %all_to_all.27.x_ref = f32[64,8,128]{2,1,0:T(8,128)S(1)} all-to-all(f32[64,8,128]{2,1,0:T(8,128)S(1)} %shard_map.59), channel_id=1, replica_groups=mesh['mem'=16,'yhi'=4,'x'=4,'core'=2] {'mem','yhi'}, dimensions={0} | all-to-all | bytes 524288 | tf_op jit(solution)/shard_map/all_to_all | solution.py:252
  76.4 0.1 shard_map.60
  76.4 7.8 %all_to_all.28.g_ref = f32[8,8,128]{2,1,0:T(8,128)S(1)} all-to-all(f32[8,8,128]{2,1,0:T(8,128)S(1)} %shard_map.60), channel_id=1, replica_groups=mesh['mem'=16,'yhi'=4,'x'=4,'core'=2] {'x','core'}, dimensions={0} | all-to-all | bytes 65536 | tf_op jit(solution)/shard_map/all_to_all | solution.py:254
  84.3 0.6 shard_map.61
  84.9 0.0 copy-start.2
  84.9 16.4 %all_to_all.29.x_ref = bf16[16,5,16,128]{3,2,1,0:T(8,128)(2,1)S(1)} all-to-all(bf16[16,5,16,128]{3,2,1,0:T(8,128)(2,1)S(1)} %shard_map.61), channel_id=1, replica_groups=mesh['mem'=16,'yhi'=4,'x'=4,'core'=2] {'mem'}, dimensions={0} | all-to-all | bytes 655360 | tf_op jit(solution)/shard_map/all_to_all | solution.py:269
  101.3 0.0 copy-done.1
  101.3 0.0 copy-done.2
  101.3 1.5 %shard_map.62 = bf16[5,64,8,128]{3,2,1,0:T(8,128)(2,1)} custom-call(bf16[16,5,16,128]{3,2,1,0:T(8,128)(2,1)S(1)} %all_to_all.29.x_ref, bf16[5,64,8,128]{3,2,1,0:T(8,128)(2,1)S(1)} %copy-done.1, bf16[64,216]{1,0:T(8,128)(2,1)S(1)} %copy-done.2), custom_call_target="tpu_custom_call" | custom-call | flops 150000000 | bytes 1700000 | tf_op jit(solution)/shard_map/pallas_call | solution.py:29
  (4 shorter events, 0.0 us)
Async XLA Ops:
  0.0 1.1 %copy-start = (bf16[5,64,8,128]{3,2,1,0:T(8,128)(2,1)S(1)}, bf16[5,64,8,128]{3,2,1,0:T(8,128)(2,1)}, u32[]{:S(2)}) copy-start(bf16[5,64,8,128]{3,2,1,0:T(8,128)(2,1)} %f_ref.5) | copy-start | bytes 1966084
  1.1 7.1 %copy-start.3 = (bf16[24,576]{1,0:T(8,128)(2,1)S(1)}, bf16[24,576]{1,0:T(8,128)(2,1)}, u32[]{:S(2)}) copy-start(bf16[24,576]{1,0:T(8,128)(2,1)} %wq_ref.1) | copy-start | bytes 82948
  1.1 7.1 %copy-start.4 = (bf16[24,576]{1,0:T(8,128)(2,1)S(1)}, bf16[24,576]{1,0:T(8,128)(2,1)}, u32[]{:S(2)}) copy-start(bf16[24,576]{1,0:T(8,128)(2,1)} %wk_ref.1) | copy-start | bytes 82948
  1.1 7.1 %copy-start.5 = (bf16[24,576]{1,0:T(8,128)(2,1)S(1)}, bf16[24,576]{1,0:T(8,128)(2,1)}, u32[]{:S(2)}) copy-start(bf16[24,576]{1,0:T(8,128)(2,1)} %wv_ref.1) | copy-start | bytes 82948
  1.3 11.0 %collective-permute-start = (bf16[5,128,128]{2,1,0:T(8,128)(2,1)S(1)}, bf16[5,128,128]{2,1,0:T(8,128)(2,1)S(1)}, u32[]{:S(2)}, u32[]{:S(2)}) collective-permute-start(bf16[5,128,128]{2,1,0:T(8,128)(2,1)S(1)} %get-tuple-element.12.nb_ref), channel_id=1, source_target_pairs={{0,31},{1,2},{2,1},{3,4},{4,3},{5,6},{6,5},{7,8},{8,7},{9,10},{10,... | collective-permute-start | bytes 491528 | tf_op jit(solution)/shard_map/ppermute | solution.py:203
  84.3 17.0 %copy-start.1 = (bf16[5,64,8,128]{3,2,1,0:T(8,128)(2,1)S(1)}, bf16[5,64,8,128]{3,2,1,0:T(8,128)(2,1)}, u32[]{:S(2)}) copy-start(bf16[5,64,8,128]{3,2,1,0:T(8,128)(2,1)} %f_ref.5) | copy-start | bytes 1966084
  84.9 16.4 %copy-start.2 = (bf16[64,216]{1,0:T(8,128)(2,1)S(1)}, bf16[64,216]{1,0:T(8,128)(2,1)}, u32[]{:S(2)}) copy-start(bf16[64,216]{1,0:T(8,128)(2,1)} %w_ref.1) | copy-start | bytes 82948

commit v5 on v4

--- a/solution.py
+++ b/solution.py
@@ -14,7 +14,7 @@
 MEM, LON = 16, 32
 OWN = 5
 TOTAL = MEM * OWN
-NEAR = 8
+NEAR = 16
 BAND = TOTAL // NEAR
 CUT = LAT - TOTAL
 COLS = 8
@@ -145,26 +145,27 @@
     gs[0] = gram
     gs[1] = jnp.where(lane < TOTAL, 0.0, pltpu.roll(gram, TOTAL, 1))
     gs[2] = jnp.where(lane < TOTAL, 0.0, pltpu.roll(gram, TOTAL - CUT, 1))
-    rest = jnp.zeros((4, LAT), F32)
+    rest = jnp.zeros((2, LAT), F32)
     for s in range(NEAR):
         row = s * BAND
-        free = [gs[1 + h, row + 8 + e : row + 9 + e, :] for e in range(2) for h in range(2)]
-        g_ref[s] = gs[0, row : row + 8, :] + jnp.concatenate(free + [rest], axis=0)
+        free = [gs[1 + h, row + 4 : row + 5, :] for h in range(2)]
+        g_ref[s] = gs[0, row : row + 4, :] + jnp.concatenate(free + [rest], axis=0)
 
 
 def spread_kernel(x_ref, o_ref):
     o_ref[...] = jnp.broadcast_to(jnp.sum(x_ref[...], axis=0)[None], o_ref.shape)
 
 
-def mix_kernel(scale, g_ref, v_ref, o_ref, ws, vs, ms):
-    lane = lax.broadcasted_iota(jnp.int32, (8, LAT), 1)
+def mix_kernel(scale, g_ref, v_ref, o_ref, gs, ws, vs, ms):
     for s in range(NEAR):
-        tile = g_ref[s]
-        head, tail = pltpu.roll(tile, LAT - TOTAL, 1), pltpu.roll(tile, LAT - TOTAL + CUT, 1)
-        ws[s * BAND : s * BAND + 8] = tile
-        for e in range(2):
-            row = jnp.where(lane[:1] < CUT, head[2 * e : 2 * e + 1], tail[2 * e + 1 : 2 * e + 2])
-            ws[s * BAND + 8 + e : s * BAND + 9 + e] = row
+        gs[4 * s : 4 * s + 4] = g_ref[s]
+    gram = gs[...]
+    head, tail = pltpu.roll(gram, LAT - TOTAL, 1), pltpu.roll(gram, LAT - TOTAL + CUT, 1)
+    lane = lax.broadcasted_iota(jnp.int32, (1, LAT), 1)
+    for s in range(NEAR):
+        ws[s * BAND : s * BAND + 4] = gram[4 * s : 4 * s + 4]
+        row = jnp.where(lane < CUT, head[4 * s : 4 * s + 1], tail[4 * s + 1 : 4 * s + 2])
+        ws[s * BAND + 4 : s * BAND + 5] = row
     lane = lax.broadcasted_iota(jnp.int32, (TOTAL, LAT), 1)
     s = jnp.where(lane < TOTAL, ws[...] * scale, -jnp.inf)
     e = jnp.exp(s - jnp.max(s, axis=1, keepdims=True))
@@ -234,11 +235,11 @@
         got_nb,
         alias={0: 0},
     )
-    qkv = lax.all_to_all(qkv, "mem", 0, 0, tiled=True)
-
-    near, far = ("x", "core"), ("mem", "yhi")
-    tiles = jax.ShapeDtypeStruct((NEAR, 8, LAT), F32)
-    copies = jax.ShapeDtypeStruct((MEM * LON // NEAR, 8, LAT), F32)
+    qkv = lax.all_to_all(qkv, ("z", "ylo"), 0, 0, tiled=True)
+
+    near, far = ("x", "ylo", "core"), ("z", "yhi")
+    tiles = jax.ShapeDtypeStruct((NEAR, 4, LAT), F32)
+    copies = jax.ShapeDtypeStruct((MEM * LON // NEAR, 4, LAT), F32)
     gram = call(
         gram_kernel,
         tiles,
@@ -257,6 +258,7 @@
         functools.partial(mix_kernel, scale),
         jax.ShapeDtypeStruct((MEM, OWN, ROWS, LAT), BF16),
         [
+            pltpu.VMEM((4 * NEAR, LAT), F32),
             pltpu.VMEM((TOTAL, LAT), F32),
             pltpu.VMEM((TOTAL * ROWS, LAT), F32),
             pltpu.VMEM((TOTAL * ROWS, LAT), F32),
@@ -266,7 +268,7 @@
         gram,
         qkv,
     )
-    mixed = lax.all_to_all(mixed, "mem", 0, 0, tiled=True)
+    mixed = lax.all_to_all(mixed, ("z", "ylo"), 0, 0, tiled=True)
     return call(
         finish_kernel,
         jax.ShapeDtypeStruct(fields.shape, BF16),
@@ -280,8 +282,8 @@
 
 
 def solution(mesh):
-    fine = Mesh(mesh.devices.reshape(MEM, LON // NEAR, NEAR // 2, 2), ("mem", "yhi", "x", "core"))
-    spec = P("mem", None, ("yhi", "x", "core"), None)
+    fine = Mesh(mesh.devices.reshape(MEM // 2, 2, LON // 8, 4, 2), ("z", "ylo", "yhi", "x", "core"))
+    spec = P(("z", "ylo"), None, ("yhi", "x", "core"), None)
     return jax.shard_map(
         shards,
         mesh=fine,

time: 103 us -> 102 us (level)
    all_to_all x1, blocking collectives: 20.8 us -> 18.5 us  [shards(): gram = lax.all_to_all(gram, far, 0, 0, tiled=True)]
where the time goes in v5:
time: 102 us
  blocking collectives  88.2 us (86%)
  starting transfers between devices  6.9 us (7%)
  Pallas kernels  4.99 us (5%)
  local copies, waits for them, and re-layouts  1.11 us (1%)
    all_to_all x1, blocking collectives, shards(): qkv = lax.all_to_all(qkv, ('z', 'ylo'), 0, 0, tiled=True)  34.2 us
    all_to_all x1, blocking collectives, shards(): gram = lax.all_to_all(gram, far, 0, 0, tiled=True)  18.5 us
    all_to_all x1, blocking collectives, shards(): mixed = lax.all_to_all(mixed, ('z', 'ylo'), 0, 0, tiled=True)  16.9 us
    all_to_all x2, blocking collectives, shards(): gram = lax.all_to_all(gram, near, 0, 0, tiled=True)  16.5 us
    ppermute x1, starting transfers between devices, shards(): got_nb = lax.ppermute(nb, ('yhi', 'x', 'core'), swaps)  6.9 us
    pallas_call x8, Pallas kernels, call(): pl.pallas_call(body, out_shape=outs, in_specs=[VMEM] * len(args), out_spe...  4.99 us
    all_gather x1, blocking collectives, shards(): got_sib = lax.all_gather(sib, 'core', axis=0, tiled=False)  2.04 us
  transfers between devices with their start and end apart: 1, of which 1 were waited for; matrix products, arithmetic and copies ran while one was open for 0% of the time, Pallas kernels for 1%

profile of v5, /device:TPU:8, one launch (start us, length us, event | category | flops | bytes accessed | tf_op | source)
XLA Modules:
  0.0 101.9 jit_solution(18005609731291292387)
XLA Ops:
  0.0 0.0 copy-start
  0.0 1.1 %copy-done = bf16[5,64,8,128]{3,2,1,0:T(8,128)(2,1)S(1)} copy-done((bf16[5,64,8,128]{3,2,1,0:T(8,128)(2,1)S(1)}, bf16[5,64,8,128]{3,2,1,0:T(8,128)(2,1)}, u32[]{:S(2)}) %copy-start) | copy-done | bytes 655384
  1.1 0.0 copy-start.3
  1.1 0.0 copy-start.4
  1.1 0.2 shard_map.56
  1.3 6.9 %collective-permute-start = (bf16[5,128,128]{2,1,0:T(8,128)(2,1)S(1)}, bf16[5,128,128]{2,1,0:T(8,128)(2,1)S(1)}, u32[]{:S(2)}, u32[]{:S(2)}) collective-permute-start(bf16[5,128,128]{2,1,0:T(8,128)(2,1)S(1)} %get-tuple-element.12.nb_ref), channel_id=1, source_target_pairs={{0,31},{1,2},{2,1},{3,4},{4,3},{5,6},{6,5},{7,8},{8,7},{9,10},{10,... | collective-permute-start | bytes 491528 | tf_op jit(solution)/shard_map/ppermute | solution.py:204
  8.2 0.0 copy-done.3
  8.2 0.0 copy-done.4
  8.2 0.0 copy-done.5
  8.2 1.3 %shard_map.55 = (bf16[16,5,40,128]{3,2,1,0:T(8,128)(2,1)S(1)}, bf16[432,256]{1,0:T(8,128)(2,1)S(1)}) custom-call(bf16[5,64,8,128]{3,2,1,0:T(8,128)(2,1)S(1)} %copy-done, bf16[24,576]{1,0:T(8,128)(2,1)S(1)} %copy-done.3, bf16[24,576]{1,0:T(8,128)(2,1)S(1)} %copy-done.4, bf16[24,576]{1,0:T(8,128)(2,1)S(1)} %copy-done.5), custom_call_target="tpu_custom_call" | custom-call | flops 450000000 | bytes 2000000 | tf_op jit(solution)/shard_map/pallas_call | solution.py:29
  9.6 2.0 %all-gather = bf16[10,128,128]{2,1,0:T(8,128)(2,1)S(1)} all-gather(bf16[5,128,128]{2,1,0:T(8,128)(2,1)S(1)} %get-tuple-element.11.sib_ref), channel_id=2, replica_groups=mesh['z'=8,'ylo'=2,'yhi'=4,'x'=4,'core'=2] {'core'}, dimensions={0}, use_global_device_ids=true | all-gather | bytes 491520 | tf_op jit(solution)/shard_map/all_gather | solution.py:205
  11.6 0.6 collective-permute-done.gn_ref
  12.2 0.9 shard_map.57
  13.1 34.2 %all_to_all.25.x_ref.v_ref = bf16[16,5,40,128]{3,2,1,0:T(8,128)(2,1)S(1)} all-to-all(bf16[16,5,40,128]{3,2,1,0:T(8,128)(2,1)S(1)} %shard_map.57), channel_id=1, replica_groups=mesh['z'=8,'ylo'=2,'yhi'=4,'x'=4,'core'=2] {'z','ylo'}, dimensions={0} | all-to-all | bytes 1638400 | tf_op jit(solution)/shard_map/all_to_all | solution.py:238
  47.3 0.4 shard_map.58
  47.7 7.9 %all_to_all.26.x_ref = f32[16,4,128]{2,1,0:T(4,128)S(1)} all-to-all(f32[16,4,128]{2,1,0:T(4,128)S(1)} %shard_map.58), channel_id=1, replica_groups=mesh['z'=8,'ylo'=2,'yhi'=4,'x'=4,'core'=2] {'x','ylo','core'}, dimensions={0} | all-to-all | bytes 65536 | tf_op jit(solution)/shard_map/all_to_all | solution.py:251
  55.6 18.5 %all_to_all.27.x_ref = f32[32,4,128]{2,1,0:T(4,128)S(1)} all-to-all(f32[32,4,128]{2,1,0:T(4,128)S(1)} %shard_map.59), channel_id=1, replica_groups=mesh['z'=8,'ylo'=2,'yhi'=4,'x'=4,'core'=2] {'z','yhi'}, dimensions={0} | all-to-all | bytes 131072 | tf_op jit(solution)/shard_map/all_to_all | solution.py:253
  74.2 8.6 %all_to_all.28.g_ref = f32[16,4,128]{2,1,0:T(4,128)S(1)} all-to-all(f32[16,4,128]{2,1,0:T(4,128)S(1)} %shard_map.60), channel_id=1, replica_groups=mesh['z'=8,'ylo'=2,'yhi'=4,'x'=4,'core'=2] {'x','ylo','core'}, dimensions={0} | all-to-all | bytes 65536 | tf_op jit(solution)/shard_map/all_to_all | solution.py:255
  82.8 0.7 shard_map.61
  83.5 0.0 copy-start.2
  83.5 16.9 %all_to_all.29.x_ref = bf16[16,5,16,128]{3,2,1,0:T(8,128)(2,1)S(1)} all-to-all(bf16[16,5,16,128]{3,2,1,0:T(8,128)(2,1)S(1)} %shard_map.61), channel_id=1, replica_groups=mesh['z'=8,'ylo'=2,'yhi'=4,'x'=4,'core'=2] {'z','ylo'}, dimensions={0} | all-to-all | bytes 655360 | tf_op jit(solution)/shard_map/all_to_all | solution.py:271
  100.4 0.0 copy-done.1
  100.4 0.0 copy-done.2
  100.4 1.5 %shard_map.62 = bf16[5,64,8,128]{3,2,1,0:T(8,128)(2,1)} custom-call(bf16[16,5,16,128]{3,2,1,0:T(8,128)(2,1)S(1)} %all_to_all.29.x_ref, bf16[5,64,8,128]{3,2,1,0:T(8,128)(2,1)S(1)} %copy-done.1, bf16[64,216]{1,0:T(8,128)(2,1)S(1)} %copy-done.2), custom_call_target="tpu_custom_call" | custom-call | flops 150000000 | bytes 1700000 | tf_op jit(solution)/shard_map/pallas_call | solution.py:29
  (4 shorter events, 0.1 us)
Async XLA Ops:
  0.0 1.1 %copy-start = (bf16[5,64,8,128]{3,2,1,0:T(8,128)(2,1)S(1)}, bf16[5,64,8,128]{3,2,1,0:T(8,128)(2,1)}, u32[]{:S(2)}) copy-start(bf16[5,64,8,128]{3,2,1,0:T(8,128)(2,1)} %f_ref.5) | copy-start | bytes 1966084
  1.1 7.1 %copy-start.3 = (bf16[24,576]{1,0:T(8,128)(2,1)S(1)}, bf16[24,576]{1,0:T(8,128)(2,1)}, u32[]{:S(2)}) copy-start(bf16[24,576]{1,0:T(8,128)(2,1)} %wq_ref.1) | copy-start | bytes 82948
  1.1 7.1 %copy-start.4 = (bf16[24,576]{1,0:T(8,128)(2,1)S(1)}, bf16[24,576]{1,0:T(8,128)(2,1)}, u32[]{:S(2)}) copy-start(bf16[24,576]{1,0:T(8,128)(2,1)} %wk_ref.1) | copy-start | bytes 82948
  1.1 7.1 %copy-start.5 = (bf16[24,576]{1,0:T(8,128)(2,1)S(1)}, bf16[24,576]{1,0:T(8,128)(2,1)}, u32[]{:S(2)}) copy-start(bf16[24,576]{1,0:T(8,128)(2,1)} %wv_ref.1) | copy-start | bytes 82948
  1.3 11.0 %collective-permute-start = (bf16[5,128,128]{2,1,0:T(8,128)(2,1)S(1)}, bf16[5,128,128]{2,1,0:T(8,128)(2,1)S(1)}, u32[]{:S(2)}, u32[]{:S(2)}) collective-permute-start(bf16[5,128,128]{2,1,0:T(8,128)(2,1)S(1)} %get-tuple-element.12.nb_ref), channel_id=1, source_target_pairs={{0,31},{1,2},{2,1},{3,4},{4,3},{5,6},{6,5},{7,8},{8,7},{9,10},{10,... | collective-permute-start | bytes 491528 | tf_op jit(solution)/shard_map/ppermute | solution.py:204
  82.8 17.6 %copy-start.1 = (bf16[5,64,8,128]{3,2,1,0:T(8,128)(2,1)S(1)}, bf16[5,64,8,128]{3,2,1,0:T(8,128)(2,1)}, u32[]{:S(2)}) copy-start(bf16[5,64,8,128]{3,2,1,0:T(8,128)(2,1)} %f_ref.5) | copy-start | bytes 1966084
  83.5 17.0 %copy-start.2 = (bf16[64,216]{1,0:T(8,128)(2,1)S(1)}, bf16[64,216]{1,0:T(8,128)(2,1)}, u32[]{:S(2)}) copy-start(bf16[64,216]{1,0:T(8,128)(2,1)} %w_ref.1) | copy-start | bytes 82948

commit v6 on v5

--- a/solution.py
+++ b/solution.py
@@ -24,13 +24,17 @@
 VMEM = pl.BlockSpec(memory_space=pltpu.VMEM)
 
 
-def call(body, outs, scratch, flops, nbytes, *args, alias=None):
+HBM = pl.BlockSpec(memory_space=pl.ANY)
+
+
+def call(body, outs, scratch, flops, nbytes, *args, alias=None, far_out=False):
     many = isinstance(outs, tuple)
+    one = HBM if far_out else VMEM
     return pl.pallas_call(
         body,
         out_shape=outs,
         in_specs=[VMEM] * len(args),
-        out_specs=(VMEM,) * len(outs) if many else VMEM,
+        out_specs=(one,) * len(outs) if many else one,
         scratch_shapes=scratch,
         input_output_aliases=alias or {},
         compiler_params=pltpu.CompilerParams(vmem_limit_bytes=32 * 1024 * 1024),
@@ -56,19 +60,23 @@
             nb_ref[m, s * CH : (s + 1) * CH] = jnp.where(even, left, right).astype(BF16)
 
 
-def conv_pair(w, x):
+def conv_pairs(w, xs):
     width = 3 * CQ
     lane = lax.broadcasted_iota(jnp.int32, (width, LAT), 1)
-    r = jnp.dot(w, x, preferred_element_type=F32)
-    outs = []
-    for s in range(2):
-        y = [r[(3 * s + b) * width : (3 * s + b + 1) * width] for b in range(3)]
-        outs.append(
-            y[1]
-            + jnp.where(lane == 0, 0.0, pltpu.roll(y[0], 1, 1))
-            + jnp.where(lane == LAT - 1, 0.0, pltpu.roll(y[2], LAT - 1, 1))
-        )
-    return outs
+    wide = jnp.dot(w, jnp.concatenate(xs, axis=1), preferred_element_type=F32)
+    pairs = []
+    for n in range(len(xs)):
+        r = wide[:, n * LAT : (n + 1) * LAT]
+        outs = []
+        for s in range(2):
+            y = [r[(3 * s + b) * width : (3 * s + b + 1) * width] for b in range(3)]
+            outs.append(
+                y[1]
+                + jnp.where(lane == 0, 0.0, pltpu.roll(y[0], 1, 1))
+                + jnp.where(lane == LAT - 1, 0.0, pltpu.roll(y[2], LAT - 1, 1))
+            )
+        pairs.append(outs)
+    return pairs
 
 
 def put_pair(o_ref, vs, m, p, outs):
@@ -98,10 +106,13 @@
     for m in range(OWN):
         xf[...] = f_ref[m].astype(F32).reshape(CH * COLS, LAT)
         for i in range(COLS):
-            xt[i * CH : (i + 1) * CH] = xf[pl.ds(i, CH, stride=COLS), :].astype(BF16)
-        for p in range(1, EXT // 2 - 1):
-            x = xt[2 * (p - 1) * CH : 2 * (p + 1) * CH]
-            put_pair(o_ref, vs, m, p, conv_pair(wp_ref[...], x))
+            xt[m, i * CH : (i + 1) * CH] = xf[pl.ds(i, CH, stride=COLS), :].astype(BF16)
+    units = [(m, p) for m in range(OWN) for p in range(1, EXT // 2 - 1)]
+    for n in range(0, len(units), 2):
+        two = units[n : n + 2]
+        xs = [xt[m, 2 * (p - 1) * CH : 2 * (p + 1) * CH] for m, p in two]
+        for (m, p), outs in zip(two, conv_pairs(wp_ref[...], xs)):
+            put_pair(o_ref, vs, m, p, outs)
 
 
 def outer_kernel(i_ref, wp_ref, sib_ref, nb_ref, gs_ref, gn_ref, o_ref, xl, xr, vs):
@@ -123,8 +134,9 @@
         xr[:, near:] = gn_ref[...]
 
     for m in range(OWN):
-        put_pair(o_ref, vs, m, 0, conv_pair(wp_ref[...], xl[m]))
-        put_pair(o_ref, vs, m, EXT // 2 - 1, conv_pair(wp_ref[...], xr[m]))
+        left, right = conv_pairs(wp_ref[...], [xl[m], xr[m]])
+        put_pair(o_ref, vs, m, 0, left)
+        put_pair(o_ref, vs, m, EXT // 2 - 1, right)
         o_ref[MEM - 1, m, CQ:] = jnp.zeros((ROWS, LAT), BF16)
 
 
@@ -178,7 +190,8 @@
     o_ref[...] = ms[...].astype(BF16).reshape(o_ref.shape)
 
 
-def finish_kernel(x_ref, f_ref, w_ref, o_ref, mc, mb, ma, br):
+def finish_kernel(x_ref, f_ref, w_ref, o_ref, mc, mb, ma, br, ob, sem):
+    copies = [pltpu.make_async_copy(ob.at[m], o_ref.at[m], sem.at[m]) for m in range(OWN)]
     for m in range(OWN):
         for j in range(MEM):
             mc[j * ROWS : (j + 1) * ROWS] = x_ref[j, m].astype(F32)
@@ -193,7 +206,10 @@
             r = jnp.dot(w_ref[...], jnp.concatenate(patches, axis=1), preferred_element_type=F32)
             for s in range(2):
                 br[pl.ds(i + s, CH, stride=COLS), :] = r[:, s * LAT : (s + 1) * LAT]
-        o_ref[m] = (f_ref[m].astype(F32) + br[...].reshape(CH, COLS, LAT)).astype(BF16)
+        ob[m] = (f_ref[m].astype(F32) + br[...].reshape(CH, COLS, LAT)).astype(BF16)
+        copies[m].start()
+    for copy in copies:
+        copy.wait()
 
 
 def shards(fields, w_query, w_key, w_value, w_out):
@@ -211,7 +227,7 @@
         [
             pltpu.VMEM((3 * CQ, 9 * CH), F32),
             plane,
-            pltpu.VMEM((CH * COLS, LAT), BF16),
+            pltpu.VMEM((OWN, CH * COLS, LAT), BF16),
             pltpu.VMEM((2 * CQ, LAT), F32),
         ],
         450_000_000,
@@ -272,12 +288,14 @@
     return call(
         finish_kernel,
         jax.ShapeDtypeStruct(fields.shape, BF16),
-        [pltpu.VMEM((MEM * ROWS, LAT), F32)] * 3 + [pltpu.VMEM((CH * COLS, LAT), F32)],
+        [pltpu.VMEM((MEM * ROWS, LAT), F32)] * 3
+        + [plane, pltpu.VMEM(fields.shape, BF16), pltpu.SemaphoreType.DMA((OWN,))],
         150_000_000,
         1_700_000,
         mixed,
         fields,
         w_out,
+        far_out=True,
     )
 
 

time: 102 us -> 102 us (level)
  no operation moved by 1% of the time
where the time goes in v6:
time: 102 us
  blocking collectives  88.2 us (86%)
  starting transfers between devices  6.9 us (7%)
  Pallas kernels  4.31 us (4%)
  local copies, waits for them, and re-layouts  1.11 us (1%)
    all_to_all x1, blocking collectives, shards(): qkv = lax.all_to_all(qkv, ('z', 'ylo'), 0, 0, tiled=True)  33.9 us
    all_to_all x1, blocking collectives, shards(): gram = lax.all_to_all(gram, far, 0, 0, tiled=True)  18.8 us
    all_to_all x1, blocking collectives, shards(): mixed = lax.all_to_all(mixed, ('z', 'ylo'), 0, 0, tiled=True)  16.9 us
    all_to_all x2, blocking collectives, shards(): gram = lax.all_to_all(gram, near, 0, 0, tiled=True)  16.5 us
    ppermute x1, starting transfers between devices, shards(): got_nb = lax.ppermute(nb, ('yhi', 'x', 'core'), swaps)  6.9 us
    pallas_call x8, Pallas kernels, call(): pl.pallas_call(body, out_shape=outs, in_specs=[VMEM] * len(args), out_spe...  4.31 us
    all_gather x1, blocking collectives, shards(): got_sib = lax.all_gather(sib, 'core', axis=0, tiled=False)  2.04 us
  transfers between devices with their start and end apart: 1, of which 1 were waited for; matrix products, arithmetic and copies ran while one was open for 0% of the time, Pallas kernels for 1%

profile of v6, /device:TPU:8, one launch (start us, length us, event | category | flops | bytes accessed | tf_op | source)
XLA Modules:
  0.0 101.5 jit_solution(7576667258170616477)
XLA Ops:
  0.0 0.0 copy-start
  0.0 1.1 %copy-done = bf16[5,64,8,128]{3,2,1,0:T(8,128)(2,1)S(1)} copy-done((bf16[5,64,8,128]{3,2,1,0:T(8,128)(2,1)S(1)}, bf16[5,64,8,128]{3,2,1,0:T(8,128)(2,1)}, u32[]{:S(2)}) %copy-start) | copy-done | bytes 655384
  1.1 0.0 copy-start.3
  1.1 0.0 copy-start.4
  1.1 0.2 shard_map.56
  1.3 6.9 %collective-permute-start = (bf16[5,128,128]{2,1,0:T(8,128)(2,1)S(1)}, bf16[5,128,128]{2,1,0:T(8,128)(2,1)S(1)}, u32[]{:S(2)}, u32[]{:S(2)}) collective-permute-start(bf16[5,128,128]{2,1,0:T(8,128)(2,1)S(1)} %get-tuple-element.12.nb_ref), channel_id=1, source_target_pairs={{0,31},{1,2},{2,1},{3,4},{4,3},{5,6},{6,5},{7,8},{8,7},{9,10},{10,... | collective-permute-start | bytes 491528 | tf_op jit(solution)/shard_map/ppermute | solution.py:220
  8.2 0.0 copy-done.3
  8.2 0.0 copy-done.4
  8.2 0.0 copy-done.5
  8.2 1.0 %shard_map.55 = (bf16[16,5,40,128]{3,2,1,0:T(8,128)(2,1)S(1)}, bf16[432,256]{1,0:T(8,128)(2,1)S(1)}) custom-call(bf16[5,64,8,128]{3,2,1,0:T(8,128)(2,1)S(1)} %copy-done, bf16[24,576]{1,0:T(8,128)(2,1)S(1)} %copy-done.3, bf16[24,576]{1,0:T(8,128)(2,1)S(1)} %copy-done.4, bf16[24,576]{1,0:T(8,128)(2,1)S(1)} %copy-done.5), custom_call_target="tpu_custom_call" | custom-call | flops 450000000 | bytes 2000000 | tf_op jit(solution)/shard_map/pallas_call | solution.py:33
  9.3 2.0 %all-gather = bf16[10,128,128]{2,1,0:T(8,128)(2,1)S(1)} all-gather(bf16[5,128,128]{2,1,0:T(8,128)(2,1)S(1)} %get-tuple-element.11.sib_ref), channel_id=2, replica_groups=mesh['z'=8,'ylo'=2,'yhi'=4,'x'=4,'core'=2] {'core'}, dimensions={0}, use_global_device_ids=true | all-gather | bytes 491520 | tf_op jit(solution)/shard_map/all_gather | solution.py:221
  11.3 0.9 collective-permute-done.gn_ref
  12.2 0.6 shard_map.57
  12.8 33.9 %all_to_all.25.x_ref.v_ref = bf16[16,5,40,128]{3,2,1,0:T(8,128)(2,1)S(1)} all-to-all(bf16[16,5,40,128]{3,2,1,0:T(8,128)(2,1)S(1)} %shard_map.57), channel_id=1, replica_groups=mesh['z'=8,'ylo'=2,'yhi'=4,'x'=4,'core'=2] {'z','ylo'}, dimensions={0} | all-to-all | bytes 1638400 | tf_op jit(solution)/shard_map/all_to_all | solution.py:254
  46.7 0.4 shard_map.58
  47.1 7.9 %all_to_all.26.x_ref = f32[16,4,128]{2,1,0:T(4,128)S(1)} all-to-all(f32[16,4,128]{2,1,0:T(4,128)S(1)} %shard_map.58), channel_id=1, replica_groups=mesh['z'=8,'ylo'=2,'yhi'=4,'x'=4,'core'=2] {'x','ylo','core'}, dimensions={0} | all-to-all | bytes 65536 | tf_op jit(solution)/shard_map/all_to_all | solution.py:267
  55.1 18.8 %all_to_all.27.x_ref = f32[32,4,128]{2,1,0:T(4,128)S(1)} all-to-all(f32[32,4,128]{2,1,0:T(4,128)S(1)} %shard_map.59), channel_id=1, replica_groups=mesh['z'=8,'ylo'=2,'yhi'=4,'x'=4,'core'=2] {'z','yhi'}, dimensions={0} | all-to-all | bytes 131072 | tf_op jit(solution)/shard_map/all_to_all | solution.py:269
  73.9 8.6 %all_to_all.28.g_ref = f32[16,4,128]{2,1,0:T(4,128)S(1)} all-to-all(f32[16,4,128]{2,1,0:T(4,128)S(1)} %shard_map.60), channel_id=1, replica_groups=mesh['z'=8,'ylo'=2,'yhi'=4,'x'=4,'core'=2] {'x','ylo','core'}, dimensions={0} | all-to-all | bytes 65536 | tf_op jit(solution)/shard_map/all_to_all | solution.py:271
  82.5 0.7 shard_map.61
  83.2 0.0 copy-start.2
  83.2 16.9 %all_to_all.29.x_ref = bf16[16,5,16,128]{3,2,1,0:T(8,128)(2,1)S(1)} all-to-all(bf16[16,5,16,128]{3,2,1,0:T(8,128)(2,1)S(1)} %shard_map.61), channel_id=1, replica_groups=mesh['z'=8,'ylo'=2,'yhi'=4,'x'=4,'core'=2] {'z','ylo'}, dimensions={0} | all-to-all | bytes 655360 | tf_op jit(solution)/shard_map/all_to_all | solution.py:287
  100.1 0.0 copy-done.1
  100.1 0.0 copy-done.2
  100.1 1.4 %shard_map.62 = bf16[5,64,8,128]{3,2,1,0:T(8,128)(2,1)} custom-call(bf16[16,5,16,128]{3,2,1,0:T(8,128)(2,1)S(1)} %all_to_all.29.x_ref, bf16[5,64,8,128]{3,2,1,0:T(8,128)(2,1)S(1)} %copy-done.1, bf16[64,216]{1,0:T(8,128)(2,1)S(1)} %copy-done.2), custom_call_target="tpu_custom_call" | custom-call | flops 150000000 | bytes 1700000 | tf_op jit(solution)/shard_map/pallas_call | solution.py:33
  (4 shorter events, 0.1 us)
Async XLA Ops:
  0.0 1.1 %copy-start = (bf16[5,64,8,128]{3,2,1,0:T(8,128)(2,1)S(1)}, bf16[5,64,8,128]{3,2,1,0:T(8,128)(2,1)}, u32[]{:S(2)}) copy-start(bf16[5,64,8,128]{3,2,1,0:T(8,128)(2,1)} %f_ref.5) | copy-start | bytes 1966084
  1.1 7.1 %copy-start.3 = (bf16[24,576]{1,0:T(8,128)(2,1)S(1)}, bf16[24,576]{1,0:T(8,128)(2,1)}, u32[]{:S(2)}) copy-start(bf16[24,576]{1,0:T(8,128)(2,1)} %wq_ref.1) | copy-start | bytes 82948
  1.1 7.1 %copy-start.4 = (bf16[24,576]{1,0:T(8,128)(2,1)S(1)}, bf16[24,576]{1,0:T(8,128)(2,1)}, u32[]{:S(2)}) copy-start(bf16[24,576]{1,0:T(8,128)(2,1)} %wk_ref.1) | copy-start | bytes 82948
  1.1 7.1 %copy-start.5 = (bf16[24,576]{1,0:T(8,128)(2,1)S(1)}, bf16[24,576]{1,0:T(8,128)(2,1)}, u32[]{:S(2)}) copy-start(bf16[24,576]{1,0:T(8,128)(2,1)} %wv_ref.1) | copy-start | bytes 82948
  1.3 11.0 %collective-permute-start = (bf16[5,128,128]{2,1,0:T(8,128)(2,1)S(1)}, bf16[5,128,128]{2,1,0:T(8,128)(2,1)S(1)}, u32[]{:S(2)}, u32[]{:S(2)}) collective-permute-start(bf16[5,128,128]{2,1,0:T(8,128)(2,1)S(1)} %get-tuple-element.12.nb_ref), channel_id=1, source_target_pairs={{0,31},{1,2},{2,1},{3,4},{4,3},{5,6},{6,5},{7,8},{8,7},{9,10},{10,... | collective-permute-start | bytes 491528 | tf_op jit(solution)/shard_map/ppermute | solution.py:220
  82.5 17.6 %copy-start.1 = (bf16[5,64,8,128]{3,2,1,0:T(8,128)(2,1)S(1)}, bf16[5,64,8,128]{3,2,1,0:T(8,128)(2,1)}, u32[]{:S(2)}) copy-start(bf16[5,64,8,128]{3,2,1,0:T(8,128)(2,1)} %f_ref.5) | copy-start | bytes 1966084
  83.2 17.0 %copy-start.2 = (bf16[64,216]{1,0:T(8,128)(2,1)S(1)}, bf16[64,216]{1,0:T(8,128)(2,1)}, u32[]{:S(2)}) copy-start(bf16[64,216]{1,0:T(8,128)(2,1)} %w_ref.1) | copy-start | bytes 82948

commit v7 on v6

--- a/solution.py
+++ b/solution.py
@@ -14,8 +14,7 @@
 MEM, LON = 16, 32
 OWN = 5
 TOTAL = MEM * OWN
-NEAR = 16
-BAND = TOTAL // NEAR
+HEAD = 16
 CUT = LAT - TOTAL
 COLS = 8
 EXT = COLS + 2
@@ -79,18 +78,18 @@
     return pairs
 
 
-def put_pair(o_ref, vs, m, p, outs):
+def put_pair(qk_ref, v_ref, vs, m, p, outs):
     for s in range(2):
         col = 2 * p + s
         vs[s * CQ : (s + 1) * CQ] = outs[s][2 * CQ :]
         if 1 <= col <= COLS:
             for h in range(2):
-                o_ref[2 * (col - 1) + h, m, 0:CQ] = outs[s][h * CQ : (h + 1) * CQ].astype(BF16)
-    for j in range(3):
-        o_ref[3 * p + j, m, CQ:] = vs[j * ROWS : (j + 1) * ROWS].astype(BF16)
-
-
-def inner_kernel(f_ref, wq_ref, wk_ref, wv_ref, o_ref, wp_ref, ws, xf, xt, vs):
+                qk_ref[2 * (col - 1) + h, m] = outs[s][h * CQ : (h + 1) * CQ].astype(BF16)
+    for n in range(6):
+        v_ref[3 * p + n // 2, n % 2, m] = vs[n * 8 : (n + 1) * 8].astype(BF16)
+
+
+def inner_kernel(f_ref, wq_ref, wk_ref, wv_ref, qk_ref, v_ref, wp_ref, ws, xf, xt, vs):
     ws[0:HALF] = wq_ref[...].astype(F32)[:HALF]
     ws[HALF : 2 * HALF] = wk_ref[...].astype(F32)[:HALF]
     ws[2 * HALF : 3 * HALF] = wq_ref[...].astype(F32)[HALF:]
@@ -112,10 +111,12 @@
         two = units[n : n + 2]
         xs = [xt[m, 2 * (p - 1) * CH : 2 * (p + 1) * CH] for m, p in two]
         for (m, p), outs in zip(two, conv_pairs(wp_ref[...], xs)):
-            put_pair(o_ref, vs, m, p, outs)
-
-
-def outer_kernel(i_ref, wp_ref, sib_ref, nb_ref, gs_ref, gn_ref, o_ref, xl, xr, vs):
+            put_pair(qk_ref, v_ref, vs, m, p, outs)
+
+
+def outer_kernel(
+    iq_ref, iv_ref, wp_ref, sib_ref, nb_ref, gs_ref, gn_ref, qk_ref, v_ref, xl, xr, vs
+):
     core = lax.axis_index("core")
     near = 2 * CH
 
@@ -135,13 +136,14 @@
 
     for m in range(OWN):
         left, right = conv_pairs(wp_ref[...], [xl[m], xr[m]])
-        put_pair(o_ref, vs, m, 0, left)
-        put_pair(o_ref, vs, m, EXT // 2 - 1, right)
-        o_ref[MEM - 1, m, CQ:] = jnp.zeros((ROWS, LAT), BF16)
-
-
-def gram_kernel(x_ref, g_ref, xs, gs):
-    xs[...] = x_ref[:, :, 0:CQ, :].astype(F32).reshape(TOTAL * CQ, LAT)
+        put_pair(qk_ref, v_ref, vs, m, 0, left)
+        put_pair(qk_ref, v_ref, vs, m, EXT // 2 - 1, right)
+        for h in range(2):
+            v_ref[MEM - 1, h, m] = jnp.zeros((8, LAT), BF16)
+
+
+def gram_kernel(x_ref, v_ref, o_ref, xs, gs, ps):
+    xs[...] = x_ref[...].astype(F32).reshape(TOTAL * CQ, LAT)
     pad = jnp.zeros((LAT - TOTAL, LAT), BF16)
     q, k = [], []
     for r in range(HALF):
@@ -158,33 +160,55 @@
     gs[1] = jnp.where(lane < TOTAL, 0.0, pltpu.roll(gram, TOTAL, 1))
     gs[2] = jnp.where(lane < TOTAL, 0.0, pltpu.roll(gram, TOTAL - CUT, 1))
     rest = jnp.zeros((2, LAT), F32)
-    for s in range(NEAR):
-        row = s * BAND
+    for s in range(MEM):
+        row = s * OWN
         free = [gs[1 + h, row + 4 : row + 5, :] for h in range(2)]
-        g_ref[s] = gs[0, row : row + 4, :] + jnp.concatenate(free + [rest], axis=0)
+        ps[0, 4 * s : 4 * s + 4] = gs[0, row : row + 4, :] + jnp.concatenate(free + [rest], axis=0)
+    for part in range(2):
+        whole = ps[part]
+        high = whole.astype(BF16).astype(F32)
+        ps[part] = high
+        ps[part + 1] = whole - high
+    for s in range(MEM):
+        for part in range(3):
+            ps[3, 4 * part : 4 * part + 4] = ps[part, 4 * s : 4 * s + 4]
+        ps[3, 12:HEAD] = jnp.zeros((HEAD - 12, LAT), F32)
+        o_ref[s, 0:HEAD] = ps[3, 0:HEAD].astype(BF16)
+    o_ref[:, HEAD:] = v_ref[:, 0].astype(F32).reshape(MEM, OWN * 8, LAT).astype(BF16)
+
+
+def total_kernel(x_ref, o_ref):
+    parts = jnp.sum(x_ref[:, 0:HEAD].astype(F32), axis=0)
+    o_ref[...] = parts[0:4] + parts[4:8] + parts[8:12]
 
 
 def spread_kernel(x_ref, o_ref):
-    o_ref[...] = jnp.broadcast_to(jnp.sum(x_ref[...], axis=0)[None], o_ref.shape)
-
-
-def mix_kernel(scale, g_ref, v_ref, o_ref, gs, ws, vs, ms):
-    for s in range(NEAR):
-        gs[4 * s : 4 * s + 4] = g_ref[s]
+    o_ref[...] = jnp.broadcast_to((x_ref[0] + x_ref[1])[None], o_ref.shape)
+
+
+def softmax_kernel(scale, x_ref, v_ref, o_ref, gs):
+    gs[...] = jnp.zeros(gs.shape, F32)
+    gs[0:4] = jnp.sum(x_ref[...], axis=0)
     gram = gs[...]
     head, tail = pltpu.roll(gram, LAT - TOTAL, 1), pltpu.roll(gram, LAT - TOTAL + CUT, 1)
-    lane = lax.broadcasted_iota(jnp.int32, (1, LAT), 1)
-    for s in range(NEAR):
-        ws[s * BAND : s * BAND + 4] = gram[4 * s : 4 * s + 4]
-        row = jnp.where(lane < CUT, head[4 * s : 4 * s + 1], tail[4 * s + 1 : 4 * s + 2])
-        ws[s * BAND + 4 : s * BAND + 5] = row
-    lane = lax.broadcasted_iota(jnp.int32, (TOTAL, LAT), 1)
-    s = jnp.where(lane < TOTAL, ws[...] * scale, -jnp.inf)
+    lane = lax.broadcasted_iota(jnp.int32, gram.shape, 1)
+    gs[4:5] = jnp.where(lane[0:1] < CUT, head[0:1], tail[1:2])
+    s = jnp.where(lane < TOTAL, gs[...] * scale, -jnp.inf)
     e = jnp.exp(s - jnp.max(s, axis=1, keepdims=True))
-    w = (e / jnp.sum(e, axis=1, keepdims=True)).astype(BF16)[:, :TOTAL]
-    vs[...] = v_ref[:, :, CQ:, :].astype(F32).reshape(TOTAL * ROWS, LAT)
-    v = jnp.concatenate([vs[pl.ds(r, TOTAL, stride=ROWS), :].astype(BF16) for r in range(ROWS)], axis=1)
-    mixed = jnp.dot(w, v, preferred_element_type=F32)
+    w = (e / jnp.sum(e, axis=1, keepdims=True)).astype(BF16)
+    o_ref[:, 0:HEAD] = jnp.broadcast_to(w[None], (MEM, HEAD, LAT))
+    o_ref[:, HEAD:] = v_ref[:, 1].astype(F32).reshape(MEM, OWN * 8, LAT).astype(BF16)
+
+
+def mix_kernel(a_ref, b_ref, o_ref, ws, vs, ms):
+    for s in range(MEM):
+        ws[s * OWN : (s + 1) * OWN, :] = b_ref[s, 0:HEAD].astype(F32)[0:OWN]
+    w = ws[...].astype(BF16)[:, :TOTAL]
+    v = []
+    for h, ref in enumerate((a_ref, b_ref)):
+        vs[h] = ref[:, HEAD:].astype(F32).reshape(TOTAL * 8, LAT)
+        v += [vs[h, pl.ds(r, TOTAL, stride=8), :].astype(BF16) for r in range(8)]
+    mixed = jnp.dot(w, jnp.concatenate(v, axis=1), preferred_element_type=F32)
     for r in range(ROWS):
         ms[pl.ds(r, TOTAL, stride=ROWS), :] = mixed[:, r * LAT : (r + 1) * LAT]
     o_ref[...] = ms[...].astype(BF16).reshape(o_ref.shape)
@@ -219,11 +243,12 @@
     swaps = [(i, (i - 1 if i % 2 == 0 else i + 1) % LON) for i in range(LON)]
     got_nb = lax.ppermute(nb, ("yhi", "x", "core"), swaps)
     got_sib = lax.all_gather(sib, "core", axis=0, tiled=False)
-    packed = jax.ShapeDtypeStruct((MEM, OWN, CQ + ROWS, LAT), BF16)
+    qk_shape = jax.ShapeDtypeStruct((MEM, OWN, CQ, LAT), BF16)
+    v_shape = jax.ShapeDtypeStruct((MEM, 2, OWN, 8, LAT), BF16)
     pair = jax.ShapeDtypeStruct((18 * CQ, 4 * CH), BF16)
-    part, w_pair = call(
+    qk, v, w_pair = call(
         inner_kernel,
-        (packed, pair),
+        (qk_shape, v_shape, pair),
         [
             pltpu.VMEM((3 * CQ, 9 * CH), F32),
             plane,
@@ -237,52 +262,67 @@
         w_key,
         w_value,
     )
-    qkv = call(
+    qk, v = call(
         outer_kernel,
-        packed,
+        (qk_shape, v_shape),
         [pltpu.VMEM((OWN, 4 * CH, LAT), BF16)] * 2 + [pltpu.VMEM((2 * CQ, LAT), F32)],
         300_000_000,
         1_500_000,
-        part,
+        qk,
+        v,
         w_pair,
         sib,
         nb,
         got_sib,
         got_nb,
-        alias={0: 0},
-    )
-    qkv = lax.all_to_all(qkv, ("z", "ylo"), 0, 0, tiled=True)
-
-    near, far = ("x", "ylo", "core"), ("z", "yhi")
-    tiles = jax.ShapeDtypeStruct((NEAR, 4, LAT), F32)
-    copies = jax.ShapeDtypeStruct((MEM * LON // NEAR, 4, LAT), F32)
-    gram = call(
+        alias={0: 0, 1: 1},
+    )
+    mem, lon = ("z", "ylo"), ("yhi", "x")
+    qk = lax.all_to_all(qk, mem, 0, 0, tiled=True)
+
+    packed = jax.ShapeDtypeStruct((MEM, HEAD + OWN * 8, LAT), BF16)
+    first = call(
         gram_kernel,
-        tiles,
-        [pltpu.VMEM((TOTAL * CQ, LAT), F32), pltpu.VMEM((3, TOTAL, LAT), F32)],
+        packed,
+        [
+            pltpu.VMEM((TOTAL * CQ, LAT), F32),
+            pltpu.VMEM((3, TOTAL, LAT), F32),
+            pltpu.VMEM((4, 4 * MEM, LAT), F32),
+        ],
         20_000_000,
-        600_000,
-        qkv,
-    )
-    gram = lax.all_to_all(gram, near, 0, 0, tiled=True)
-    gram = call(spread_kernel, copies, [], 20_000, 300_000, gram)
-    gram = lax.all_to_all(gram, far, 0, 0, tiled=True)
-    gram = call(spread_kernel, tiles, [], 80_000, 300_000, gram)
-    gram = lax.all_to_all(gram, near, 0, 0, tiled=True)
+        800_000,
+        qk,
+        v,
+    )
+    first = lax.all_to_all(first, mem, 0, 0, tiled=True)
+    gram = call(total_kernel, jax.ShapeDtypeStruct((4, LAT), F32), [], 40_000, 200_000, first)
+    gram = lax.all_gather(gram, "core", axis=0, tiled=False)
+    copies = jax.ShapeDtypeStruct((LON // 2, 4, LAT), F32)
+    gram = call(spread_kernel, copies, [], 10_000, 40_000, gram)
+    gram = lax.all_to_all(gram, lon, 0, 0, tiled=True)
     scale = 1.0 / math.sqrt(CQ * LAT * COLS * LON)
+    second = call(
+        functools.partial(softmax_kernel, scale),
+        packed,
+        [pltpu.VMEM((HEAD, LAT), F32)],
+        40_000,
+        400_000,
+        gram,
+        v,
+    )
+    second = lax.all_to_all(second, mem, 0, 0, tiled=True)
     mixed = call(
-        functools.partial(mix_kernel, scale),
+        mix_kernel,
         jax.ShapeDtypeStruct((MEM, OWN, ROWS, LAT), BF16),
         [
-            pltpu.VMEM((4 * NEAR, LAT), F32),
             pltpu.VMEM((TOTAL, LAT), F32),
-            pltpu.VMEM((TOTAL * ROWS, LAT), F32),
+            pltpu.VMEM((2, TOTAL * 8, LAT), F32),
             pltpu.VMEM((TOTAL * ROWS, LAT), F32),
         ],
         30_000_000,
         700_000,
-        gram,
-        qkv,
+        first,
+        second,
     )
     mixed = lax.all_to_all(mixed, ("z", "ylo"), 0, 0, tiled=True)
     return call(

time: 102 us -> 101 us (level)
  the two profiles are of different devices: /device:TPU:8 before, /device:TPU:4 now
where the time goes in v7:
time: 101 us
  blocking collectives  92.7 us (92%)
  Pallas kernels  4.37 us (4%)
  starting transfers between devices  1.92 us (2%)
  local copies, waits for them, and re-layouts  1.11 us (1%)
    all_to_all x1, blocking collectives, shards(): qk = lax.all_to_all(qk, mem, 0, 0, tiled=True)  27.8 us
    all_to_all x1, blocking collectives, shards(): gram = lax.all_to_all(gram, lon, 0, 0, tiled=True)  17.5 us
    all_to_all x1, blocking collectives, shards(): mixed = lax.all_to_all(mixed, ('z', 'ylo'), 0, 0, tiled=True)  15.4 us
    all_to_all x1, blocking collectives, shards(): first = lax.all_to_all(first, mem, 0, 0, tiled=True)  14.1 us
    all_to_all x1, blocking collectives, shards(): second = lax.all_to_all(second, mem, 0, 0, tiled=True)  13.1 us
    pallas_call x9, Pallas kernels, call(): pl.pallas_call(body, out_shape=outs, in_specs=[VMEM] * len(args), out_spe...  4.37 us
    all_gather x1, blocking collectives, shards(): got_sib = lax.all_gather(sib, 'core', axis=0, tiled=False)  2.98 us
  transfers between devices with their start and end apart: 1, of which 1 were waited for; matrix products, arithmetic and copies ran while one was open for 0% of the time, Pallas kernels for 1%

profile of v7, /device:TPU:4, one launch (start us, length us, event | category | flops | bytes accessed | tf_op | source)
XLA Modules:
  0.0 100.8 jit_solution(3846560977127004878)
XLA Ops:
  0.0 0.0 copy-start
  0.0 1.1 %copy-done = bf16[5,64,8,128]{3,2,1,0:T(8,128)(2,1)S(1)} copy-done((bf16[5,64,8,128]{3,2,1,0:T(8,128)(2,1)S(1)}, bf16[5,64,8,128]{3,2,1,0:T(8,128)(2,1)}, u32[]{:S(2)}) %copy-start) | copy-done | bytes 655384
  1.1 0.2 shard_map.56
  1.3 1.9 %collective-permute-start = (bf16[5,128,128]{2,1,0:T(8,128)(2,1)S(1)}, bf16[5,128,128]{2,1,0:T(8,128)(2,1)S(1)}, u32[]{:S(2)}, u32[]{:S(2)}) collective-permute-start(bf16[5,128,128]{2,1,0:T(8,128)(2,1)S(1)} %get-tuple-element.16.nb_ref), channel_id=1, source_target_pairs={{0,31},{1,2},{2,1},{3,4},{4,3},{5,6},{6,5},{7,8},{8,7},{9,10},{10,... | collective-permute-start | bytes 491528 | tf_op jit(solution)/shard_map/ppermute | solution.py:244
  3.2 0.0 copy-done.3
  3.2 0.0 copy-done.4
  3.2 0.0 copy-done.5
  3.2 1.0 %shard_map.55 = (bf16[16,5,24,128]{3,2,1,0:T(8,128)(2,1)S(1)}, bf16[16,2,5,8,128]{4,3,2,1,0:T(8,128)(2,1)S(1)}, bf16[432,256]{1,0:T(8,128)(2,1)S(1)}) custom-call(bf16[5,64,8,128]{3,2,1,0:T(8,128)(2,1)S(1)} %copy-done, bf16[24,576]{1,0:T(8,128)(2,1)S(1)} %copy-done.3, bf16[24,576]{1,0:T(8,128)(2,1)S(1)} %copy-done.4, bf16[24,576]{1,0:T(8,128)(2,1)S(1)} %copy-done.5), custom_call_target="tpu_custom_call" | custom-call | flops 450000000 | bytes 2000000 | tf_op jit(solution)/shard_map/pallas_call | solution.py:32
  4.3 3.0 %all-gather = bf16[10,128,128]{2,1,0:T(8,128)(2,1)S(1)} all-gather(bf16[5,128,128]{2,1,0:T(8,128)(2,1)S(1)} %get-tuple-element.15.sib_ref), channel_id=2, replica_groups=mesh['z'=8,'ylo'=2,'yhi'=4,'x'=4,'core'=2] {'core'}, dimensions={0}, use_global_device_ids=true | all-gather | bytes 491520 | tf_op jit(solution)/shard_map/all_gather | solution.py:245
  7.3 0.7 collective-permute-done.gn_ref
  7.9 0.6 shard_map.57
  8.5 27.8 %all_to_all.25.x_ref = bf16[16,5,24,128]{3,2,1,0:T(8,128)(2,1)S(1)} all-to-all(bf16[16,5,24,128]{3,2,1,0:T(8,128)(2,1)S(1)} %get-tuple-element.17), channel_id=1, replica_groups=mesh['z'=8,'ylo'=2,'yhi'=4,'x'=4,'core'=2] {'z','ylo'}, dimensions={0} | all-to-all | bytes 983040 | tf_op jit(solution)/shard_map/all_to_all | solution.py:281
  36.3 0.5 shard_map.58
  36.8 14.1 %all_to_all.26.x_ref.a_ref = bf16[16,56,128]{2,1,0:T(8,128)(2,1)S(1)} all-to-all(bf16[16,56,128]{2,1,0:T(8,128)(2,1)S(1)} %shard_map.58), channel_id=1, replica_groups=mesh['z'=8,'ylo'=2,'yhi'=4,'x'=4,'core'=2] {'z','ylo'}, dimensions={0} | all-to-all | bytes 458752 | tf_op jit(solution)/shard_map/all_to_all | solution.py:297
  50.9 1.8 %all-gather.2.x_ref = f32[2,4,128]{2,1,0:T(4,128)S(1)} all-gather(f32[1,4,128]{2,1,0:T(4,128)S(1)} %bitcast.3), channel_id=3, replica_groups=mesh['z'=8,'ylo'=2,'yhi'=4,'x'=4,'core'=2] {'core'}, dimensions={0}, use_global_device_ids=true | all-gather | bytes 6144 | tf_op jit(solution)/shard_map/all_gather | solution.py:299
  52.7 17.5 %all_to_all.27.x_ref = f32[16,4,128]{2,1,0:T(4,128)S(1)} all-to-all(f32[16,4,128]{2,1,0:T(4,128)S(1)} %shard_map.60), channel_id=1, replica_groups=mesh['z'=8,'ylo'=2,'yhi'=4,'x'=4,'core'=2] {'yhi','x'}, dimensions={0} | all-to-all | bytes 65536 | tf_op jit(solution)/shard_map/all_to_all | solution.py:302
  70.2 0.3 shard_map.61
  70.4 13.1 %all_to_all.28.b_ref = bf16[16,56,128]{2,1,0:T(8,128)(2,1)S(1)} all-to-all(bf16[16,56,128]{2,1,0:T(8,128)(2,1)S(1)} %shard_map.61), channel_id=1, replica_groups=mesh['z'=8,'ylo'=2,'yhi'=4,'x'=4,'core'=2] {'z','ylo'}, dimensions={0} | all-to-all | bytes 458752 | tf_op jit(solution)/shard_map/all_to_all | solution.py:313
  83.6 0.4 shard_map.62
  84.0 0.0 copy-start.2
  84.0 15.4 %all_to_all.29.x_ref = bf16[16,5,16,128]{3,2,1,0:T(8,128)(2,1)S(1)} all-to-all(bf16[16,5,16,128]{3,2,1,0:T(8,128)(2,1)S(1)} %shard_map.62), channel_id=1, replica_groups=mesh['z'=8,'ylo'=2,'yhi'=4,'x'=4,'core'=2] {'z','ylo'}, dimensions={0} | all-to-all | bytes 655360 | tf_op jit(solution)/shard_map/all_to_all | solution.py:327
  99.4 0.0 copy-done.1
  99.4 0.0 copy-done.2
  99.4 1.4 %shard_map.63 = bf16[5,64,8,128]{3,2,1,0:T(8,128)(2,1)} custom-call(bf16[16,5,16,128]{3,2,1,0:T(8,128)(2,1)S(1)} %all_to_all.29.x_ref, bf16[5,64,8,128]{3,2,1,0:T(8,128)(2,1)S(1)} %copy-done.1, bf16[64,216]{1,0:T(8,128)(2,1)S(1)} %copy-done.2), custom_call_target="tpu_custom_call" | custom-call | flops 150000000 | bytes 1700000 | tf_op jit(solution)/shard_map/pallas_call | solution.py:32
  (6 shorter events, 0.0 us)
Async XLA Ops:
  0.0 1.1 %copy-start = (bf16[5,64,8,128]{3,2,1,0:T(8,128)(2,1)S(1)}, bf16[5,64,8,128]{3,2,1,0:T(8,128)(2,1)}, u32[]{:S(2)}) copy-start(bf16[5,64,8,128]{3,2,1,0:T(8,128)(2,1)} %f_ref.5) | copy-start | bytes 1966084
  1.1 2.1 %copy-start.3 = (bf16[24,576]{1,0:T(8,128)(2,1)S(1)}, bf16[24,576]{1,0:T(8,128)(2,1)}, u32[]{:S(2)}) copy-start(bf16[24,576]{1,0:T(8,128)(2,1)} %wq_ref.1) | copy-start | bytes 82948
  1.1 2.1 %copy-start.4 = (bf16[24,576]{1,0:T(8,128)(2,1)S(1)}, bf16[24,576]{1,0:T(8,128)(2,1)}, u32[]{:S(2)}) copy-start(bf16[24,576]{1,0:T(8,128)(2,1)} %wk_ref.1) | copy-start | bytes 82948
  1.1 2.1 %copy-start.5 = (bf16[24,576]{1,0:T(8,128)(2,1)S(1)}, bf16[24,576]{1,0:T(8,128)(2,1)}, u32[]{:S(2)}) copy-start(bf16[24,576]{1,0:T(8,128)(2,1)} %wv_ref.1) | copy-start | bytes 82948
  1.3 6.6 %collective-permute-start = (bf16[5,128,128]{2,1,0:T(8,128)(2,1)S(1)}, bf16[5,128,128]{2,1,0:T(8,128)(2,1)S(1)}, u32[]{:S(2)}, u32[]{:S(2)}) collective-permute-start(bf16[5,128,128]{2,1,0:T(8,128)(2,1)S(1)} %get-tuple-element.16.nb_ref), channel_id=1, source_target_pairs={{0,31},{1,2},{2,1},{3,4},{4,3},{5,6},{6,5},{7,8},{8,7},{9,10},{10,... | collective-permute-start | bytes 491528 | tf_op jit(solution)/shard_map/ppermute | solution.py:244
  83.6 15.8 %copy-start.1 = (bf16[5,64,8,128]{3,2,1,0:T(8,128)(2,1)S(1)}, bf16[5,64,8,128]{3,2,1,0:T(8,128)(2,1)}, u32[]{:S(2)}) copy-start(bf16[5,64,8,128]{3,2,1,0:T(8,128)(2,1)} %f_ref.5) | copy-start | bytes 1966084
  84.0 15.4 %copy-start.2 = (bf16[64,216]{1,0:T(8,128)(2,1)S(1)}, bf16[64,216]{1,0:T(8,128)(2,1)}, u32[]{:S(2)}) copy-start(bf16[64,216]{1,0:T(8,128)(2,1)} %w_ref.1) | copy-start | bytes 82948

commit v8 on v7

--- a/solution.py
+++ b/solution.py
@@ -14,11 +14,11 @@
 MEM, LON = 16, 32
 OWN = 5
 TOTAL = MEM * OWN
-HEAD = 16
 CUT = LAT - TOTAL
 COLS = 8
 EXT = COLS + 2
 ROWS = 16
+USED = EXT * CQ // MEM
 F32, BF16 = jnp.float32, jnp.bfloat16
 VMEM = pl.BlockSpec(memory_space=pltpu.VMEM)
 
@@ -78,18 +78,16 @@
     return pairs
 
 
-def put_pair(qk_ref, v_ref, vs, m, p, outs):
+def put_pair(qk_ref, vs, m, p, outs):
     for s in range(2):
         col = 2 * p + s
         vs[s * CQ : (s + 1) * CQ] = outs[s][2 * CQ :]
         if 1 <= col <= COLS:
             for h in range(2):
                 qk_ref[2 * (col - 1) + h, m] = outs[s][h * CQ : (h + 1) * CQ].astype(BF16)
-    for n in range(6):
-        v_ref[3 * p + n // 2, n % 2, m] = vs[n * 8 : (n + 1) * 8].astype(BF16)
-
-
-def inner_kernel(f_ref, wq_ref, wk_ref, wv_ref, qk_ref, v_ref, wp_ref, ws, xf, xt, vs):
+
+
+def inner_kernel(f_ref, wq_ref, wk_ref, wv_ref, qk_ref, v_ref, e_ref, wp_ref, ws, xf, xt, vs):
     ws[0:HALF] = wq_ref[...].astype(F32)[:HALF]
     ws[HALF : 2 * HALF] = wk_ref[...].astype(F32)[:HALF]
     ws[2 * HALF : 3 * HALF] = wq_ref[...].astype(F32)[HALF:]
@@ -111,11 +109,17 @@
         two = units[n : n + 2]
         xs = [xt[m, 2 * (p - 1) * CH : 2 * (p + 1) * CH] for m, p in two]
         for (m, p), outs in zip(two, conv_pairs(wp_ref[...], xs)):
-            put_pair(qk_ref, v_ref, vs, m, p, outs)
+            put_pair(qk_ref, vs.at[m, pl.ds((p - 1) * 2 * CQ, 2 * CQ)], m, p, outs)
+    for m in range(OWN):
+        for j in range(4, 12):
+            row = j * USED - 2 * CQ
+            v_ref[j, m] = vs[m, row : row + ROWS].astype(BF16)
+        e_ref[m, 0:ROWS] = vs[m, 0:ROWS]
+        e_ref[m, ROWS:] = vs[m, 6 * CQ - ROWS :]
 
 
 def outer_kernel(
-    iq_ref, iv_ref, wp_ref, sib_ref, nb_ref, gs_ref, gn_ref, qk_ref, v_ref, xl, xr, vs
+    iq_ref, iv_ref, e_ref, wp_ref, sib_ref, nb_ref, gs_ref, gn_ref, qk_ref, v_ref, xl, xr, vl, vr
 ):
     core = lax.axis_index("core")
     near = 2 * CH
@@ -136,13 +140,18 @@
 
     for m in range(OWN):
         left, right = conv_pairs(wp_ref[...], [xl[m], xr[m]])
-        put_pair(qk_ref, v_ref, vs, m, 0, left)
-        put_pair(qk_ref, v_ref, vs, m, EXT // 2 - 1, right)
-        for h in range(2):
-            v_ref[MEM - 1, h, m] = jnp.zeros((8, LAT), BF16)
-
-
-def gram_kernel(x_ref, v_ref, o_ref, xs, gs, ps):
+        put_pair(qk_ref, vl.at[pl.ds(0, 2 * CQ)], m, 0, left)
+        put_pair(qk_ref, vr.at[pl.ds(ROWS, 2 * CQ)], m, EXT // 2 - 1, right)
+        vl[2 * CQ :] = e_ref[m, 0:ROWS]
+        vr[0:ROWS] = e_ref[m, ROWS:]
+        vr[ROWS + 2 * CQ :] = jnp.zeros((8, LAT), F32)
+        for j in range(4):
+            v_ref[j, m] = vl[j * USED : j * USED + ROWS].astype(BF16)
+            row = (12 + j) * USED - (8 * CQ - ROWS)
+            v_ref[12 + j, m] = vr[row : row + ROWS].astype(BF16)
+
+
+def gram_kernel(x_ref, g_ref, xs, gs):
     xs[...] = x_ref[...].astype(F32).reshape(TOTAL * CQ, LAT)
     pad = jnp.zeros((LAT - TOTAL, LAT), BF16)
     q, k = [], []
@@ -163,27 +172,11 @@
     for s in range(MEM):
         row = s * OWN
         free = [gs[1 + h, row + 4 : row + 5, :] for h in range(2)]
-        ps[0, 4 * s : 4 * s + 4] = gs[0, row : row + 4, :] + jnp.concatenate(free + [rest], axis=0)
-    for part in range(2):
-        whole = ps[part]
-        high = whole.astype(BF16).astype(F32)
-        ps[part] = high
-        ps[part + 1] = whole - high
-    for s in range(MEM):
-        for part in range(3):
-            ps[3, 4 * part : 4 * part + 4] = ps[part, 4 * s : 4 * s + 4]
-        ps[3, 12:HEAD] = jnp.zeros((HEAD - 12, LAT), F32)
-        o_ref[s, 0:HEAD] = ps[3, 0:HEAD].astype(BF16)
-    o_ref[:, HEAD:] = v_ref[:, 0].astype(F32).reshape(MEM, OWN * 8, LAT).astype(BF16)
-
-
-def total_kernel(x_ref, o_ref):
-    parts = jnp.sum(x_ref[:, 0:HEAD].astype(F32), axis=0)
-    o_ref[...] = parts[0:4] + parts[4:8] + parts[8:12]
+        g_ref[s] = gs[0, row : row + 4, :] + jnp.concatenate(free + [rest], axis=0)
 
 
 def spread_kernel(x_ref, o_ref):
-    o_ref[...] = jnp.broadcast_to((x_ref[0] + x_ref[1])[None], o_ref.shape)
+    o_ref[...] = jnp.broadcast_to(jnp.sum(x_ref[...], axis=0)[None], o_ref.shape)
 
 
 def softmax_kernel(scale, x_ref, v_ref, o_ref, gs):
@@ -195,22 +188,21 @@
     gs[4:5] = jnp.where(lane[0:1] < CUT, head[0:1], tail[1:2])
     s = jnp.where(lane < TOTAL, gs[...] * scale, -jnp.inf)
     e = jnp.exp(s - jnp.max(s, axis=1, keepdims=True))
-    w = (e / jnp.sum(e, axis=1, keepdims=True)).astype(BF16)
-    o_ref[:, 0:HEAD] = jnp.broadcast_to(w[None], (MEM, HEAD, LAT))
-    o_ref[:, HEAD:] = v_ref[:, 1].astype(F32).reshape(MEM, OWN * 8, LAT).astype(BF16)
-
-
-def mix_kernel(a_ref, b_ref, o_ref, ws, vs, ms):
-    for s in range(MEM):
-        ws[s * OWN : (s + 1) * OWN, :] = b_ref[s, 0:HEAD].astype(F32)[0:OWN]
-    w = ws[...].astype(BF16)[:, :TOTAL]
-    v = []
-    for h, ref in enumerate((a_ref, b_ref)):
-        vs[h] = ref[:, HEAD:].astype(F32).reshape(TOTAL * 8, LAT)
-        v += [vs[h, pl.ds(r, TOTAL, stride=8), :].astype(BF16) for r in range(8)]
-    mixed = jnp.dot(w, jnp.concatenate(v, axis=1), preferred_element_type=F32)
-    for r in range(ROWS):
+    w = e / jnp.sum(e, axis=1, keepdims=True)
+    row = lax.broadcasted_iota(jnp.int32, (MEM, ROWS, LAT), 1)
+    for m in range(OWN):
+        block = v_ref[:, m].astype(F32)
+        o_ref[:, m] = jnp.where(row == USED, w[m : m + 1][None], block).astype(BF16)
+
+
+def mix_kernel(x_ref, o_ref, vs, ms):
+    vs[...] = x_ref[...].astype(F32).reshape(TOTAL * ROWS, LAT)
+    w = vs[pl.ds(USED, TOTAL, stride=ROWS), :].astype(BF16)[:, :TOTAL]
+    v = jnp.concatenate([vs[pl.ds(r, TOTAL, stride=ROWS), :].astype(BF16) for r in range(USED)], axis=1)
+    mixed = jnp.dot(w, v, preferred_element_type=F32)
+    for r in range(USED):
         ms[pl.ds(r, TOTAL, stride=ROWS), :] = mixed[:, r * LAT : (r + 1) * LAT]
+    ms[pl.ds(USED, TOTAL, stride=ROWS), :] = jnp.zeros((TOTAL, LAT), F32)
     o_ref[...] = ms[...].astype(BF16).reshape(o_ref.shape)
 
 
@@ -218,7 +210,7 @@
     copies = [pltpu.make_async_copy(ob.at[m], o_ref.at[m], sem.at[m]) for m in range(OWN)]
     for m in range(OWN):
         for j in range(MEM):
-            mc[j * ROWS : (j + 1) * ROWS] = x_ref[j, m].astype(F32)
+            mc[j * USED : j * USED + ROWS] = x_ref[j, m].astype(F32)
         mb[...], ma[...] = lat_shifts(mc[...])
         for i in range(0, COLS, 2):
             patches = []
@@ -244,16 +236,17 @@
     got_nb = lax.ppermute(nb, ("yhi", "x", "core"), swaps)
     got_sib = lax.all_gather(sib, "core", axis=0, tiled=False)
     qk_shape = jax.ShapeDtypeStruct((MEM, OWN, CQ, LAT), BF16)
-    v_shape = jax.ShapeDtypeStruct((MEM, 2, OWN, 8, LAT), BF16)
+    v_shape = jax.ShapeDtypeStruct((MEM, OWN, ROWS, LAT), BF16)
+    ends = jax.ShapeDtypeStruct((OWN, 2 * ROWS, LAT), F32)
     pair = jax.ShapeDtypeStruct((18 * CQ, 4 * CH), BF16)
-    qk, v, w_pair = call(
+    qk, v, ends, w_pair = call(
         inner_kernel,
-        (qk_shape, v_shape, pair),
+        (qk_shape, v_shape, ends, pair),
         [
             pltpu.VMEM((3 * CQ, 9 * CH), F32),
             plane,
             pltpu.VMEM((OWN, CH * COLS, LAT), BF16),
-            pltpu.VMEM((2 * CQ, LAT), F32),
+            pltpu.VMEM((OWN, 6 * CQ, LAT), F32),
         ],
         450_000_000,
         2_000_000,
@@ -265,11 +258,13 @@
     qk, v = call(
         outer_kernel,
         (qk_shape, v_shape),
-        [pltpu.VMEM((OWN, 4 * CH, LAT), BF16)] * 2 + [pltpu.VMEM((2 * CQ, LAT), F32)],
+        [pltpu.VMEM((OWN, 4 * CH, LAT), BF16)] * 2
+        + [pltpu.VMEM((2 * CQ + ROWS, LAT), F32), pltpu.VMEM((2 * CQ + ROWS + 8, LAT), F32)],
         300_000_000,
         1_500_000,
         qk,
         v,
+        ends,
         w_pair,
         sib,
         nb,
@@ -277,52 +272,38 @@
         got_nb,
         alias={0: 0, 1: 1},
     )
-    mem, lon = ("z", "ylo"), ("yhi", "x")
+    mem, lon = ("z", "ylo"), ("yhi", "x", "core")
     qk = lax.all_to_all(qk, mem, 0, 0, tiled=True)
-
-    packed = jax.ShapeDtypeStruct((MEM, HEAD + OWN * 8, LAT), BF16)
-    first = call(
+    gram = call(
         gram_kernel,
-        packed,
-        [
-            pltpu.VMEM((TOTAL * CQ, LAT), F32),
-            pltpu.VMEM((3, TOTAL, LAT), F32),
-            pltpu.VMEM((4, 4 * MEM, LAT), F32),
-        ],
+        jax.ShapeDtypeStruct((MEM, 4, LAT), F32),
+        [pltpu.VMEM((TOTAL * CQ, LAT), F32), pltpu.VMEM((3, TOTAL, LAT), F32)],
         20_000_000,
-        800_000,
+        600_000,
         qk,
-        v,
-    )
-    first = lax.all_to_all(first, mem, 0, 0, tiled=True)
-    gram = call(total_kernel, jax.ShapeDtypeStruct((4, LAT), F32), [], 40_000, 200_000, first)
-    gram = lax.all_gather(gram, "core", axis=0, tiled=False)
-    copies = jax.ShapeDtypeStruct((LON // 2, 4, LAT), F32)
-    gram = call(spread_kernel, copies, [], 10_000, 40_000, gram)
+    )
+    gram = lax.all_to_all(gram, mem, 0, 0, tiled=True)
+    gram = call(spread_kernel, jax.ShapeDtypeStruct((LON, 4, LAT), F32), [], 10_000, 100_000, gram)
     gram = lax.all_to_all(gram, lon, 0, 0, tiled=True)
     scale = 1.0 / math.sqrt(CQ * LAT * COLS * LON)
-    second = call(
+    v = call(
         functools.partial(softmax_kernel, scale),
-        packed,
-        [pltpu.VMEM((HEAD, LAT), F32)],
+        v_shape,
+        [pltpu.VMEM((8, LAT), F32)],
         40_000,
-        400_000,
+        700_000,
         gram,
         v,
-    )
-    second = lax.all_to_all(second, mem, 0, 0, tiled=True)
+        alias={1: 0},
+    )
+    v = lax.all_to_all(v, mem, 0, 0, tiled=True)
     mixed = call(
         mix_kernel,
-        jax.ShapeDtypeStruct((MEM, OWN, ROWS, LAT), BF16),
-        [
-            pltpu.VMEM((TOTAL, LAT), F32),
-            pltpu.VMEM((2, TOTAL * 8, LAT), F32),
-            pltpu.VMEM((TOTAL * ROWS, LAT), F32),
-        ],
+        v_shape,
+        [pltpu.VMEM((TOTAL * ROWS, LAT), F32)] * 2,
         30_000_000,
         700_000,
-        first,
-        second,
+        v,
     )
     mixed = lax.all_to_all(mixed, ("z", "ylo"), 0, 0, tiled=True)
     return call(

time: 101 us -> 102 us (level)
  the two profiles are of different devices: /device:TPU:4 before, /device:TPU:8 now
where the time goes in v8:
time: 102 us; the launch traced here: 101 us
  blocking collectives  87.8 us (86%)
  starting transfers between devices  6.9 us (7%)
  Pallas kernels  4.49 us (4%)
  local copies, waits for them, and re-layouts  1.11 us (1%)
    all_to_all x1, blocking collectives, shards(): qk = lax.all_to_all(qk, mem, 0, 0, tiled=True)  26.5 us
    all_to_all x1, blocking collectives, shards(): v = lax.all_to_all(v, mem, 0, 0, tiled=True)  16.8 us
    all_to_all x1, blocking collectives, shards(): gram = lax.all_to_all(gram, lon, 0, 0, tiled=True)  16.2 us
    all_to_all x1, blocking collectives, shards(): mixed = lax.all_to_all(mixed, ('z', 'ylo'), 0, 0, tiled=True)  15 us
    all_to_all x1, blocking collectives, shards(): gram = lax.all_to_all(gram, mem, 0, 0, tiled=True)  11.2 us
    ppermute x1, starting transfers between devices, shards(): got_nb = lax.ppermute(nb, ('yhi', 'x', 'core'), swaps)  6.9 us
    pallas_call x8, Pallas kernels, call(): pl.pallas_call(body, out_shape=outs, in_specs=[VMEM] * len(args), out_spe...  4.49 us
    all_gather x1, blocking collectives, shards(): got_sib = lax.all_gather(sib, 'core', axis=0, tiled=False)  2.04 us
  transfers between devices with their start and end apart: 1, of which 1 were waited for; matrix products, arithmetic and copies ran while one was open for 0% of the time, Pallas kernels for 1%

profile of v8, /device:TPU:8, one launch (start us, length us, event | category | flops | bytes accessed | tf_op | source)
XLA Modules:
  0.0 101.3 jit_solution(1582038163314935457)
XLA Ops:
  0.0 0.0 copy-start
  0.0 1.1 %copy-done = bf16[5,64,8,128]{3,2,1,0:T(8,128)(2,1)S(1)} copy-done((bf16[5,64,8,128]{3,2,1,0:T(8,128)(2,1)S(1)}, bf16[5,64,8,128]{3,2,1,0:T(8,128)(2,1)}, u32[]{:S(2)}) %copy-start) | copy-done | bytes 655384
  1.1 0.0 copy-start.3
  1.1 0.2 shard_map.56
  1.3 6.9 %collective-permute-start = (bf16[5,128,128]{2,1,0:T(8,128)(2,1)S(1)}, bf16[5,128,128]{2,1,0:T(8,128)(2,1)S(1)}, u32[]{:S(2)}, u32[]{:S(2)}) collective-permute-start(bf16[5,128,128]{2,1,0:T(8,128)(2,1)S(1)} %get-tuple-element.18.nb_ref), channel_id=1, source_target_pairs={{0,31},{1,2},{2,1},{3,4},{4,3},{5,6},{6,5},{7,8},{8,7},{9,10},{10,... | collective-permute-start | bytes 491528 | tf_op jit(solution)/shard_map/ppermute | solution.py:236
  8.2 0.0 copy-done.3
  8.2 0.0 copy-done.4
  8.2 0.0 copy-done.5
  8.2 1.1 %shard_map.55 = (bf16[16,5,24,128]{3,2,1,0:T(8,128)(2,1)S(1)}, bf16[16,5,16,128]{3,2,1,0:T(8,128)(2,1)S(1)}, f32[5,32,128]{2,1,0:T(8,128)S(1)}, bf16[432,256]{1,0:T(8,128)(2,1)S(1)}) custom-call(bf16[5,64,8,128]{3,2,1,0:T(8,128)(2,1)S(1)} %copy-done, bf16[24,576]{1,0:T(8,128)(2,1)S(1)} %copy-done.3, bf16[24,576]{1,0:T(8,128)(2,1)S(1)} %copy-done.4, ...), custom_call_target="tpu_custom_call" | custom-call | flops 450000000 | bytes 2000000 | tf_op jit(solution)/shard_map/pallas_call | solution.py:32
  9.3 2.0 %all-gather = bf16[10,128,128]{2,1,0:T(8,128)(2,1)S(1)} all-gather(bf16[5,128,128]{2,1,0:T(8,128)(2,1)S(1)} %get-tuple-element.17.sib_ref), channel_id=2, replica_groups=mesh['z'=8,'ylo'=2,'yhi'=4,'x'=4,'core'=2] {'core'}, dimensions={0}, use_global_device_ids=true | all-gather | bytes 491520 | tf_op jit(solution)/shard_map/all_gather | solution.py:237
  11.3 0.9 collective-permute-done.gn_ref
  12.2 0.6 shard_map.57
  12.9 26.5 %all_to_all.25.x_ref = bf16[16,5,24,128]{3,2,1,0:T(8,128)(2,1)S(1)} all-to-all(bf16[16,5,24,128]{3,2,1,0:T(8,128)(2,1)S(1)} %get-tuple-element.19), channel_id=1, replica_groups=mesh['z'=8,'ylo'=2,'yhi'=4,'x'=4,'core'=2] {'z','ylo'}, dimensions={0} | all-to-all | bytes 983040 | tf_op jit(solution)/shard_map/all_to_all | solution.py:276
  39.4 0.4 shard_map.58
  39.8 11.2 %all_to_all.26.x_ref = f32[16,4,128]{2,1,0:T(4,128)S(1)} all-to-all(f32[16,4,128]{2,1,0:T(4,128)S(1)} %shard_map.58), channel_id=1, replica_groups=mesh['z'=8,'ylo'=2,'yhi'=4,'x'=4,'core'=2] {'z','ylo'}, dimensions={0} | all-to-all | bytes 65536 | tf_op jit(solution)/shard_map/all_to_all | solution.py:285
  51.0 16.2 %all_to_all.27.x_ref = f32[32,4,128]{2,1,0:T(4,128)S(1)} all-to-all(f32[32,4,128]{2,1,0:T(4,128)S(1)} %shard_map.59), channel_id=1, replica_groups=mesh['z'=8,'ylo'=2,'yhi'=4,'x'=4,'core'=2] {'yhi','x','core'}, dimensions={0} | all-to-all | bytes 131072 | tf_op jit(solution)/shard_map/all_to_all | solution.py:287
  67.2 0.3 shard_map.60
  67.5 16.8 %all_to_all.28.x_ref = bf16[16,5,16,128]{3,2,1,0:T(8,128)(2,1)S(1)} all-to-all(bf16[16,5,16,128]{3,2,1,0:T(8,128)(2,1)S(1)} %shard_map.60), channel_id=1, replica_groups=mesh['z'=8,'ylo'=2,'yhi'=4,'x'=4,'core'=2] {'z','ylo'}, dimensions={0} | all-to-all | bytes 655360 | tf_op jit(solution)/shard_map/all_to_all | solution.py:299
  84.3 0.5 shard_map.61
  84.8 0.0 copy-start.2
  84.8 15.0 %all_to_all.29.x_ref = bf16[16,5,16,128]{3,2,1,0:T(8,128)(2,1)S(1)} all-to-all(bf16[16,5,16,128]{3,2,1,0:T(8,128)(2,1)S(1)} %shard_map.61), channel_id=1, replica_groups=mesh['z'=8,'ylo'=2,'yhi'=4,'x'=4,'core'=2] {'z','ylo'}, dimensions={0} | all-to-all | bytes 655360 | tf_op jit(solution)/shard_map/all_to_all | solution.py:308
  99.9 0.0 copy-done.1
  99.9 0.0 copy-done.2
  99.9 1.4 %shard_map.62 = bf16[5,64,8,128]{3,2,1,0:T(8,128)(2,1)} custom-call(bf16[16,5,16,128]{3,2,1,0:T(8,128)(2,1)S(1)} %all_to_all.29.x_ref, bf16[5,64,8,128]{3,2,1,0:T(8,128)(2,1)S(1)} %copy-done.1, bf16[64,216]{1,0:T(8,128)(2,1)S(1)} %copy-done.2), custom_call_target="tpu_custom_call" | custom-call | flops 150000000 | bytes 1700000 | tf_op jit(solution)/shard_map/pallas_call | solution.py:32
  (4 shorter events, 0.0 us)
Async XLA Ops:
  0.0 1.1 %copy-start = (bf16[5,64,8,128]{3,2,1,0:T(8,128)(2,1)S(1)}, bf16[5,64,8,128]{3,2,1,0:T(8,128)(2,1)}, u32[]{:S(2)}) copy-start(bf16[5,64,8,128]{3,2,1,0:T(8,128)(2,1)} %f_ref.5) | copy-start | bytes 1966084
  1.1 7.1 %copy-start.3 = (bf16[24,576]{1,0:T(8,128)(2,1)S(1)}, bf16[24,576]{1,0:T(8,128)(2,1)}, u32[]{:S(2)}) copy-start(bf16[24,576]{1,0:T(8,128)(2,1)} %wq_ref.1) | copy-start | bytes 82948
  1.1 7.1 %copy-start.4 = (bf16[24,576]{1,0:T(8,128)(2,1)S(1)}, bf16[24,576]{1,0:T(8,128)(2,1)}, u32[]{:S(2)}) copy-start(bf16[24,576]{1,0:T(8,128)(2,1)} %wk_ref.1) | copy-start | bytes 82948
  1.1 7.1 %copy-start.5 = (bf16[24,576]{1,0:T(8,128)(2,1)S(1)}, bf16[24,576]{1,0:T(8,128)(2,1)}, u32[]{:S(2)}) copy-start(bf16[24,576]{1,0:T(8,128)(2,1)} %wv_ref.1) | copy-start | bytes 82948
  1.3 11.0 %collective-permute-start = (bf16[5,128,128]{2,1,0:T(8,128)(2,1)S(1)}, bf16[5,128,128]{2,1,0:T(8,128)(2,1)S(1)}, u32[]{:S(2)}, u32[]{:S(2)}) collective-permute-start(bf16[5,128,128]{2,1,0:T(8,128)(2,1)S(1)} %get-tuple-element.18.nb_ref), channel_id=1, source_target_pairs={{0,31},{1,2},{2,1},{3,4},{4,3},{5,6},{6,5},{7,8},{8,7},{9,10},{10,... | collective-permute-start | bytes 491528 | tf_op jit(solution)/shard_map/ppermute | solution.py:236
  84.3 15.5 %copy-start.1 = (bf16[5,64,8,128]{3,2,1,0:T(8,128)(2,1)S(1)}, bf16[5,64,8,128]{3,2,1,0:T(8,128)(2,1)}, u32[]{:S(2)}) copy-start(bf16[5,64,8,128]{3,2,1,0:T(8,128)(2,1)} %f_ref.5) | copy-start | bytes 1966084
  84.8 15.1 %copy-start.2 = (bf16[64,216]{1,0:T(8,128)(2,1)S(1)}, bf16[64,216]{1,0:T(8,128)(2,1)}, u32[]{:S(2)}) copy-start(bf16[64,216]{1,0:T(8,128)(2,1)} %w_ref.1) | copy-start | bytes 82948

commit v9 on v8

--- a/solution.py
+++ b/solution.py
@@ -19,6 +19,7 @@
 EXT = COLS + 2
 ROWS = 16
 USED = EXT * CQ // MEM
+HEAD = 16
 F32, BF16 = jnp.float32, jnp.bfloat16
 VMEM = pl.BlockSpec(memory_space=pltpu.VMEM)
 
@@ -78,6 +79,11 @@
     return pairs
 
 
+def put_block(v0_ref, v1_ref, j, m, block):
+    v0_ref[j, HEAD + m * 8 : HEAD + m * 8 + 8] = block[:8].astype(BF16)
+    v1_ref[j, m] = block[8:].astype(BF16)
+
+
 def put_pair(qk_ref, vs, m, p, outs):
     for s in range(2):
         col = 2 * p + s
@@ -87,7 +93,9 @@
                 qk_ref[2 * (col - 1) + h, m] = outs[s][h * CQ : (h + 1) * CQ].astype(BF16)
 
 
-def inner_kernel(f_ref, wq_ref, wk_ref, wv_ref, qk_ref, v_ref, e_ref, wp_ref, ws, xf, xt, vs):
+def inner_kernel(
+    f_ref, wq_ref, wk_ref, wv_ref, wo_ref, qk_ref, v0_ref, v1_ref, e_ref, wp_ref, wf_ref, ws, xf, xt, vs
+):
     ws[0:HALF] = wq_ref[...].astype(F32)[:HALF]
     ws[HALF : 2 * HALF] = wk_ref[...].astype(F32)[:HALF]
     ws[2 * HALF : 3 * HALF] = wq_ref[...].astype(F32)[HALF:]
@@ -100,6 +108,14 @@
             row = (3 * s + b) * 3 * CQ
             full = [zero] + taps if s else taps + [zero]
             wp_ref[row : row + 3 * CQ] = jnp.concatenate(full, axis=1).astype(BF16)
+    wo = wo_ref[...].astype(F32)
+    zero = jnp.zeros((CH, CQ), F32)
+    for s in range(2):
+        full = []
+        for b in range(3):
+            taps = [wo[:, (3 * a + b) * CQ : (3 * a + b + 1) * CQ] for a in range(3)]
+            full += [zero] + taps if s else taps + [zero]
+        wf_ref[s * CH : (s + 1) * CH] = jnp.concatenate(full, axis=1).astype(BF16)
     for m in range(OWN):
         xf[...] = f_ref[m].astype(F32).reshape(CH * COLS, LAT)
         for i in range(COLS):
@@ -113,13 +129,14 @@
     for m in range(OWN):
         for j in range(4, 12):
             row = j * USED - 2 * CQ
-            v_ref[j, m] = vs[m, row : row + ROWS].astype(BF16)
+            put_block(v0_ref, v1_ref, j, m, vs[m, row : row + ROWS])
         e_ref[m, 0:ROWS] = vs[m, 0:ROWS]
         e_ref[m, ROWS:] = vs[m, 6 * CQ - ROWS :]
 
 
 def outer_kernel(
-    iq_ref, iv_ref, e_ref, wp_ref, sib_ref, nb_ref, gs_ref, gn_ref, qk_ref, v_ref, xl, xr, vl, vr
+    iq_ref, i0_ref, i1_ref, e_ref, wp_ref, sib_ref, nb_ref, gs_ref, gn_ref,
+    qk_ref, v0_ref, v1_ref, xl, xr, vl, vr
 ):
     core = lax.axis_index("core")
     near = 2 * CH
@@ -146,12 +163,12 @@
         vr[0:ROWS] = e_ref[m, ROWS:]
         vr[ROWS + 2 * CQ :] = jnp.zeros((8, LAT), F32)
         for j in range(4):
-            v_ref[j, m] = vl[j * USED : j * USED + ROWS].astype(BF16)
+            put_block(v0_ref, v1_ref, j, m, vl[j * USED : j * USED + ROWS])
             row = (12 + j) * USED - (8 * CQ - ROWS)
-            v_ref[12 + j, m] = vr[row : row + ROWS].astype(BF16)
-
-
-def gram_kernel(x_ref, g_ref, xs, gs):
+            put_block(v0_ref, v1_ref, 12 + j, m, vr[row : row + ROWS])
+
+
+def gram_kernel(x_ref, v0_ref, o_ref, xs, gs, ps):
     xs[...] = x_ref[...].astype(F32).reshape(TOTAL * CQ, LAT)
     pad = jnp.zeros((LAT - TOTAL, LAT), BF16)
     q, k = [], []
@@ -172,14 +189,29 @@
     for s in range(MEM):
         row = s * OWN
         free = [gs[1 + h, row + 4 : row + 5, :] for h in range(2)]
-        g_ref[s] = gs[0, row : row + 4, :] + jnp.concatenate(free + [rest], axis=0)
+        ps[0, 4 * s : 4 * s + 4] = gs[0, row : row + 4, :] + jnp.concatenate(free + [rest], axis=0)
+    for part in range(2):
+        whole = ps[part]
+        high = whole.astype(BF16).astype(F32)
+        ps[part] = high
+        ps[part + 1] = whole - high
+    for s in range(MEM):
+        for part in range(3):
+            ps[3, 4 * part : 4 * part + 4] = ps[part, 4 * s : 4 * s + 4]
+        ps[3, 12:HEAD] = jnp.zeros((HEAD - 12, LAT), F32)
+        o_ref[s, 0:HEAD] = ps[3, 0:HEAD].astype(BF16)
+
+
+def total_kernel(x_ref, o_ref):
+    parts = jnp.sum(x_ref[:, 0:HEAD].astype(F32), axis=0)
+    o_ref[...] = parts[0:4] + parts[4:8] + parts[8:12]
 
 
 def spread_kernel(x_ref, o_ref):
-    o_ref[...] = jnp.broadcast_to(jnp.sum(x_ref[...], axis=0)[None], o_ref.shape)
-
-
-def softmax_kernel(scale, x_ref, v_ref, o_ref, gs):
+    o_ref[...] = jnp.broadcast_to((x_ref[0] + x_ref[1])[None], o_ref.shape)
+
+
+def softmax_kernel(scale, x_ref, v1_ref, o_ref, gs):
     gs[...] = jnp.zeros(gs.shape, F32)
     gs[0:4] = jnp.sum(x_ref[...], axis=0)
     gram = gs[...]
@@ -189,16 +221,18 @@
     s = jnp.where(lane < TOTAL, gs[...] * scale, -jnp.inf)
     e = jnp.exp(s - jnp.max(s, axis=1, keepdims=True))
     w = e / jnp.sum(e, axis=1, keepdims=True)
-    row = lax.broadcasted_iota(jnp.int32, (MEM, ROWS, LAT), 1)
-    for m in range(OWN):
-        block = v_ref[:, m].astype(F32)
-        o_ref[:, m] = jnp.where(row == USED, w[m : m + 1][None], block).astype(BF16)
-
-
-def mix_kernel(x_ref, o_ref, vs, ms):
-    vs[...] = x_ref[...].astype(F32).reshape(TOTAL * ROWS, LAT)
-    w = vs[pl.ds(USED, TOTAL, stride=ROWS), :].astype(BF16)[:, :TOTAL]
-    v = jnp.concatenate([vs[pl.ds(r, TOTAL, stride=ROWS), :].astype(BF16) for r in range(USED)], axis=1)
+    row = lax.broadcasted_iota(jnp.int32, (MEM, 8, LAT), 1)
+    for m in range(OWN):
+        block = v1_ref[:, m].astype(F32)
+        o_ref[:, m] = jnp.where(row == USED - 8, w[m : m + 1][None], block).astype(BF16)
+
+
+def mix_kernel(v0_ref, v1_ref, o_ref, vs, ms):
+    vs[0] = v0_ref[:, HEAD:].astype(F32).reshape(TOTAL * 8, LAT)
+    vs[1] = v1_ref[...].astype(F32).reshape(TOTAL * 8, LAT)
+    rows = [vs[r // 8, pl.ds(r % 8, TOTAL, stride=8), :].astype(BF16) for r in range(ROWS)]
+    w = rows[USED][:, :TOTAL]
+    v = jnp.concatenate(rows[:USED], axis=1)
     mixed = jnp.dot(w, v, preferred_element_type=F32)
     for r in range(USED):
         ms[pl.ds(r, TOTAL, stride=ROWS), :] = mixed[:, r * LAT : (r + 1) * LAT]
@@ -206,22 +240,24 @@
     o_ref[...] = ms[...].astype(BF16).reshape(o_ref.shape)
 
 
-def finish_kernel(x_ref, f_ref, w_ref, o_ref, mc, mb, ma, br, ob, sem):
+def finish_kernel(x_ref, f_ref, w_ref, o_ref, mc, sh, br, ob, sem):
     copies = [pltpu.make_async_copy(ob.at[m], o_ref.at[m], sem.at[m]) for m in range(OWN)]
     for m in range(OWN):
         for j in range(MEM):
             mc[j * USED : j * USED + ROWS] = x_ref[j, m].astype(F32)
-        mb[...], ma[...] = lat_shifts(mc[...])
-        for i in range(0, COLS, 2):
-            patches = []
-            for col in (i, i + 1):
-                parts = [
-                    t[(col + a) * CQ : (col + a + 1) * CQ, :] for a in range(3) for t in (mb, mc, ma)
-                ]
-                patches.append(jnp.concatenate(parts, axis=0).astype(BF16))
+        whole = mc[0 : EXT * CQ]
+        before, after = lat_shifts(whole)
+        for b, x in enumerate((before, whole, after)):
+            sh[b] = x.astype(BF16)
+        for i in range(0, COLS, 4):
+            patches = [
+                jnp.concatenate([sh[b, p * CQ : (p + 4) * CQ] for b in range(3)], axis=0)
+                for p in (i, i + 2)
+            ]
             r = jnp.dot(w_ref[...], jnp.concatenate(patches, axis=1), preferred_element_type=F32)
-            for s in range(2):
-                br[pl.ds(i + s, CH, stride=COLS), :] = r[:, s * LAT : (s + 1) * LAT]
+            for n in range(4):
+                rows, lanes = (n % 2) * CH, (n // 2) * LAT
+                br[pl.ds(i + n, CH, stride=COLS), :] = r[rows : rows + CH, lanes : lanes + LAT]
         ob[m] = (f_ref[m].astype(F32) + br[...].reshape(CH, COLS, LAT)).astype(BF16)
         copies[m].start()
     for copy in copies:
@@ -236,12 +272,14 @@
     got_nb = lax.ppermute(nb, ("yhi", "x", "core"), swaps)
     got_sib = lax.all_gather(sib, "core", axis=0, tiled=False)
     qk_shape = jax.ShapeDtypeStruct((MEM, OWN, CQ, LAT), BF16)
-    v_shape = jax.ShapeDtypeStruct((MEM, OWN, ROWS, LAT), BF16)
+    v0_shape = jax.ShapeDtypeStruct((MEM, HEAD + OWN * 8, LAT), BF16)
+    v1_shape = jax.ShapeDtypeStruct((MEM, OWN, 8, LAT), BF16)
     ends = jax.ShapeDtypeStruct((OWN, 2 * ROWS, LAT), F32)
     pair = jax.ShapeDtypeStruct((18 * CQ, 4 * CH), BF16)
-    qk, v, ends, w_pair = call(
+    pair_out = jax.ShapeDtypeStruct((2 * CH, 12 * CQ), BF16)
+    qk, v0, v1, ends, w_pair, w_last = call(
         inner_kernel,
-        (qk_shape, v_shape, ends, pair),
+        (qk_shape, v0_shape, v1_shape, ends, pair, pair_out),
         [
             pltpu.VMEM((3 * CQ, 9 * CH), F32),
             plane,
@@ -254,68 +292,85 @@
         w_query,
         w_key,
         w_value,
-    )
-    qk, v = call(
+        w_out,
+    )
+    qk, v0, v1 = call(
         outer_kernel,
-        (qk_shape, v_shape),
+        (qk_shape, v0_shape, v1_shape),
         [pltpu.VMEM((OWN, 4 * CH, LAT), BF16)] * 2
         + [pltpu.VMEM((2 * CQ + ROWS, LAT), F32), pltpu.VMEM((2 * CQ + ROWS + 8, LAT), F32)],
         300_000_000,
         1_500_000,
         qk,
-        v,
+        v0,
+        v1,
         ends,
         w_pair,
         sib,
         nb,
         got_sib,
         got_nb,
-        alias={0: 0, 1: 1},
-    )
-    mem, lon = ("z", "ylo"), ("yhi", "x", "core")
+        alias={0: 0, 1: 1, 2: 2},
+    )
+    mem, lon = ("z", "ylo"), ("yhi", "x")
     qk = lax.all_to_all(qk, mem, 0, 0, tiled=True)
-    gram = call(
+    v0 = call(
         gram_kernel,
-        jax.ShapeDtypeStruct((MEM, 4, LAT), F32),
-        [pltpu.VMEM((TOTAL * CQ, LAT), F32), pltpu.VMEM((3, TOTAL, LAT), F32)],
+        v0_shape,
+        [
+            pltpu.VMEM((TOTAL * CQ, LAT), F32),
+            pltpu.VMEM((3, TOTAL, LAT), F32),
+            pltpu.VMEM((4, 4 * MEM, LAT), F32),
+        ],
         20_000_000,
-        600_000,
+        800_000,
         qk,
-    )
-    gram = lax.all_to_all(gram, mem, 0, 0, tiled=True)
-    gram = call(spread_kernel, jax.ShapeDtypeStruct((LON, 4, LAT), F32), [], 10_000, 100_000, gram)
+        v0,
+        alias={1: 0},
+    )
+    v0 = lax.all_to_all(v0, mem, 0, 0, tiled=True)
+    gram = call(total_kernel, jax.ShapeDtypeStruct((4, LAT), F32), [], 40_000, 200_000, v0)
+    gram = lax.all_gather(gram, "core", axis=0, tiled=False)
+    copies = jax.ShapeDtypeStruct((LON // 2, 4, LAT), F32)
+    gram = call(spread_kernel, copies, [], 10_000, 40_000, gram)
     gram = lax.all_to_all(gram, lon, 0, 0, tiled=True)
     scale = 1.0 / math.sqrt(CQ * LAT * COLS * LON)
-    v = call(
+    v1 = call(
         functools.partial(softmax_kernel, scale),
-        v_shape,
+        v1_shape,
         [pltpu.VMEM((8, LAT), F32)],
         40_000,
-        700_000,
+        400_000,
         gram,
-        v,
+        v1,
         alias={1: 0},
     )
-    v = lax.all_to_all(v, mem, 0, 0, tiled=True)
+    v1 = lax.all_to_all(v1, mem, 0, 0, tiled=True)
     mixed = call(
         mix_kernel,
-        v_shape,
-        [pltpu.VMEM((TOTAL * ROWS, LAT), F32)] * 2,
+        jax.ShapeDtypeStruct((MEM, OWN, ROWS, LAT), BF16),
+        [pltpu.VMEM((2, TOTAL * 8, LAT), F32), pltpu.VMEM((TOTAL * ROWS, LAT), F32)],
         30_000_000,
         700_000,
-        v,
+        v0,
+        v1,
     )
     mixed = lax.all_to_all(mixed, ("z", "ylo"), 0, 0, tiled=True)
     return call(
         finish_kernel,
         jax.ShapeDtypeStruct(fields.shape, BF16),
-        [pltpu.VMEM((MEM * ROWS, LAT), F32)] * 3
-        + [plane, pltpu.VMEM(fields.shape, BF16), pltpu.SemaphoreType.DMA((OWN,))],
+        [
+            pltpu.VMEM((MEM * ROWS, LAT), F32),
+            pltpu.VMEM((3, EXT * CQ, LAT), BF16),
+            plane,
+            pltpu.VMEM(fields.shape, BF16),
+            pltpu.SemaphoreType.DMA((OWN,)),
+        ],
         150_000_000,
         1_700_000,
         mixed,
         fields,
-        w_out,
+        w_last,
         far_out=True,
     )
 

time: 102 us -> 100 us (0.980)
  blocking collectives: 87.8 us -> 86.1 us
    all_gather x0 -> x1, blocking collectives: none -> 1.78 us  [shards(): gram = lax.all_gather(gram, 'core', axis=0, tiled=False)]
    all_to_all x2, blocking collectives: 28 us -> 26.2 us  [the longest x1 14.2 us: shards(): v0 = lax.all_to_all(v0, mem, 0, 0, tiled=True)]
    all_to_all x1, blocking collectives: 15 us -> 13.5 us  [shards(): mixed = lax.all_to_all(mixed, ('z', 'ylo'), 0, 0, tiled=True)]
    pallas_call x8 -> x9, Pallas kernels: 4.49 us -> 4.57 us  [call(): pl.pallas_call(body, out_shape=outs, in_specs=[VMEM] * len(args), out_spe...]
where the time goes in v9:
time: 100 us; the launch traced here: 99.6 us
  blocking collectives  86.1 us (86%)
  starting transfers between devices  6.9 us (7%)
  Pallas kernels  4.57 us (5%)
  local copies, waits for them, and re-layouts  1.11 us (1%)
    all_to_all x1, blocking collectives, shards(): qk = lax.all_to_all(qk, mem, 0, 0, tiled=True)  26.6 us
    all_to_all x1, blocking collectives, shards(): gram = lax.all_to_all(gram, lon, 0, 0, tiled=True)  16 us
    all_to_all x1, blocking collectives, shards(): v0 = lax.all_to_all(v0, mem, 0, 0, tiled=True)  14.2 us
    all_to_all x1, blocking collectives, shards(): mixed = lax.all_to_all(mixed, ('z', 'ylo'), 0, 0, tiled=True)  13.5 us
    all_to_all x1, blocking collectives, shards(): v1 = lax.all_to_all(v1, mem, 0, 0, tiled=True)  12.1 us
    ppermute x1, starting transfers between devices, shards(): got_nb = lax.ppermute(nb, ('yhi', 'x', 'core'), swaps)  6.9 us
    pallas_call x9, Pallas kernels, call(): pl.pallas_call(body, out_shape=outs, in_specs=[VMEM] * len(args), out_spe...  4.57 us
    all_gather x1, blocking collectives, shards(): got_sib = lax.all_gather(sib, 'core', axis=0, tiled=False)  2.04 us
  transfers between devices with their start and end apart: 1, of which 1 were waited for; matrix products, arithmetic and copies ran while one was open for 0% of the time, Pallas kernels for 1%

profile of v9, /device:TPU:8, one launch (start us, length us, event | category | flops | bytes accessed | tf_op | source)
XLA Modules:
  0.0 99.6 jit_solution(9075787860206385482)
XLA Ops:
  0.0 0.0 copy-start
  0.0 1.1 %copy-done = bf16[5,64,8,128]{3,2,1,0:T(8,128)(2,1)S(1)} copy-done((bf16[5,64,8,128]{3,2,1,0:T(8,128)(2,1)S(1)}, bf16[5,64,8,128]{3,2,1,0:T(8,128)(2,1)}, u32[]{:S(2)}) %copy-start) | copy-done | bytes 655384
  1.1 0.0 copy-start.2
  1.1 0.2 shard_map.56
  1.3 6.9 %collective-permute-start = (bf16[5,128,128]{2,1,0:T(8,128)(2,1)S(1)}, bf16[5,128,128]{2,1,0:T(8,128)(2,1)S(1)}, u32[]{:S(2)}, u32[]{:S(2)}) collective-permute-start(bf16[5,128,128]{2,1,0:T(8,128)(2,1)S(1)} %get-tuple-element.22.nb_ref), channel_id=1, source_target_pairs={{0,31},{1,2},{2,1},{3,4},{4,3},{5,6},{6,5},{7,8},{8,7},{9,10},{10,... | collective-permute-start | bytes 491528 | tf_op jit(solution)/shard_map/ppermute | solution.py:272
  8.2 0.0 copy-done.2
  8.2 0.0 copy-done.3
  8.2 0.0 copy-done.4
  8.2 0.0 copy-done.5
  8.2 1.1 %shard_map.55 = (bf16[16,5,24,128]{3,2,1,0:T(8,128)(2,1)S(1)}, bf16[16,56,128]{2,1,0:T(8,128)(2,1)S(1)}, bf16[16,5,8,128]{3,2,1,0:T(8,128)(2,1)S(1)}, f32[5,32,1...) custom-call(bf16[5,64,8,128]{3,2,1,0:T(8,128)(2,1)S(1)} %copy-done, ...), custom_call_target="tpu_custom_call" | custom-call | flops 450000000 | bytes 2000000 | tf_op jit(solution)/shard_map/pallas_call | solution.py:33
  9.4 2.0 %all-gather = bf16[10,128,128]{2,1,0:T(8,128)(2,1)S(1)} all-gather(bf16[5,128,128]{2,1,0:T(8,128)(2,1)S(1)} %get-tuple-element.21.sib_ref), channel_id=2, replica_groups=mesh['z'=8,'ylo'=2,'yhi'=4,'x'=4,'core'=2] {'core'}, dimensions={0}, use_global_device_ids=true | all-gather | bytes 491520 | tf_op jit(solution)/shard_map/all_gather | solution.py:273
  11.4 0.8 collective-permute-done.gn_ref
  12.2 0.6 shard_map.57
  12.9 26.6 %all_to_all.25.x_ref = bf16[16,5,24,128]{3,2,1,0:T(8,128)(2,1)S(1)} all-to-all(bf16[16,5,24,128]{3,2,1,0:T(8,128)(2,1)S(1)} %get-tuple-element.23), channel_id=1, replica_groups=mesh['z'=8,'ylo'=2,'yhi'=4,'x'=4,'core'=2] {'z','ylo'}, dimensions={0} | all-to-all | bytes 983040 | tf_op jit(solution)/shard_map/all_to_all | solution.py:316
  39.5 0.5 shard_map.58
  39.9 14.2 %all_to_all.26.x_ref.v0_ref = bf16[16,56,128]{2,1,0:T(8,128)(2,1)S(1)} all-to-all(bf16[16,56,128]{2,1,0:T(8,128)(2,1)S(1)} %shard_map.58), channel_id=1, replica_groups=mesh['z'=8,'ylo'=2,'yhi'=4,'x'=4,'core'=2] {'z','ylo'}, dimensions={0} | all-to-all | bytes 458752 | tf_op jit(solution)/shard_map/all_to_all | solution.py:331
  54.1 1.8 %all-gather.2.x_ref = f32[2,4,128]{2,1,0:T(4,128)S(1)} all-gather(f32[1,4,128]{2,1,0:T(4,128)S(1)} %bitcast.3), channel_id=3, replica_groups=mesh['z'=8,'ylo'=2,'yhi'=4,'x'=4,'core'=2] {'core'}, dimensions={0}, use_global_device_ids=true | all-gather | bytes 6144 | tf_op jit(solution)/shard_map/all_gather | solution.py:333
  55.9 16.0 %all_to_all.27.x_ref = f32[16,4,128]{2,1,0:T(4,128)S(1)} all-to-all(f32[16,4,128]{2,1,0:T(4,128)S(1)} %shard_map.60), channel_id=1, replica_groups=mesh['z'=8,'ylo'=2,'yhi'=4,'x'=4,'core'=2] {'yhi','x'}, dimensions={0} | all-to-all | bytes 65536 | tf_op jit(solution)/shard_map/all_to_all | solution.py:336
  71.9 0.3 shard_map.61
  72.2 12.1 %all_to_all.28.v1_ref = bf16[16,5,8,128]{3,2,1,0:T(8,128)(2,1)S(1)} all-to-all(bf16[16,5,8,128]{3,2,1,0:T(8,128)(2,1)S(1)} %shard_map.61), channel_id=1, replica_groups=mesh['z'=8,'ylo'=2,'yhi'=4,'x'=4,'core'=2] {'z','ylo'}, dimensions={0} | all-to-all | bytes 327680 | tf_op jit(solution)/shard_map/all_to_all | solution.py:348
  84.3 0.4 shard_map.62
  84.7 13.5 %all_to_all.29.x_ref = bf16[16,5,16,128]{3,2,1,0:T(8,128)(2,1)S(1)} all-to-all(bf16[16,5,16,128]{3,2,1,0:T(8,128)(2,1)S(1)} %shard_map.62), channel_id=1, replica_groups=mesh['z'=8,'ylo'=2,'yhi'=4,'x'=4,'core'=2] {'z','ylo'}, dimensions={0} | all-to-all | bytes 655360 | tf_op jit(solution)/shard_map/all_to_all | solution.py:358
  98.2 0.0 copy-done.1
  98.2 1.4 %shard_map.63 = bf16[5,64,8,128]{3,2,1,0:T(8,128)(2,1)} custom-call(bf16[16,5,16,128]{3,2,1,0:T(8,128)(2,1)S(1)} %all_to_all.29.x_ref, bf16[5,64,8,128]{3,2,1,0:T(8,128)(2,1)S(1)} %copy-done.1, bf16[128,288]{1,0:T(8,128)(2,1)S(1)} %get-tuple-element.26.w_ref), custom_call_target="tpu_custom_call" | custom-call | flops 150000000 | bytes 1700000 | tf_op jit(solution)/shard_map/pallas_call | solution.py:33
  (6 shorter events, 0.0 us)
Async XLA Ops:
  0.0 1.1 %copy-start = (bf16[5,64,8,128]{3,2,1,0:T(8,128)(2,1)S(1)}, bf16[5,64,8,128]{3,2,1,0:T(8,128)(2,1)}, u32[]{:S(2)}) copy-start(bf16[5,64,8,128]{3,2,1,0:T(8,128)(2,1)} %f_ref.5) | copy-start | bytes 1966084
  1.1 7.1 %copy-start.2 = (bf16[64,216]{1,0:T(8,128)(2,1)S(1)}, bf16[64,216]{1,0:T(8,128)(2,1)}, u32[]{:S(2)}) copy-start(bf16[64,216]{1,0:T(8,128)(2,1)} %wo_ref.1) | copy-start | bytes 82948
  1.1 7.1 %copy-start.3 = (bf16[24,576]{1,0:T(8,128)(2,1)S(1)}, bf16[24,576]{1,0:T(8,128)(2,1)}, u32[]{:S(2)}) copy-start(bf16[24,576]{1,0:T(8,128)(2,1)} %wq_ref.1) | copy-start | bytes 82948
  1.1 7.1 %copy-start.4 = (bf16[24,576]{1,0:T(8,128)(2,1)S(1)}, bf16[24,576]{1,0:T(8,128)(2,1)}, u32[]{:S(2)}) copy-start(bf16[24,576]{1,0:T(8,128)(2,1)} %wk_ref.1) | copy-start | bytes 82948
  1.1 7.1 %copy-start.5 = (bf16[24,576]{1,0:T(8,128)(2,1)S(1)}, bf16[24,576]{1,0:T(8,128)(2,1)}, u32[]{:S(2)}) copy-start(bf16[24,576]{1,0:T(8,128)(2,1)} %wv_ref.1) | copy-start | bytes 82948
  1.3 11.0 %collective-permute-start = (bf16[5,128,128]{2,1,0:T(8,128)(2,1)S(1)}, bf16[5,128,128]{2,1,0:T(8,128)(2,1)S(1)}, u32[]{:S(2)}, u32[]{:S(2)}) collective-permute-start(bf16[5,128,128]{2,1,0:T(8,128)(2,1)S(1)} %get-tuple-element.22.nb_ref), channel_id=1, source_target_pairs={{0,31},{1,2},{2,1},{3,4},{4,3},{5,6},{6,5},{7,8},{8,7},{9,10},{10,... | collective-permute-start | bytes 491528 | tf_op jit(solution)/shard_map/ppermute | solution.py:272
  84.3 13.9 %copy-start.1 = (bf16[5,64,8,128]{3,2,1,0:T(8,128)(2,1)S(1)}, bf16[5,64,8,128]{3,2,1,0:T(8,128)(2,1)}, u32[]{:S(2)}) copy-start(bf16[5,64,8,128]{3,2,1,0:T(8,128)(2,1)} %f_ref.5) | copy-start | bytes 1966084

commit v10 on v9

--- a/solution.py
+++ b/solution.py
@@ -19,7 +19,7 @@
 EXT = COLS + 2
 ROWS = 16
 USED = EXT * CQ // MEM
-HEAD = 16
+HEAD = 8
 F32, BF16 = jnp.float32, jnp.bfloat16
 VMEM = pl.BlockSpec(memory_space=pltpu.VMEM)
 
@@ -190,25 +190,18 @@
         row = s * OWN
         free = [gs[1 + h, row + 4 : row + 5, :] for h in range(2)]
         ps[0, 4 * s : 4 * s + 4] = gs[0, row : row + 4, :] + jnp.concatenate(free + [rest], axis=0)
-    for part in range(2):
-        whole = ps[part]
-        high = whole.astype(BF16).astype(F32)
-        ps[part] = high
-        ps[part + 1] = whole - high
+    whole = ps[0]
+    high = whole.astype(BF16).astype(F32)
+    ps[0] = high
+    ps[1] = whole - high
     for s in range(MEM):
-        for part in range(3):
-            ps[3, 4 * part : 4 * part + 4] = ps[part, 4 * s : 4 * s + 4]
-        ps[3, 12:HEAD] = jnp.zeros((HEAD - 12, LAT), F32)
-        o_ref[s, 0:HEAD] = ps[3, 0:HEAD].astype(BF16)
-
-
-def total_kernel(x_ref, o_ref):
+        parts = [ps[part, 4 * s : 4 * s + 4] for part in range(2)]
+        o_ref[s, 0:HEAD] = jnp.concatenate(parts, axis=0).astype(BF16)
+
+
+def spread_kernel(x_ref, o_ref):
     parts = jnp.sum(x_ref[:, 0:HEAD].astype(F32), axis=0)
-    o_ref[...] = parts[0:4] + parts[4:8] + parts[8:12]
-
-
-def spread_kernel(x_ref, o_ref):
-    o_ref[...] = jnp.broadcast_to((x_ref[0] + x_ref[1])[None], o_ref.shape)
+    o_ref[...] = jnp.broadcast_to((parts[0:4] + parts[4:8])[None], o_ref.shape)
 
 
 def softmax_kernel(scale, x_ref, v1_ref, o_ref, gs):
@@ -312,7 +305,7 @@
         got_nb,
         alias={0: 0, 1: 1, 2: 2},
     )
-    mem, lon = ("z", "ylo"), ("yhi", "x")
+    mem, lon = ("z", "ylo"), ("yhi", "x", "core")
     qk = lax.all_to_all(qk, mem, 0, 0, tiled=True)
     v0 = call(
         gram_kernel,
@@ -320,7 +313,7 @@
         [
             pltpu.VMEM((TOTAL * CQ, LAT), F32),
             pltpu.VMEM((3, TOTAL, LAT), F32),
-            pltpu.VMEM((4, 4 * MEM, LAT), F32),
+            pltpu.VMEM((2, 4 * MEM, LAT), F32),
         ],
         20_000_000,
         800_000,
@@ -329,10 +322,8 @@
         alias={1: 0},
     )
     v0 = lax.all_to_all(v0, mem, 0, 0, tiled=True)
-    gram = call(total_kernel, jax.ShapeDtypeStruct((4, LAT), F32), [], 40_000, 200_000, v0)
-    gram = lax.all_gather(gram, "core", axis=0, tiled=False)
-    copies = jax.ShapeDtypeStruct((LON // 2, 4, LAT), F32)
-    gram = call(spread_kernel, copies, [], 10_000, 40_000, gram)
+    copies = jax.ShapeDtypeStruct((LON, 4, LAT), F32)
+    gram = call(spread_kernel, copies, [], 40_000, 200_000, v0)
     gram = lax.all_to_all(gram, lon, 0, 0, tiled=True)
     scale = 1.0 / math.sqrt(CQ * LAT * COLS * LON)
     v1 = call(

time: 100 us -> 100 us (level)
    all_gather x1 -> x0, blocking collectives: 1.78 us -> none  [shards(): gram = lax.all_gather(gram, 'core', axis=0, tiled=False)]
    all_to_all x1, blocking collectives: 13.5 us -> 15 us  [shards(): mixed = lax.all_to_all(mixed, ('z', 'ylo'), 0, 0, tiled=True)]
    pallas_call x9 -> x8, Pallas kernels: 4.57 us -> 4.5 us  [call(): pl.pallas_call(body, out_shape=outs, in_specs=[VMEM] * len(args), out_spe...]
where the time goes in v10:
time: 100 us; the launch traced here: 99.8 us
  blocking collectives  86.4 us (86%)
  starting transfers between devices  6.9 us (7%)
  Pallas kernels  4.5 us (4%)
  local copies, waits for them, and re-layouts  1.11 us (1%)
    all_to_all x1, blocking collectives, shards(): qk = lax.all_to_all(qk, mem, 0, 0, tiled=True)  26.6 us
    all_to_all x1, blocking collectives, shards(): gram = lax.all_to_all(gram, lon, 0, 0, tiled=True)  16.2 us
    all_to_all x1, blocking collectives, shards(): mixed = lax.all_to_all(mixed, ('z', 'ylo'), 0, 0, tiled=True)  15 us
    all_to_all x1, blocking collectives, shards(): v0 = lax.all_to_all(v0, mem, 0, 0, tiled=True)  13.6 us
    all_to_all x1, blocking collectives, shards(): v1 = lax.all_to_all(v1, mem, 0, 0, tiled=True)  13 us
    ppermute x1, starting transfers between devices, shards(): got_nb = lax.ppermute(nb, ('yhi', 'x', 'core'), swaps)  6.9 us
    pallas_call x8, Pallas kernels, call(): pl.pallas_call(body, out_shape=outs, in_specs=[VMEM] * len(args), out_spe...  4.5 us
    all_gather x1, blocking collectives, shards(): got_sib = lax.all_gather(sib, 'core', axis=0, tiled=False)  2.04 us
  transfers between devices with their start and end apart: 1, of which 1 were waited for; matrix products, arithmetic and copies ran while one was open for 0% of the time, Pallas kernels for 1%

profile of v10, /device:TPU:8, one launch (start us, length us, event | category | flops | bytes accessed | tf_op | source)
XLA Modules:
  0.0 99.8 jit_solution(16297142571216739956)
XLA Ops:
  0.0 0.0 copy-start
  0.0 1.1 %copy-done = bf16[5,64,8,128]{3,2,1,0:T(8,128)(2,1)S(1)} copy-done((bf16[5,64,8,128]{3,2,1,0:T(8,128)(2,1)S(1)}, bf16[5,64,8,128]{3,2,1,0:T(8,128)(2,1)}, u32[]{:S(2)}) %copy-start) | copy-done | bytes 655384
  1.1 0.0 copy-start.2
  1.1 0.0 copy-start.3
  1.1 0.2 shard_map.56
  1.3 6.9 %collective-permute-start = (bf16[5,128,128]{2,1,0:T(8,128)(2,1)S(1)}, bf16[5,128,128]{2,1,0:T(8,128)(2,1)S(1)}, u32[]{:S(2)}, u32[]{:S(2)}) collective-permute-start(bf16[5,128,128]{2,1,0:T(8,128)(2,1)S(1)} %get-tuple-element.22.nb_ref), channel_id=1, source_target_pairs={{0,31},{1,2},{2,1},{3,4},{4,3},{5,6},{6,5},{7,8},{8,7},{9,10},{10,... | collective-permute-start | bytes 491528 | tf_op jit(solution)/shard_map/ppermute | solution.py:265
  8.2 0.0 copy-done.2
  8.2 0.0 copy-done.3
  8.2 0.0 copy-done.4
  8.2 0.0 copy-done.5
  8.2 1.1 %shard_map.55 = (bf16[16,5,24,128]{3,2,1,0:T(8,128)(2,1)S(1)}, bf16[16,48,128]{2,1,0:T(8,128)(2,1)S(1)}, bf16[16,5,8,128]{3,2,1,0:T(8,128)(2,1)S(1)}, f32[5,32,1...) custom-call(bf16[5,64,8,128]{3,2,1,0:T(8,128)(2,1)S(1)} %copy-done, ...), custom_call_target="tpu_custom_call" | custom-call | flops 450000000 | bytes 2000000 | tf_op jit(solution)/shard_map/pallas_call | solution.py:33
  9.4 2.0 %all-gather = bf16[10,128,128]{2,1,0:T(8,128)(2,1)S(1)} all-gather(bf16[5,128,128]{2,1,0:T(8,128)(2,1)S(1)} %get-tuple-element.21.sib_ref), channel_id=2, replica_groups=mesh['z'=8,'ylo'=2,'yhi'=4,'x'=4,'core'=2] {'core'}, dimensions={0}, use_global_device_ids=true | all-gather | bytes 491520 | tf_op jit(solution)/shard_map/all_gather | solution.py:266
  11.4 0.8 collective-permute-done.gn_ref
  12.2 0.6 shard_map.57
  12.9 26.6 %all_to_all.25.x_ref = bf16[16,5,24,128]{3,2,1,0:T(8,128)(2,1)S(1)} all-to-all(bf16[16,5,24,128]{3,2,1,0:T(8,128)(2,1)S(1)} %get-tuple-element.23), channel_id=1, replica_groups=mesh['z'=8,'ylo'=2,'yhi'=4,'x'=4,'core'=2] {'z','ylo'}, dimensions={0} | all-to-all | bytes 983040 | tf_op jit(solution)/shard_map/all_to_all | solution.py:309
  39.5 0.4 shard_map.58
  39.9 13.6 %all_to_all.26.x_ref.v0_ref = bf16[16,48,128]{2,1,0:T(8,128)(2,1)S(1)} all-to-all(bf16[16,48,128]{2,1,0:T(8,128)(2,1)S(1)} %shard_map.58), channel_id=1, replica_groups=mesh['z'=8,'ylo'=2,'yhi'=4,'x'=4,'core'=2] {'z','ylo'}, dimensions={0} | all-to-all | bytes 393216 | tf_op jit(solution)/shard_map/all_to_all | solution.py:324
  53.5 16.2 %all_to_all.27.x_ref = f32[32,4,128]{2,1,0:T(4,128)S(1)} all-to-all(f32[32,4,128]{2,1,0:T(4,128)S(1)} %shard_map.59), channel_id=1, replica_groups=mesh['z'=8,'ylo'=2,'yhi'=4,'x'=4,'core'=2] {'yhi','x','core'}, dimensions={0} | all-to-all | bytes 131072 | tf_op jit(solution)/shard_map/all_to_all | solution.py:327
  69.7 0.3 shard_map.60
  70.0 13.0 %all_to_all.28.v1_ref = bf16[16,5,8,128]{3,2,1,0:T(8,128)(2,1)S(1)} all-to-all(bf16[16,5,8,128]{3,2,1,0:T(8,128)(2,1)S(1)} %shard_map.60), channel_id=1, replica_groups=mesh['z'=8,'ylo'=2,'yhi'=4,'x'=4,'core'=2] {'z','ylo'}, dimensions={0} | all-to-all | bytes 327680 | tf_op jit(solution)/shard_map/all_to_all | solution.py:339
  83.0 0.4 shard_map.61
  83.4 15.0 %all_to_all.29.x_ref = bf16[16,5,16,128]{3,2,1,0:T(8,128)(2,1)S(1)} all-to-all(bf16[16,5,16,128]{3,2,1,0:T(8,128)(2,1)S(1)} %shard_map.61), channel_id=1, replica_groups=mesh['z'=8,'ylo'=2,'yhi'=4,'x'=4,'core'=2] {'z','ylo'}, dimensions={0} | all-to-all | bytes 655360 | tf_op jit(solution)/shard_map/all_to_all | solution.py:349
  98.4 0.0 copy-done.1
  98.4 1.4 %shard_map.62 = bf16[5,64,8,128]{3,2,1,0:T(8,128)(2,1)} custom-call(bf16[16,5,16,128]{3,2,1,0:T(8,128)(2,1)S(1)} %all_to_all.29.x_ref, bf16[5,64,8,128]{3,2,1,0:T(8,128)(2,1)S(1)} %copy-done.1, bf16[128,288]{1,0:T(8,128)(2,1)S(1)} %get-tuple-element.26.w_ref), custom_call_target="tpu_custom_call" | custom-call | flops 150000000 | bytes 1700000 | tf_op jit(solution)/shard_map/pallas_call | solution.py:33
  (4 shorter events, 0.0 us)
Async XLA Ops:
  0.0 1.1 %copy-start = (bf16[5,64,8,128]{3,2,1,0:T(8,128)(2,1)S(1)}, bf16[5,64,8,128]{3,2,1,0:T(8,128)(2,1)}, u32[]{:S(2)}) copy-start(bf16[5,64,8,128]{3,2,1,0:T(8,128)(2,1)} %f_ref.5) | copy-start | bytes 1966084
  1.1 7.1 %copy-start.2 = (bf16[64,216]{1,0:T(8,128)(2,1)S(1)}, bf16[64,216]{1,0:T(8,128)(2,1)}, u32[]{:S(2)}) copy-start(bf16[64,216]{1,0:T(8,128)(2,1)} %wo_ref.1) | copy-start | bytes 82948
  1.1 7.1 %copy-start.3 = (bf16[24,576]{1,0:T(8,128)(2,1)S(1)}, bf16[24,576]{1,0:T(8,128)(2,1)}, u32[]{:S(2)}) copy-start(bf16[24,576]{1,0:T(8,128)(2,1)} %wq_ref.1) | copy-start | bytes 82948
  1.1 7.1 %copy-start.4 = (bf16[24,576]{1,0:T(8,128)(2,1)S(1)}, bf16[24,576]{1,0:T(8,128)(2,1)}, u32[]{:S(2)}) copy-start(bf16[24,576]{1,0:T(8,128)(2,1)} %wk_ref.1) | copy-start | bytes 82948
  1.1 7.1 %copy-start.5 = (bf16[24,576]{1,0:T(8,128)(2,1)S(1)}, bf16[24,576]{1,0:T(8,128)(2,1)}, u32[]{:S(2)}) copy-start(bf16[24,576]{1,0:T(8,128)(2,1)} %wv_ref.1) | copy-start | bytes 82948
  1.3 11.0 %collective-permute-start = (bf16[5,128,128]{2,1,0:T(8,128)(2,1)S(1)}, bf16[5,128,128]{2,1,0:T(8,128)(2,1)S(1)}, u32[]{:S(2)}, u32[]{:S(2)}) collective-permute-start(bf16[5,128,128]{2,1,0:T(8,128)(2,1)S(1)} %get-tuple-element.22.nb_ref), channel_id=1, source_target_pairs={{0,31},{1,2},{2,1},{3,4},{4,3},{5,6},{6,5},{7,8},{8,7},{9,10},{10,... | collective-permute-start | bytes 491528 | tf_op jit(solution)/shard_map/ppermute | solution.py:265
  83.0 15.4 %copy-start.1 = (bf16[5,64,8,128]{3,2,1,0:T(8,128)(2,1)S(1)}, bf16[5,64,8,128]{3,2,1,0:T(8,128)(2,1)}, u32[]{:S(2)}) copy-start(bf16[5,64,8,128]{3,2,1,0:T(8,128)(2,1)} %f_ref.5) | copy-start | bytes 1966084

commit v11 on v10

--- a/solution.py
+++ b/solution.py
@@ -199,9 +199,13 @@
         o_ref[s, 0:HEAD] = jnp.concatenate(parts, axis=0).astype(BF16)
 
 
+def total_kernel(x_ref, o_ref):
+    parts = jnp.sum(x_ref[:, 0:HEAD].astype(F32), axis=0)
+    o_ref[...] = parts[0:4] + parts[4:8]
+
+
 def spread_kernel(x_ref, o_ref):
-    parts = jnp.sum(x_ref[:, 0:HEAD].astype(F32), axis=0)
-    o_ref[...] = jnp.broadcast_to((parts[0:4] + parts[4:8])[None], o_ref.shape)
+    o_ref[...] = jnp.broadcast_to((x_ref[0] + x_ref[1])[None], o_ref.shape)
 
 
 def softmax_kernel(scale, x_ref, v1_ref, o_ref, gs):
@@ -305,7 +309,7 @@
         got_nb,
         alias={0: 0, 1: 1, 2: 2},
     )
-    mem, lon = ("z", "ylo"), ("yhi", "x", "core")
+    mem, lon = ("z", "ylo"), ("yhi", "x")
     qk = lax.all_to_all(qk, mem, 0, 0, tiled=True)
     v0 = call(
         gram_kernel,
@@ -322,8 +326,10 @@
         alias={1: 0},
     )
     v0 = lax.all_to_all(v0, mem, 0, 0, tiled=True)
-    copies = jax.ShapeDtypeStruct((LON, 4, LAT), F32)
-    gram = call(spread_kernel, copies, [], 40_000, 200_000, v0)
+    gram = call(total_kernel, jax.ShapeDtypeStruct((4, LAT), F32), [], 40_000, 200_000, v0)
+    gram = lax.all_gather(gram, "core", axis=0, tiled=False)
+    copies = jax.ShapeDtypeStruct((LON // 2, 4, LAT), F32)
+    gram = call(spread_kernel, copies, [], 10_000, 40_000, gram)
     gram = lax.all_to_all(gram, lon, 0, 0, tiled=True)
     scale = 1.0 / math.sqrt(CQ * LAT * COLS * LON)
     v1 = call(

time: 100 us -> 99.2 us (level)
  blocking collectives: 86.4 us -> 85.4 us
    all_gather x0 -> x1, blocking collectives: none -> 1.78 us  [shards(): gram = lax.all_gather(gram, 'core', axis=0, tiled=False)]
    all_to_all x1, blocking collectives: 15 us -> 13.5 us  [shards(): mixed = lax.all_to_all(mixed, ('z', 'ylo'), 0, 0, tiled=True)]
    all_to_all x1, blocking collectives: 13 us -> 11.9 us  [shards(): v1 = lax.all_to_all(v1, mem, 0, 0, tiled=True)]
    pallas_call x8 -> x9, Pallas kernels: 4.5 us -> 4.48 us  [call(): pl.pallas_call(body, out_shape=outs, in_specs=[VMEM] * len(args), out_spe...]
where the time goes in v11:
time: 99.2 us; the launch traced here: 98.8 us
  blocking collectives  85.4 us (86%)
  starting transfers between devices  6.9 us (7%)
  Pallas kernels  4.48 us (5%)
  local copies, waits for them, and re-layouts  1.11 us (1%)
    all_to_all x1, blocking collectives, shards(): qk = lax.all_to_all(qk, mem, 0, 0, tiled=True)  26.6 us
    all_to_all x1, blocking collectives, shards(): gram = lax.all_to_all(gram, lon, 0, 0, tiled=True)  16 us
    all_to_all x1, blocking collectives, shards(): v0 = lax.all_to_all(v0, mem, 0, 0, tiled=True)  13.6 us
    all_to_all x1, blocking collectives, shards(): mixed = lax.all_to_all(mixed, ('z', 'ylo'), 0, 0, tiled=True)  13.5 us
    all_to_all x1, blocking collectives, shards(): v1 = lax.all_to_all(v1, mem, 0, 0, tiled=True)  11.9 us
    ppermute x1, starting transfers between devices, shards(): got_nb = lax.ppermute(nb, ('yhi', 'x', 'core'), swaps)  6.9 us
    pallas_call x9, Pallas kernels, call(): pl.pallas_call(body, out_shape=outs, in_specs=[VMEM] * len(args), out_spe...  4.48 us
    all_gather x1, blocking collectives, shards(): got_sib = lax.all_gather(sib, 'core', axis=0, tiled=False)  2.04 us
  transfers between devices with their start and end apart: 1, of which 1 were waited for; matrix products, arithmetic and copies ran while one was open for 0% of the time, Pallas kernels for 1%

profile of v11, /device:TPU:8, one launch (start us, length us, event | category | flops | bytes accessed | tf_op | source)
XLA Modules:
  0.0 98.8 jit_solution(12037379418001324547)
XLA Ops:
  0.0 0.0 copy-start
  0.0 1.1 %copy-done = bf16[5,64,8,128]{3,2,1,0:T(8,128)(2,1)S(1)} copy-done((bf16[5,64,8,128]{3,2,1,0:T(8,128)(2,1)S(1)}, bf16[5,64,8,128]{3,2,1,0:T(8,128)(2,1)}, u32[]{:S(2)}) %copy-start) | copy-done | bytes 655384
  1.1 0.0 copy-start.2
  1.1 0.2 shard_map.56
  1.3 6.9 %collective-permute-start = (bf16[5,128,128]{2,1,0:T(8,128)(2,1)S(1)}, bf16[5,128,128]{2,1,0:T(8,128)(2,1)S(1)}, u32[]{:S(2)}, u32[]{:S(2)}) collective-permute-start(bf16[5,128,128]{2,1,0:T(8,128)(2,1)S(1)} %get-tuple-element.22.nb_ref), channel_id=1, source_target_pairs={{0,31},{1,2},{2,1},{3,4},{4,3},{5,6},{6,5},{7,8},{8,7},{9,10},{10,... | collective-permute-start | bytes 491528 | tf_op jit(solution)/shard_map/ppermute | solution.py:269
  8.2 0.0 copy-done.2
  8.2 0.0 copy-done.3
  8.2 0.0 copy-done.4
  8.2 0.0 copy-done.5
  8.2 1.1 %shard_map.55 = (bf16[16,5,24,128]{3,2,1,0:T(8,128)(2,1)S(1)}, bf16[16,48,128]{2,1,0:T(8,128)(2,1)S(1)}, bf16[16,5,8,128]{3,2,1,0:T(8,128)(2,1)S(1)}, f32[5,32,1...) custom-call(bf16[5,64,8,128]{3,2,1,0:T(8,128)(2,1)S(1)} %copy-done, ...), custom_call_target="tpu_custom_call" | custom-call | flops 450000000 | bytes 2000000 | tf_op jit(solution)/shard_map/pallas_call | solution.py:33
  9.4 2.0 %all-gather = bf16[10,128,128]{2,1,0:T(8,128)(2,1)S(1)} all-gather(bf16[5,128,128]{2,1,0:T(8,128)(2,1)S(1)} %get-tuple-element.21.sib_ref), channel_id=2, replica_groups=mesh['z'=8,'ylo'=2,'yhi'=4,'x'=4,'core'=2] {'core'}, dimensions={0}, use_global_device_ids=true | all-gather | bytes 491520 | tf_op jit(solution)/shard_map/all_gather | solution.py:270
  11.4 0.8 collective-permute-done.gn_ref
  12.2 0.6 shard_map.57
  12.9 26.6 %all_to_all.25.x_ref = bf16[16,5,24,128]{3,2,1,0:T(8,128)(2,1)S(1)} all-to-all(bf16[16,5,24,128]{3,2,1,0:T(8,128)(2,1)S(1)} %get-tuple-element.23), channel_id=1, replica_groups=mesh['z'=8,'ylo'=2,'yhi'=4,'x'=4,'core'=2] {'z','ylo'}, dimensions={0} | all-to-all | bytes 983040 | tf_op jit(solution)/shard_map/all_to_all | solution.py:313
  39.5 0.4 shard_map.58
  39.9 13.6 %all_to_all.26.x_ref.v0_ref = bf16[16,48,128]{2,1,0:T(8,128)(2,1)S(1)} all-to-all(bf16[16,48,128]{2,1,0:T(8,128)(2,1)S(1)} %shard_map.58), channel_id=1, replica_groups=mesh['z'=8,'ylo'=2,'yhi'=4,'x'=4,'core'=2] {'z','ylo'}, dimensions={0} | all-to-all | bytes 393216 | tf_op jit(solution)/shard_map/all_to_all | solution.py:328
  53.5 1.8 %all-gather.2.x_ref = f32[2,4,128]{2,1,0:T(4,128)S(1)} all-gather(f32[1,4,128]{2,1,0:T(4,128)S(1)} %bitcast.3), channel_id=3, replica_groups=mesh['z'=8,'ylo'=2,'yhi'=4,'x'=4,'core'=2] {'core'}, dimensions={0}, use_global_device_ids=true | all-gather | bytes 6144 | tf_op jit(solution)/shard_map/all_gather | solution.py:330
  55.3 16.0 %all_to_all.27.x_ref = f32[16,4,128]{2,1,0:T(4,128)S(1)} all-to-all(f32[16,4,128]{2,1,0:T(4,128)S(1)} %shard_map.60), channel_id=1, replica_groups=mesh['z'=8,'ylo'=2,'yhi'=4,'x'=4,'core'=2] {'yhi','x'}, dimensions={0} | all-to-all | bytes 65536 | tf_op jit(solution)/shard_map/all_to_all | solution.py:333
  71.3 0.3 shard_map.61
  71.6 11.9 %all_to_all.28.v1_ref = bf16[16,5,8,128]{3,2,1,0:T(8,128)(2,1)S(1)} all-to-all(bf16[16,5,8,128]{3,2,1,0:T(8,128)(2,1)S(1)} %shard_map.61), channel_id=1, replica_groups=mesh['z'=8,'ylo'=2,'yhi'=4,'x'=4,'core'=2] {'z','ylo'}, dimensions={0} | all-to-all | bytes 327680 | tf_op jit(solution)/shard_map/all_to_all | solution.py:345
  83.5 0.4 shard_map.62
  83.9 13.5 %all_to_all.29.x_ref = bf16[16,5,16,128]{3,2,1,0:T(8,128)(2,1)S(1)} all-to-all(bf16[16,5,16,128]{3,2,1,0:T(8,128)(2,1)S(1)} %shard_map.62), channel_id=1, replica_groups=mesh['z'=8,'ylo'=2,'yhi'=4,'x'=4,'core'=2] {'z','ylo'}, dimensions={0} | all-to-all | bytes 655360 | tf_op jit(solution)/shard_map/all_to_all | solution.py:355
  97.4 0.0 copy-done.1
  97.4 1.4 %shard_map.63 = bf16[5,64,8,128]{3,2,1,0:T(8,128)(2,1)} custom-call(bf16[16,5,16,128]{3,2,1,0:T(8,128)(2,1)S(1)} %all_to_all.29.x_ref, bf16[5,64,8,128]{3,2,1,0:T(8,128)(2,1)S(1)} %copy-done.1, bf16[128,288]{1,0:T(8,128)(2,1)S(1)} %get-tuple-element.26.w_ref), custom_call_target="tpu_custom_call" | custom-call | flops 150000000 | bytes 1700000 | tf_op jit(solution)/shard_map/pallas_call | solution.py:33
  (6 shorter events, 0.0 us)
Async XLA Ops:
  0.0 1.1 %copy-start = (bf16[5,64,8,128]{3,2,1,0:T(8,128)(2,1)S(1)}, bf16[5,64,8,128]{3,2,1,0:T(8,128)(2,1)}, u32[]{:S(2)}) copy-start(bf16[5,64,8,128]{3,2,1,0:T(8,128)(2,1)} %f_ref.5) | copy-start | bytes 1966084
  1.1 7.1 %copy-start.2 = (bf16[64,216]{1,0:T(8,128)(2,1)S(1)}, bf16[64,216]{1,0:T(8,128)(2,1)}, u32[]{:S(2)}) copy-start(bf16[64,216]{1,0:T(8,128)(2,1)} %wo_ref.1) | copy-start | bytes 82948
  1.1 7.1 %copy-start.3 = (bf16[24,576]{1,0:T(8,128)(2,1)S(1)}, bf16[24,576]{1,0:T(8,128)(2,1)}, u32[]{:S(2)}) copy-start(bf16[24,576]{1,0:T(8,128)(2,1)} %wq_ref.1) | copy-start | bytes 82948
  1.1 7.1 %copy-start.4 = (bf16[24,576]{1,0:T(8,128)(2,1)S(1)}, bf16[24,576]{1,0:T(8,128)(2,1)}, u32[]{:S(2)}) copy-start(bf16[24,576]{1,0:T(8,128)(2,1)} %wk_ref.1) | copy-start | bytes 82948
  1.1 7.1 %copy-start.5 = (bf16[24,576]{1,0:T(8,128)(2,1)S(1)}, bf16[24,576]{1,0:T(8,128)(2,1)}, u32[]{:S(2)}) copy-start(bf16[24,576]{1,0:T(8,128)(2,1)} %wv_ref.1) | copy-start | bytes 82948
  1.3 11.0 %collective-permute-start = (bf16[5,128,128]{2,1,0:T(8,128)(2,1)S(1)}, bf16[5,128,128]{2,1,0:T(8,128)(2,1)S(1)}, u32[]{:S(2)}, u32[]{:S(2)}) collective-permute-start(bf16[5,128,128]{2,1,0:T(8,128)(2,1)S(1)} %get-tuple-element.22.nb_ref), channel_id=1, source_target_pairs={{0,31},{1,2},{2,1},{3,4},{4,3},{5,6},{6,5},{7,8},{8,7},{9,10},{10,... | collective-permute-start | bytes 491528 | tf_op jit(solution)/shard_map/ppermute | solution.py:269
  83.5 13.9 %copy-start.1 = (bf16[5,64,8,128]{3,2,1,0:T(8,128)(2,1)S(1)}, bf16[5,64,8,128]{3,2,1,0:T(8,128)(2,1)}, u32[]{:S(2)}) copy-start(bf16[5,64,8,128]{3,2,1,0:T(8,128)(2,1)} %f_ref.5) | copy-start | bytes 1966084

commit v12 on v11

--- a/solution.py
+++ b/solution.py
@@ -94,7 +94,8 @@
 
 
 def inner_kernel(
-    f_ref, wq_ref, wk_ref, wv_ref, wo_ref, qk_ref, v0_ref, v1_ref, e_ref, wp_ref, wf_ref, ws, xf, xt, vs
+    f_ref, wq_ref, wk_ref, wv_ref, wo_ref,
+    qk_ref, v0_ref, v1_ref, e_ref, wp_ref, wf_ref, xt, ws, xf, vs,
 ):
     ws[0:HALF] = wq_ref[...].astype(F32)[:HALF]
     ws[HALF : 2 * HALF] = wk_ref[...].astype(F32)[:HALF]
@@ -110,11 +111,14 @@
             wp_ref[row : row + 3 * CQ] = jnp.concatenate(full, axis=1).astype(BF16)
     wo = wo_ref[...].astype(F32)
     zero = jnp.zeros((CH, CQ), F32)
+    row = lax.broadcasted_iota(jnp.int32, (CH, 2 * CH), 0)
+    lane = lax.broadcasted_iota(jnp.int32, (CH, 2 * CH), 1)
     for s in range(2):
         full = []
         for b in range(3):
             taps = [wo[:, (3 * a + b) * CQ : (3 * a + b + 1) * CQ] for a in range(3)]
             full += [zero] + taps if s else taps + [zero]
+        full.append(jnp.where(lane == row + s * CH, 1.0, 0.0))
         wf_ref[s * CH : (s + 1) * CH] = jnp.concatenate(full, axis=1).astype(BF16)
     for m in range(OWN):
         xf[...] = f_ref[m].astype(F32).reshape(CH * COLS, LAT)
@@ -237,7 +241,7 @@
     o_ref[...] = ms[...].astype(BF16).reshape(o_ref.shape)
 
 
-def finish_kernel(x_ref, f_ref, w_ref, o_ref, mc, sh, br, ob, sem):
+def finish_kernel(x_ref, xt_ref, w_ref, o_ref, mc, sh, br, ob, sem):
     copies = [pltpu.make_async_copy(ob.at[m], o_ref.at[m], sem.at[m]) for m in range(OWN)]
     for m in range(OWN):
         for j in range(MEM):
@@ -247,15 +251,16 @@
         for b, x in enumerate((before, whole, after)):
             sh[b] = x.astype(BF16)
         for i in range(0, COLS, 4):
-            patches = [
-                jnp.concatenate([sh[b, p * CQ : (p + 4) * CQ] for b in range(3)], axis=0)
-                for p in (i, i + 2)
-            ]
+            patches = []
+            for p in (i, i + 2):
+                parts = [sh[b, p * CQ : (p + 4) * CQ] for b in range(3)]
+                parts.append(xt_ref[m, p * CH : (p + 2) * CH])
+                patches.append(jnp.concatenate(parts, axis=0))
             r = jnp.dot(w_ref[...], jnp.concatenate(patches, axis=1), preferred_element_type=F32)
             for n in range(4):
                 rows, lanes = (n % 2) * CH, (n // 2) * LAT
                 br[pl.ds(i + n, CH, stride=COLS), :] = r[rows : rows + CH, lanes : lanes + LAT]
-        ob[m] = (f_ref[m].astype(F32) + br[...].reshape(CH, COLS, LAT)).astype(BF16)
+        ob[m] = br[...].reshape(CH, COLS, LAT).astype(BF16)
         copies[m].start()
     for copy in copies:
         copy.wait()
@@ -273,14 +278,14 @@
     v1_shape = jax.ShapeDtypeStruct((MEM, OWN, 8, LAT), BF16)
     ends = jax.ShapeDtypeStruct((OWN, 2 * ROWS, LAT), F32)
     pair = jax.ShapeDtypeStruct((18 * CQ, 4 * CH), BF16)
-    pair_out = jax.ShapeDtypeStruct((2 * CH, 12 * CQ), BF16)
-    qk, v0, v1, ends, w_pair, w_last = call(
+    pair_out = jax.ShapeDtypeStruct((2 * CH, 12 * CQ + 2 * CH), BF16)
+    turned = jax.ShapeDtypeStruct((OWN, CH * COLS, LAT), BF16)
+    qk, v0, v1, ends, w_pair, w_last, turned = call(
         inner_kernel,
-        (qk_shape, v0_shape, v1_shape, ends, pair, pair_out),
+        (qk_shape, v0_shape, v1_shape, ends, pair, pair_out, turned),
         [
             pltpu.VMEM((3 * CQ, 9 * CH), F32),
             plane,
-            pltpu.VMEM((OWN, CH * COLS, LAT), BF16),
             pltpu.VMEM((OWN, 6 * CQ, LAT), F32),
         ],
         450_000_000,
@@ -366,7 +371,7 @@
         150_000_000,
         1_700_000,
         mixed,
-        fields,
+        turned,
         w_last,
         far_out=True,
     )

time: 99.2 us -> 99.2 us (level)
  no operation moved by 1% of the time
where the time goes in v12:
time: 99.2 us; the launch traced here: 98.8 us
  blocking collectives  85.4 us (86%)
  starting transfers between devices  6.9 us (7%)
  Pallas kernels  4.47 us (5%)
  local copies, waits for them, and re-layouts  1.1 us (1%)
    all_to_all x1, blocking collectives, shards(): qk = lax.all_to_all(qk, mem, 0, 0, tiled=True)  26.6 us
    all_to_all x1, blocking collectives, shards(): gram = lax.all_to_all(gram, lon, 0, 0, tiled=True)  16 us
    all_to_all x1, blocking collectives, shards(): v0 = lax.all_to_all(v0, mem, 0, 0, tiled=True)  13.6 us
    all_to_all x1, blocking collectives, shards(): mixed = lax.all_to_all(mixed, ('z', 'ylo'), 0, 0, tiled=True)  13.5 us
    all_to_all x1, blocking collectives, shards(): v1 = lax.all_to_all(v1, mem, 0, 0, tiled=True)  11.9 us
    ppermute x1, starting transfers between devices, shards(): got_nb = lax.ppermute(nb, ('yhi', 'x', 'core'), swaps)  6.9 us
    pallas_call x9, Pallas kernels, call(): pl.pallas_call(body, out_shape=outs, in_specs=[VMEM] * len(args), out_spe...  4.47 us
    all_gather x1, blocking collectives, shards(): got_sib = lax.all_gather(sib, 'core', axis=0, tiled=False)  2.04 us
  transfers between devices with their start and end apart: 1, of which 1 were waited for; matrix products, arithmetic and copies ran while one was open for 0% of the time, Pallas kernels for 1%

profile of v12, /device:TPU:8, one launch (start us, length us, event | category | flops | bytes accessed | tf_op | source)
XLA Modules:
  0.0 98.8 jit_solution(16334622627061323306)
XLA Ops:
  0.0 0.0 copy-start
  0.0 1.1 %copy-done = bf16[5,64,8,128]{3,2,1,0:T(8,128)(2,1)S(1)} copy-done((bf16[5,64,8,128]{3,2,1,0:T(8,128)(2,1)S(1)}, bf16[5,64,8,128]{3,2,1,0:T(8,128)(2,1)}, u32[]{:S(2)}) %copy-start) | copy-done | bytes 655384
  1.1 0.0 copy-start.1
  1.1 0.0 copy-start.2
  1.1 0.2 shard_map.56
  1.3 6.9 %collective-permute-start = (bf16[5,128,128]{2,1,0:T(8,128)(2,1)S(1)}, bf16[5,128,128]{2,1,0:T(8,128)(2,1)S(1)}, u32[]{:S(2)}, u32[]{:S(2)}) collective-permute-start(bf16[5,128,128]{2,1,0:T(8,128)(2,1)S(1)} %get-tuple-element.23.nb_ref), channel_id=1, source_target_pairs={{0,31},{1,2},{2,1},{3,4},{4,3},{5,6},{6,5},{7,8},{8,7},{9,10},{10,... | collective-permute-start | bytes 491528 | tf_op jit(solution)/shard_map/ppermute | solution.py:274
  8.2 0.0 copy-done.1
  8.2 0.0 copy-done.2
  8.2 0.0 copy-done.3
  8.2 0.0 copy-done.4
  8.2 1.1 %shard_map.55 = (bf16[16,5,24,128]{3,2,1,0:T(8,128)(2,1)S(1)}, bf16[16,48,128]{2,1,0:T(8,128)(2,1)S(1)}, bf16[16,5,8,128]{3,2,1,0:T(8,128)(2,1)S(1)}, f32[5,32,1...) custom-call(bf16[5,64,8,128]{3,2,1,0:T(8,128)(2,1)S(1)} %copy-done, ...), custom_call_target="tpu_custom_call" | custom-call | flops 450000000 | bytes 2000000 | tf_op jit(solution)/shard_map/pallas_call | solution.py:33
  9.4 2.0 %all-gather = bf16[10,128,128]{2,1,0:T(8,128)(2,1)S(1)} all-gather(bf16[5,128,128]{2,1,0:T(8,128)(2,1)S(1)} %get-tuple-element.22.sib_ref), channel_id=2, replica_groups=mesh['z'=8,'ylo'=2,'yhi'=4,'x'=4,'core'=2] {'core'}, dimensions={0}, use_global_device_ids=true | all-gather | bytes 491520 | tf_op jit(solution)/shard_map/all_gather | solution.py:275
  11.4 0.8 collective-permute-done.gn_ref
  12.2 0.6 shard_map.57
  12.9 26.6 %all_to_all.25.x_ref = bf16[16,5,24,128]{3,2,1,0:T(8,128)(2,1)S(1)} all-to-all(bf16[16,5,24,128]{3,2,1,0:T(8,128)(2,1)S(1)} %get-tuple-element.24), channel_id=1, replica_groups=mesh['z'=8,'ylo'=2,'yhi'=4,'x'=4,'core'=2] {'z','ylo'}, dimensions={0} | all-to-all | bytes 983040 | tf_op jit(solution)/shard_map/all_to_all | solution.py:318
  39.5 0.4 shard_map.58
  39.9 13.6 %all_to_all.26.x_ref.v0_ref = bf16[16,48,128]{2,1,0:T(8,128)(2,1)S(1)} all-to-all(bf16[16,48,128]{2,1,0:T(8,128)(2,1)S(1)} %shard_map.58), channel_id=1, replica_groups=mesh['z'=8,'ylo'=2,'yhi'=4,'x'=4,'core'=2] {'z','ylo'}, dimensions={0} | all-to-all | bytes 393216 | tf_op jit(solution)/shard_map/all_to_all | solution.py:333
  53.5 1.8 %all-gather.2.x_ref = f32[2,4,128]{2,1,0:T(4,128)S(1)} all-gather(f32[1,4,128]{2,1,0:T(4,128)S(1)} %bitcast.3), channel_id=3, replica_groups=mesh['z'=8,'ylo'=2,'yhi'=4,'x'=4,'core'=2] {'core'}, dimensions={0}, use_global_device_ids=true | all-gather | bytes 6144 | tf_op jit(solution)/shard_map/all_gather | solution.py:335
  55.3 16.0 %all_to_all.27.x_ref = f32[16,4,128]{2,1,0:T(4,128)S(1)} all-to-all(f32[16,4,128]{2,1,0:T(4,128)S(1)} %shard_map.60), channel_id=1, replica_groups=mesh['z'=8,'ylo'=2,'yhi'=4,'x'=4,'core'=2] {'yhi','x'}, dimensions={0} | all-to-all | bytes 65536 | tf_op jit(solution)/shard_map/all_to_all | solution.py:338
  71.3 0.3 shard_map.61
  71.6 11.9 %all_to_all.28.v1_ref = bf16[16,5,8,128]{3,2,1,0:T(8,128)(2,1)S(1)} all-to-all(bf16[16,5,8,128]{3,2,1,0:T(8,128)(2,1)S(1)} %shard_map.61), channel_id=1, replica_groups=mesh['z'=8,'ylo'=2,'yhi'=4,'x'=4,'core'=2] {'z','ylo'}, dimensions={0} | all-to-all | bytes 327680 | tf_op jit(solution)/shard_map/all_to_all | solution.py:350
  83.5 0.4 shard_map.62
  83.9 13.5 %all_to_all.29.x_ref = bf16[16,5,16,128]{3,2,1,0:T(8,128)(2,1)S(1)} all-to-all(bf16[16,5,16,128]{3,2,1,0:T(8,128)(2,1)S(1)} %shard_map.62), channel_id=1, replica_groups=mesh['z'=8,'ylo'=2,'yhi'=4,'x'=4,'core'=2] {'z','ylo'}, dimensions={0} | all-to-all | bytes 655360 | tf_op jit(solution)/shard_map/all_to_all | solution.py:360
  97.4 1.4 %shard_map.63 = bf16[5,64,8,128]{3,2,1,0:T(8,128)(2,1)} custom-call(bf16[16,5,16,128]{3,2,1,0:T(8,128)(2,1)S(1)} %all_to_all.29.x_ref, bf16[5,512,128]{2,1,0:T(8,128)(2,1)S(1)} %get-tuple-element.27.xt_ref, bf16[128,416]{1,0:T(8,128)(2,1)S(1)} %get-tuple-element.28.w_ref), custom_call_target="tpu_custom_call" | custom-call | flops 150000000 | bytes 1700000 | tf_op jit(solution)/shard_map/pallas_call | solution.py:33
  (4 shorter events, 0.0 us)
Async XLA Ops:
  0.0 1.1 %copy-start = (bf16[5,64,8,128]{3,2,1,0:T(8,128)(2,1)S(1)}, bf16[5,64,8,128]{3,2,1,0:T(8,128)(2,1)}, u32[]{:S(2)}) copy-start(bf16[5,64,8,128]{3,2,1,0:T(8,128)(2,1)} %f_ref.3) | copy-start | bytes 1966084
  1.1 7.1 %copy-start.1 = (bf16[64,216]{1,0:T(8,128)(2,1)S(1)}, bf16[64,216]{1,0:T(8,128)(2,1)}, u32[]{:S(2)}) copy-start(bf16[64,216]{1,0:T(8,128)(2,1)} %wo_ref.1) | copy-start | bytes 82948
  1.1 7.1 %copy-start.2 = (bf16[24,576]{1,0:T(8,128)(2,1)S(1)}, bf16[24,576]{1,0:T(8,128)(2,1)}, u32[]{:S(2)}) copy-start(bf16[24,576]{1,0:T(8,128)(2,1)} %wq_ref.1) | copy-start | bytes 82948
  1.1 7.1 %copy-start.3 = (bf16[24,576]{1,0:T(8,128)(2,1)S(1)}, bf16[24,576]{1,0:T(8,128)(2,1)}, u32[]{:S(2)}) copy-start(bf16[24,576]{1,0:T(8,128)(2,1)} %wk_ref.1) | copy-start | bytes 82948
  1.1 7.1 %copy-start.4 = (bf16[24,576]{1,0:T(8,128)(2,1)S(1)}, bf16[24,576]{1,0:T(8,128)(2,1)}, u32[]{:S(2)}) copy-start(bf16[24,576]{1,0:T(8,128)(2,1)} %wv_ref.1) | copy-start | bytes 82948
  1.3 11.0 %collective-permute-start = (bf16[5,128,128]{2,1,0:T(8,128)(2,1)S(1)}, bf16[5,128,128]{2,1,0:T(8,128)(2,1)S(1)}, u32[]{:S(2)}, u32[]{:S(2)}) collective-permute-start(bf16[5,128,128]{2,1,0:T(8,128)(2,1)S(1)} %get-tuple-element.23.nb_ref), channel_id=1, source_target_pairs={{0,31},{1,2},{2,1},{3,4},{4,3},{5,6},{6,5},{7,8},{8,7},{9,10},{10,... | collective-permute-start | bytes 491528 | tf_op jit(solution)/shard_map/ppermute | solution.py:274

commit v13 on v8

--- a/solution.py
+++ b/solution.py
@@ -87,7 +87,10 @@
                 qk_ref[2 * (col - 1) + h, m] = outs[s][h * CQ : (h + 1) * CQ].astype(BF16)
 
 
-def inner_kernel(f_ref, wq_ref, wk_ref, wv_ref, qk_ref, v_ref, e_ref, wp_ref, ws, xf, xt, vs):
+def inner_kernel(
+    f_ref, wq_ref, wk_ref, wv_ref, wo_ref,
+    qk_ref, v_ref, e_ref, wp_ref, wf_ref, xt, ws, xf, vs,
+):
     ws[0:HALF] = wq_ref[...].astype(F32)[:HALF]
     ws[HALF : 2 * HALF] = wk_ref[...].astype(F32)[:HALF]
     ws[2 * HALF : 3 * HALF] = wq_ref[...].astype(F32)[HALF:]
@@ -100,6 +103,17 @@
             row = (3 * s + b) * 3 * CQ
             full = [zero] + taps if s else taps + [zero]
             wp_ref[row : row + 3 * CQ] = jnp.concatenate(full, axis=1).astype(BF16)
+    wo = wo_ref[...].astype(F32)
+    zero = jnp.zeros((CH, CQ), F32)
+    row = lax.broadcasted_iota(jnp.int32, (CH, 2 * CH), 0)
+    lane = lax.broadcasted_iota(jnp.int32, (CH, 2 * CH), 1)
+    for s in range(2):
+        full = []
+        for b in range(3):
+            taps = [wo[:, (3 * a + b) * CQ : (3 * a + b + 1) * CQ] for a in range(3)]
+            full += [zero] + taps if s else taps + [zero]
+        full.append(jnp.where(lane == row + s * CH, 1.0, 0.0))
+        wf_ref[s * CH : (s + 1) * CH] = jnp.concatenate(full, axis=1).astype(BF16)
     for m in range(OWN):
         xf[...] = f_ref[m].astype(F32).reshape(CH * COLS, LAT)
         for i in range(COLS):
@@ -119,7 +133,8 @@
 
 
 def outer_kernel(
-    iq_ref, iv_ref, e_ref, wp_ref, sib_ref, nb_ref, gs_ref, gn_ref, qk_ref, v_ref, xl, xr, vl, vr
+    iq_ref, iv_ref, e_ref, wp_ref, sib_ref, nb_ref, gs_ref, gn_ref,
+    qk_ref, v_ref, xl, xr, vl, vr
 ):
     core = lax.axis_index("core")
     near = 2 * CH
@@ -175,8 +190,12 @@
         g_ref[s] = gs[0, row : row + 4, :] + jnp.concatenate(free + [rest], axis=0)
 
 
+def total_kernel(x_ref, o_ref):
+    o_ref[...] = jnp.sum(x_ref[...], axis=0)
+
+
 def spread_kernel(x_ref, o_ref):
-    o_ref[...] = jnp.broadcast_to(jnp.sum(x_ref[...], axis=0)[None], o_ref.shape)
+    o_ref[...] = jnp.broadcast_to((x_ref[0] + x_ref[1])[None], o_ref.shape)
 
 
 def softmax_kernel(scale, x_ref, v_ref, o_ref, gs):
@@ -206,23 +225,26 @@
     o_ref[...] = ms[...].astype(BF16).reshape(o_ref.shape)
 
 
-def finish_kernel(x_ref, f_ref, w_ref, o_ref, mc, mb, ma, br, ob, sem):
+def finish_kernel(x_ref, xt_ref, w_ref, o_ref, mc, sh, br, ob, sem):
     copies = [pltpu.make_async_copy(ob.at[m], o_ref.at[m], sem.at[m]) for m in range(OWN)]
     for m in range(OWN):
         for j in range(MEM):
             mc[j * USED : j * USED + ROWS] = x_ref[j, m].astype(F32)
-        mb[...], ma[...] = lat_shifts(mc[...])
-        for i in range(0, COLS, 2):
+        whole = mc[0 : EXT * CQ]
+        before, after = lat_shifts(whole)
+        for b, x in enumerate((before, whole, after)):
+            sh[b] = x.astype(BF16)
+        for i in range(0, COLS, 4):
             patches = []
-            for col in (i, i + 1):
-                parts = [
-                    t[(col + a) * CQ : (col + a + 1) * CQ, :] for a in range(3) for t in (mb, mc, ma)
-                ]
-                patches.append(jnp.concatenate(parts, axis=0).astype(BF16))
+            for p in (i, i + 2):
+                parts = [sh[b, p * CQ : (p + 4) * CQ] for b in range(3)]
+                parts.append(xt_ref[m, p * CH : (p + 2) * CH])
+                patches.append(jnp.concatenate(parts, axis=0))
             r = jnp.dot(w_ref[...], jnp.concatenate(patches, axis=1), preferred_element_type=F32)
-            for s in range(2):
-                br[pl.ds(i + s, CH, stride=COLS), :] = r[:, s * LAT : (s + 1) * LAT]
-        ob[m] = (f_ref[m].astype(F32) + br[...].reshape(CH, COLS, LAT)).astype(BF16)
+            for n in range(4):
+                rows, lanes = (n % 2) * CH, (n // 2) * LAT
+                br[pl.ds(i + n, CH, stride=COLS), :] = r[rows : rows + CH, lanes : lanes + LAT]
+        ob[m] = br[...].reshape(CH, COLS, LAT).astype(BF16)
         copies[m].start()
     for copy in copies:
         copy.wait()
@@ -239,13 +261,14 @@
     v_shape = jax.ShapeDtypeStruct((MEM, OWN, ROWS, LAT), BF16)
     ends = jax.ShapeDtypeStruct((OWN, 2 * ROWS, LAT), F32)
     pair = jax.ShapeDtypeStruct((18 * CQ, 4 * CH), BF16)
-    qk, v, ends, w_pair = call(
+    pair_out = jax.ShapeDtypeStruct((2 * CH, 12 * CQ + 2 * CH), BF16)
+    turned = jax.ShapeDtypeStruct((OWN, CH * COLS, LAT), BF16)
+    qk, v, ends, w_pair, w_last, turned = call(
         inner_kernel,
-        (qk_shape, v_shape, ends, pair),
+        (qk_shape, v_shape, ends, pair, pair_out, turned),
         [
             pltpu.VMEM((3 * CQ, 9 * CH), F32),
             plane,
-            pltpu.VMEM((OWN, CH * COLS, LAT), BF16),
             pltpu.VMEM((OWN, 6 * CQ, LAT), F32),
         ],
         450_000_000,
@@ -254,6 +277,7 @@
         w_query,
         w_key,
         w_value,
+        w_out,
     )
     qk, v = call(
         outer_kernel,
@@ -272,7 +296,7 @@
         got_nb,
         alias={0: 0, 1: 1},
     )
-    mem, lon = ("z", "ylo"), ("yhi", "x", "core")
+    mem, lon = ("z", "ylo"), ("yhi", "x")
     qk = lax.all_to_all(qk, mem, 0, 0, tiled=True)
     gram = call(
         gram_kernel,
@@ -283,7 +307,10 @@
         qk,
     )
     gram = lax.all_to_all(gram, mem, 0, 0, tiled=True)
-    gram = call(spread_kernel, jax.ShapeDtypeStruct((LON, 4, LAT), F32), [], 10_000, 100_000, gram)
+    gram = call(total_kernel, jax.ShapeDtypeStruct((4, LAT), F32), [], 10_000, 40_000, gram)
+    gram = lax.all_gather(gram, "core", axis=0, tiled=False)
+    copies = jax.ShapeDtypeStruct((LON // 2, 4, LAT), F32)
+    gram = call(spread_kernel, copies, [], 10_000, 40_000, gram)
     gram = lax.all_to_all(gram, lon, 0, 0, tiled=True)
     scale = 1.0 / math.sqrt(CQ * LAT * COLS * LON)
     v = call(
@@ -309,13 +336,18 @@
     return call(
         finish_kernel,
         jax.ShapeDtypeStruct(fields.shape, BF16),
-        [pltpu.VMEM((MEM * ROWS, LAT), F32)] * 3
-        + [plane, pltpu.VMEM(fields.shape, BF16), pltpu.SemaphoreType.DMA((OWN,))],
+        [
+            pltpu.VMEM((MEM * ROWS, LAT), F32),
+            pltpu.VMEM((3, EXT * CQ, LAT), BF16),
+            plane,
+            pltpu.VMEM(fields.shape, BF16),
+            pltpu.SemaphoreType.DMA((OWN,)),
+        ],
         150_000_000,
         1_700_000,
         mixed,
-        fields,
-        w_out,
+        turned,
+        w_last,
         far_out=True,
     )
 

time: 102 us -> 102 us (level)
    all_gather x0 -> x1, blocking collectives: none -> 1.78 us  [shards(): gram = lax.all_gather(gram, 'core', axis=0, tiled=False)]
    all_to_all x1, blocking collectives: 16.8 us -> 15.6 us  [shards(): v = lax.all_to_all(v, mem, 0, 0, tiled=True)]
    pallas_call x8 -> x9, Pallas kernels: 4.49 us -> 4.5 us  [call(): pl.pallas_call(body, out_shape=outs, in_specs=[VMEM] * len(args), out_spe...]
where the time goes in v13:
time: 102 us; the launch traced here: 101 us
  blocking collectives  88 us (86%)
  starting transfers between devices  6.9 us (7%)
  Pallas kernels  4.5 us (4%)
  local copies, waits for them, and re-layouts  1.1 us (1%)
    all_to_all x1, blocking collectives, shards(): qk = lax.all_to_all(qk, mem, 0, 0, tiled=True)  26.6 us
    all_to_all x1, blocking collectives, shards(): gram = lax.all_to_all(gram, lon, 0, 0, tiled=True)  15.8 us
    all_to_all x1, blocking collectives, shards(): v = lax.all_to_all(v, mem, 0, 0, tiled=True)  15.6 us
    all_to_all x1, blocking collectives, shards(): mixed = lax.all_to_all(mixed, ('z', 'ylo'), 0, 0, tiled=True)  15 us
    all_to_all x1, blocking collectives, shards(): gram = lax.all_to_all(gram, mem, 0, 0, tiled=True)  11.2 us
    ppermute x1, starting transfers between devices, shards(): got_nb = lax.ppermute(nb, ('yhi', 'x', 'core'), swaps)  6.9 us
    pallas_call x9, Pallas kernels, call(): pl.pallas_call(body, out_shape=outs, in_specs=[VMEM] * len(args), out_spe...  4.5 us
    all_gather x1, blocking collectives, shards(): got_sib = lax.all_gather(sib, 'core', axis=0, tiled=False)  2.04 us
  transfers between devices with their start and end apart: 1, of which 1 were waited for; matrix products, arithmetic and copies ran while one was open for 0% of the time, Pallas kernels for 1%

profile of v13, /device:TPU:8, one launch (start us, length us, event | category | flops | bytes accessed | tf_op | source)
XLA Modules:
  0.0 101.4 jit_solution(5552540384332477547)
XLA Ops:
  0.0 0.0 copy-start
  0.0 1.1 %copy-done = bf16[5,64,8,128]{3,2,1,0:T(8,128)(2,1)S(1)} copy-done((bf16[5,64,8,128]{3,2,1,0:T(8,128)(2,1)S(1)}, bf16[5,64,8,128]{3,2,1,0:T(8,128)(2,1)}, u32[]{:S(2)}) %copy-start) | copy-done | bytes 655384
  1.1 0.0 copy-start.1
  1.1 0.0 copy-start.2
  1.1 0.2 shard_map.56
  1.3 6.9 %collective-permute-start = (bf16[5,128,128]{2,1,0:T(8,128)(2,1)S(1)}, bf16[5,128,128]{2,1,0:T(8,128)(2,1)S(1)}, u32[]{:S(2)}, u32[]{:S(2)}) collective-permute-start(bf16[5,128,128]{2,1,0:T(8,128)(2,1)S(1)} %get-tuple-element.20.nb_ref), channel_id=1, source_target_pairs={{0,31},{1,2},{2,1},{3,4},{4,3},{5,6},{6,5},{7,8},{8,7},{9,10},{10,... | collective-permute-start | bytes 491528 | tf_op jit(solution)/shard_map/ppermute | solution.py:258
  8.2 0.0 copy-done.1
  8.2 0.0 copy-done.2
  8.2 0.0 copy-done.3
  8.2 0.0 copy-done.4
  8.2 1.1 %shard_map.55 = (bf16[16,5,24,128]{3,2,1,0:T(8,128)(2,1)S(1)}, bf16[16,5,16,128]{3,2,1,0:T(8,128)(2,1)S(1)}, f32[5,32,128]{2,1,0:T(8,128)S(1)}, bf16[432,256]{1,...) custom-call(bf16[5,64,8,128]{3,2,1,0:T(8,128)(2,1)S(1)} %copy-done, ...), custom_call_target="tpu_custom_call" | custom-call | flops 450000000 | bytes 2000000 | tf_op jit(solution)/shard_map/pallas_call | solution.py:32
  9.4 2.0 %all-gather = bf16[10,128,128]{2,1,0:T(8,128)(2,1)S(1)} all-gather(bf16[5,128,128]{2,1,0:T(8,128)(2,1)S(1)} %get-tuple-element.19.sib_ref), channel_id=2, replica_groups=mesh['z'=8,'ylo'=2,'yhi'=4,'x'=4,'core'=2] {'core'}, dimensions={0}, use_global_device_ids=true | all-gather | bytes 491520 | tf_op jit(solution)/shard_map/all_gather | solution.py:259
  11.4 0.8 collective-permute-done.gn_ref
  12.2 0.6 shard_map.57
  12.9 26.6 %all_to_all.25.x_ref = bf16[16,5,24,128]{3,2,1,0:T(8,128)(2,1)S(1)} all-to-all(bf16[16,5,24,128]{3,2,1,0:T(8,128)(2,1)S(1)} %get-tuple-element.21), channel_id=1, replica_groups=mesh['z'=8,'ylo'=2,'yhi'=4,'x'=4,'core'=2] {'z','ylo'}, dimensions={0} | all-to-all | bytes 983040 | tf_op jit(solution)/shard_map/all_to_all | solution.py:300
  39.5 0.4 shard_map.58
  39.8 11.2 %all_to_all.26.x_ref = f32[16,4,128]{2,1,0:T(4,128)S(1)} all-to-all(f32[16,4,128]{2,1,0:T(4,128)S(1)} %shard_map.58), channel_id=1, replica_groups=mesh['z'=8,'ylo'=2,'yhi'=4,'x'=4,'core'=2] {'z','ylo'}, dimensions={0} | all-to-all | bytes 65536 | tf_op jit(solution)/shard_map/all_to_all | solution.py:309
  51.1 1.8 %all-gather.2.x_ref = f32[2,4,128]{2,1,0:T(4,128)S(1)} all-gather(f32[1,4,128]{2,1,0:T(4,128)S(1)} %bitcast.3), channel_id=3, replica_groups=mesh['z'=8,'ylo'=2,'yhi'=4,'x'=4,'core'=2] {'core'}, dimensions={0}, use_global_device_ids=true | all-gather | bytes 6144 | tf_op jit(solution)/shard_map/all_gather | solution.py:311
  52.8 15.8 %all_to_all.27.x_ref = f32[16,4,128]{2,1,0:T(4,128)S(1)} all-to-all(f32[16,4,128]{2,1,0:T(4,128)S(1)} %shard_map.60), channel_id=1, replica_groups=mesh['z'=8,'ylo'=2,'yhi'=4,'x'=4,'core'=2] {'yhi','x'}, dimensions={0} | all-to-all | bytes 65536 | tf_op jit(solution)/shard_map/all_to_all | solution.py:314
  68.6 0.3 shard_map.61
  68.9 15.6 %all_to_all.28.x_ref = bf16[16,5,16,128]{3,2,1,0:T(8,128)(2,1)S(1)} all-to-all(bf16[16,5,16,128]{3,2,1,0:T(8,128)(2,1)S(1)} %shard_map.61), channel_id=1, replica_groups=mesh['z'=8,'ylo'=2,'yhi'=4,'x'=4,'core'=2] {'z','ylo'}, dimensions={0} | all-to-all | bytes 655360 | tf_op jit(solution)/shard_map/all_to_all | solution.py:326
  84.5 0.5 shard_map.62
  85.0 15.0 %all_to_all.29.x_ref = bf16[16,5,16,128]{3,2,1,0:T(8,128)(2,1)S(1)} all-to-all(bf16[16,5,16,128]{3,2,1,0:T(8,128)(2,1)S(1)} %shard_map.62), channel_id=1, replica_groups=mesh['z'=8,'ylo'=2,'yhi'=4,'x'=4,'core'=2] {'z','ylo'}, dimensions={0} | all-to-all | bytes 655360 | tf_op jit(solution)/shard_map/all_to_all | solution.py:335
  100.0 1.4 %shard_map.63 = bf16[5,64,8,128]{3,2,1,0:T(8,128)(2,1)} custom-call(bf16[16,5,16,128]{3,2,1,0:T(8,128)(2,1)S(1)} %all_to_all.29.x_ref, bf16[5,512,128]{2,1,0:T(8,128)(2,1)S(1)} %get-tuple-element.23.xt_ref, bf16[128,416]{1,0:T(8,128)(2,1)S(1)} %get-tuple-element.24.w_ref), custom_call_target="tpu_custom_call" | custom-call | flops 150000000 | bytes 1700000 | tf_op jit(solution)/shard_map/pallas_call | solution.py:32
  (4 shorter events, 0.0 us)
Async XLA Ops:
  0.0 1.1 %copy-start = (bf16[5,64,8,128]{3,2,1,0:T(8,128)(2,1)S(1)}, bf16[5,64,8,128]{3,2,1,0:T(8,128)(2,1)}, u32[]{:S(2)}) copy-start(bf16[5,64,8,128]{3,2,1,0:T(8,128)(2,1)} %f_ref.3) | copy-start | bytes 1966084
  1.1 7.1 %copy-start.1 = (bf16[64,216]{1,0:T(8,128)(2,1)S(1)}, bf16[64,216]{1,0:T(8,128)(2,1)}, u32[]{:S(2)}) copy-start(bf16[64,216]{1,0:T(8,128)(2,1)} %wo_ref.1) | copy-start | bytes 82948
  1.1 7.1 %copy-start.2 = (bf16[24,576]{1,0:T(8,128)(2,1)S(1)}, bf16[24,576]{1,0:T(8,128)(2,1)}, u32[]{:S(2)}) copy-start(bf16[24,576]{1,0:T(8,128)(2,1)} %wq_ref.1) | copy-start | bytes 82948
  1.1 7.1 %copy-start.3 = (bf16[24,576]{1,0:T(8,128)(2,1)S(1)}, bf16[24,576]{1,0:T(8,128)(2,1)}, u32[]{:S(2)}) copy-start(bf16[24,576]{1,0:T(8,128)(2,1)} %wk_ref.1) | copy-start | bytes 82948
  1.1 7.1 %copy-start.4 = (bf16[24,576]{1,0:T(8,128)(2,1)S(1)}, bf16[24,576]{1,0:T(8,128)(2,1)}, u32[]{:S(2)}) copy-start(bf16[24,576]{1,0:T(8,128)(2,1)} %wv_ref.1) | copy-start | bytes 82948
  1.3 11.0 %collective-permute-start = (bf16[5,128,128]{2,1,0:T(8,128)(2,1)S(1)}, bf16[5,128,128]{2,1,0:T(8,128)(2,1)S(1)}, u32[]{:S(2)}, u32[]{:S(2)}) collective-permute-start(bf16[5,128,128]{2,1,0:T(8,128)(2,1)S(1)} %get-tuple-element.20.nb_ref), channel_id=1, source_target_pairs={{0,31},{1,2},{2,1},{3,4},{4,3},{5,6},{6,5},{7,8},{8,7},{9,10},{10,... | collective-permute-start | bytes 491528 | tf_op jit(solution)/shard_map/ppermute | solution.py:258

commit v14 on v12

--- a/solution.py
+++ b/solution.py
@@ -172,7 +172,7 @@
             put_block(v0_ref, v1_ref, 12 + j, m, vr[row : row + ROWS])
 
 
-def gram_kernel(x_ref, v0_ref, o_ref, xs, gs, ps):
+def gram_kernel(x_ref, g_ref, xs, gs):
     xs[...] = x_ref[...].astype(F32).reshape(TOTAL * CQ, LAT)
     pad = jnp.zeros((LAT - TOTAL, LAT), BF16)
     q, k = [], []
@@ -193,8 +193,11 @@
     for s in range(MEM):
         row = s * OWN
         free = [gs[1 + h, row + 4 : row + 5, :] for h in range(2)]
-        ps[0, 4 * s : 4 * s + 4] = gs[0, row : row + 4, :] + jnp.concatenate(free + [rest], axis=0)
-    whole = ps[0]
+        g_ref[4 * s : 4 * s + 4] = gs[0, row : row + 4, :] + jnp.concatenate(free + [rest], axis=0)
+
+
+def header_kernel(g_ref, v0_ref, o_ref, ps):
+    whole = g_ref[0] + g_ref[1]
     high = whole.astype(BF16).astype(F32)
     ps[0] = high
     ps[1] = whole - high
@@ -203,13 +206,9 @@
         o_ref[s, 0:HEAD] = jnp.concatenate(parts, axis=0).astype(BF16)
 
 
-def total_kernel(x_ref, o_ref):
+def spread_kernel(x_ref, o_ref):
     parts = jnp.sum(x_ref[:, 0:HEAD].astype(F32), axis=0)
-    o_ref[...] = parts[0:4] + parts[4:8]
-
-
-def spread_kernel(x_ref, o_ref):
-    o_ref[...] = jnp.broadcast_to((x_ref[0] + x_ref[1])[None], o_ref.shape)
+    o_ref[...] = jnp.broadcast_to((parts[0:4] + parts[4:8])[None], o_ref.shape)
 
 
 def softmax_kernel(scale, x_ref, v1_ref, o_ref, gs):
@@ -316,25 +315,28 @@
     )
     mem, lon = ("z", "ylo"), ("yhi", "x")
     qk = lax.all_to_all(qk, mem, 0, 0, tiled=True)
+    gram = call(
+        gram_kernel,
+        jax.ShapeDtypeStruct((4 * MEM, LAT), F32),
+        [pltpu.VMEM((TOTAL * CQ, LAT), F32), pltpu.VMEM((3, TOTAL, LAT), F32)],
+        20_000_000,
+        600_000,
+        qk,
+    )
+    gram = lax.all_gather(gram, "core", axis=0, tiled=False)
     v0 = call(
-        gram_kernel,
+        header_kernel,
         v0_shape,
-        [
-            pltpu.VMEM((TOTAL * CQ, LAT), F32),
-            pltpu.VMEM((3, TOTAL, LAT), F32),
-            pltpu.VMEM((2, 4 * MEM, LAT), F32),
-        ],
-        20_000_000,
-        800_000,
-        qk,
+        [pltpu.VMEM((2, 4 * MEM, LAT), F32)],
+        20_000,
+        100_000,
+        gram,
         v0,
         alias={1: 0},
     )
     v0 = lax.all_to_all(v0, mem, 0, 0, tiled=True)
-    gram = call(total_kernel, jax.ShapeDtypeStruct((4, LAT), F32), [], 40_000, 200_000, v0)
-    gram = lax.all_gather(gram, "core", axis=0, tiled=False)
     copies = jax.ShapeDtypeStruct((LON // 2, 4, LAT), F32)
-    gram = call(spread_kernel, copies, [], 10_000, 40_000, gram)
+    gram = call(spread_kernel, copies, [], 40_000, 200_000, v0)
     gram = lax.all_to_all(gram, lon, 0, 0, tiled=True)
     scale = 1.0 / math.sqrt(CQ * LAT * COLS * LON)
     v1 = call(

time: 99.2 us -> 99.2 us (level)
  no operation moved by 1% of the time
where the time goes in v14:
time: 99.2 us; the launch traced here: 98.8 us
  blocking collectives  85.4 us (86%)
  starting transfers between devices  6.9 us (7%)
  Pallas kernels  4.47 us (5%)
  local copies, waits for them, and re-layouts  1.1 us (1%)
    all_to_all x1, blocking collectives, shards(): qk = lax.all_to_all(qk, mem, 0, 0, tiled=True)  26.6 us
    all_to_all x1, blocking collectives, shards(): gram = lax.all_to_all(gram, lon, 0, 0, tiled=True)  15.8 us
    all_to_all x1, blocking collectives, shards(): v0 = lax.all_to_all(v0, mem, 0, 0, tiled=True)  13.8 us
    all_to_all x1, blocking collectives, shards(): mixed = lax.all_to_all(mixed, ('z', 'ylo'), 0, 0, tiled=True)  13.4 us
    all_to_all x1, blocking collectives, shards(): v1 = lax.all_to_all(v1, mem, 0, 0, tiled=True)  11.9 us
    ppermute x1, starting transfers between devices, shards(): got_nb = lax.ppermute(nb, ('yhi', 'x', 'core'), swaps)  6.9 us
    pallas_call x9, Pallas kernels, call(): pl.pallas_call(body, out_shape=outs, in_specs=[VMEM] * len(args), out_spe...  4.47 us
    all_gather x1, blocking collectives, shards(): got_sib = lax.all_gather(sib, 'core', axis=0, tiled=False)  2.04 us
  transfers between devices with their start and end apart: 1, of which 1 were waited for; matrix products, arithmetic and copies ran while one was open for 0% of the time, Pallas kernels for 1%

profile of v14, /device:TPU:8, one launch (start us, length us, event | category | flops | bytes accessed | tf_op | source)
XLA Modules:
  0.0 98.8 jit_solution(4721554995307827428)
XLA Ops:
  0.0 0.0 copy-start
  0.0 1.1 %copy-done = bf16[5,64,8,128]{3,2,1,0:T(8,128)(2,1)S(1)} copy-done((bf16[5,64,8,128]{3,2,1,0:T(8,128)(2,1)S(1)}, bf16[5,64,8,128]{3,2,1,0:T(8,128)(2,1)}, u32[]{:S(2)}) %copy-start) | copy-done | bytes 655384
  1.1 0.0 copy-start.1
  1.1 0.0 copy-start.2
  1.1 0.2 shard_map.56
  1.3 6.9 %collective-permute-start = (bf16[5,128,128]{2,1,0:T(8,128)(2,1)S(1)}, bf16[5,128,128]{2,1,0:T(8,128)(2,1)S(1)}, u32[]{:S(2)}, u32[]{:S(2)}) collective-permute-start(bf16[5,128,128]{2,1,0:T(8,128)(2,1)S(1)} %get-tuple-element.23.nb_ref), channel_id=1, source_target_pairs={{0,31},{1,2},{2,1},{3,4},{4,3},{5,6},{6,5},{7,8},{8,7},{9,10},{10,... | collective-permute-start | bytes 491528 | tf_op jit(solution)/shard_map/ppermute | solution.py:273
  8.2 0.0 copy-done.1
  8.2 0.0 copy-done.2
  8.2 0.0 copy-done.3
  8.2 0.0 copy-done.4
  8.2 1.1 %shard_map.55 = (bf16[16,5,24,128]{3,2,1,0:T(8,128)(2,1)S(1)}, bf16[16,48,128]{2,1,0:T(8,128)(2,1)S(1)}, bf16[16,5,8,128]{3,2,1,0:T(8,128)(2,1)S(1)}, f32[5,32,1...) custom-call(bf16[5,64,8,128]{3,2,1,0:T(8,128)(2,1)S(1)} %copy-done, ...), custom_call_target="tpu_custom_call" | custom-call | flops 450000000 | bytes 2000000 | tf_op jit(solution)/shard_map/pallas_call | solution.py:33
  9.4 2.0 %all-gather = bf16[10,128,128]{2,1,0:T(8,128)(2,1)S(1)} all-gather(bf16[5,128,128]{2,1,0:T(8,128)(2,1)S(1)} %get-tuple-element.22.sib_ref), channel_id=2, replica_groups=mesh['z'=8,'ylo'=2,'yhi'=4,'x'=4,'core'=2] {'core'}, dimensions={0}, use_global_device_ids=true | all-gather | bytes 491520 | tf_op jit(solution)/shard_map/all_gather | solution.py:274
  11.4 0.8 collective-permute-done.gn_ref
  12.2 0.6 shard_map.57
  12.9 26.6 %all_to_all.25.x_ref = bf16[16,5,24,128]{3,2,1,0:T(8,128)(2,1)S(1)} all-to-all(bf16[16,5,24,128]{3,2,1,0:T(8,128)(2,1)S(1)} %get-tuple-element.24), channel_id=1, replica_groups=mesh['z'=8,'ylo'=2,'yhi'=4,'x'=4,'core'=2] {'z','ylo'}, dimensions={0} | all-to-all | bytes 983040 | tf_op jit(solution)/shard_map/all_to_all | solution.py:317
  39.5 0.4 shard_map.58
  39.9 1.9 %all-gather.1 = f32[128,128]{1,0:T(8,128)S(1)} all-gather(f32[64,128]{1,0:T(8,128)S(1)} %shard_map.58), channel_id=3, replica_groups=mesh['z'=8,'ylo'=2,'yhi'=4,'x'=4,'core'=2] {'core'}, dimensions={0}, use_global_device_ids=true | all-gather | bytes 98304 | tf_op jit(solution)/shard_map/all_gather | solution.py:326
  41.7 13.8 %all_to_all.26.x_ref.v0_ref = bf16[16,48,128]{2,1,0:T(8,128)(2,1)S(1)} all-to-all(bf16[16,48,128]{2,1,0:T(8,128)(2,1)S(1)} %shard_map.59), channel_id=1, replica_groups=mesh['z'=8,'ylo'=2,'yhi'=4,'x'=4,'core'=2] {'z','ylo'}, dimensions={0} | all-to-all | bytes 393216 | tf_op jit(solution)/shard_map/all_to_all | solution.py:337
  55.6 15.8 %all_to_all.27.x_ref = f32[16,4,128]{2,1,0:T(4,128)S(1)} all-to-all(f32[16,4,128]{2,1,0:T(4,128)S(1)} %shard_map.60), channel_id=1, replica_groups=mesh['z'=8,'ylo'=2,'yhi'=4,'x'=4,'core'=2] {'yhi','x'}, dimensions={0} | all-to-all | bytes 65536 | tf_op jit(solution)/shard_map/all_to_all | solution.py:340
  71.4 0.3 shard_map.61
  71.7 11.9 %all_to_all.28.v1_ref = bf16[16,5,8,128]{3,2,1,0:T(8,128)(2,1)S(1)} all-to-all(bf16[16,5,8,128]{3,2,1,0:T(8,128)(2,1)S(1)} %shard_map.61), channel_id=1, replica_groups=mesh['z'=8,'ylo'=2,'yhi'=4,'x'=4,'core'=2] {'z','ylo'}, dimensions={0} | all-to-all | bytes 327680 | tf_op jit(solution)/shard_map/all_to_all | solution.py:352
  83.6 0.4 shard_map.62
  84.0 13.4 %all_to_all.29.x_ref = bf16[16,5,16,128]{3,2,1,0:T(8,128)(2,1)S(1)} all-to-all(bf16[16,5,16,128]{3,2,1,0:T(8,128)(2,1)S(1)} %shard_map.62), channel_id=1, replica_groups=mesh['z'=8,'ylo'=2,'yhi'=4,'x'=4,'core'=2] {'z','ylo'}, dimensions={0} | all-to-all | bytes 655360 | tf_op jit(solution)/shard_map/all_to_all | solution.py:362
  97.4 1.4 %shard_map.63 = bf16[5,64,8,128]{3,2,1,0:T(8,128)(2,1)} custom-call(bf16[16,5,16,128]{3,2,1,0:T(8,128)(2,1)S(1)} %all_to_all.29.x_ref, bf16[5,512,128]{2,1,0:T(8,128)(2,1)S(1)} %get-tuple-element.27.xt_ref, bf16[128,416]{1,0:T(8,128)(2,1)S(1)} %get-tuple-element.28.w_ref), custom_call_target="tpu_custom_call" | custom-call | flops 150000000 | bytes 1700000 | tf_op jit(solution)/shard_map/pallas_call | solution.py:33
  (4 shorter events, 0.1 us)
Async XLA Ops:
  0.0 1.1 %copy-start = (bf16[5,64,8,128]{3,2,1,0:T(8,128)(2,1)S(1)}, bf16[5,64,8,128]{3,2,1,0:T(8,128)(2,1)}, u32[]{:S(2)}) copy-start(bf16[5,64,8,128]{3,2,1,0:T(8,128)(2,1)} %f_ref.3) | copy-start | bytes 1966084
  1.1 7.1 %copy-start.1 = (bf16[64,216]{1,0:T(8,128)(2,1)S(1)}, bf16[64,216]{1,0:T(8,128)(2,1)}, u32[]{:S(2)}) copy-start(bf16[64,216]{1,0:T(8,128)(2,1)} %wo_ref.1) | copy-start | bytes 82948
  1.1 7.1 %copy-start.2 = (bf16[24,576]{1,0:T(8,128)(2,1)S(1)}, bf16[24,576]{1,0:T(8,128)(2,1)}, u32[]{:S(2)}) copy-start(bf16[24,576]{1,0:T(8,128)(2,1)} %wq_ref.1) | copy-start | bytes 82948
  1.1 7.1 %copy-start.3 = (bf16[24,576]{1,0:T(8,128)(2,1)S(1)}, bf16[24,576]{1,0:T(8,128)(2,1)}, u32[]{:S(2)}) copy-start(bf16[24,576]{1,0:T(8,128)(2,1)} %wk_ref.1) | copy-start | bytes 82948
  1.1 7.1 %copy-start.4 = (bf16[24,576]{1,0:T(8,128)(2,1)S(1)}, bf16[24,576]{1,0:T(8,128)(2,1)}, u32[]{:S(2)}) copy-start(bf16[24,576]{1,0:T(8,128)(2,1)} %wv_ref.1) | copy-start | bytes 82948
  1.3 11.0 %collective-permute-start = (bf16[5,128,128]{2,1,0:T(8,128)(2,1)S(1)}, bf16[5,128,128]{2,1,0:T(8,128)(2,1)S(1)}, u32[]{:S(2)}, u32[]{:S(2)}) collective-permute-start(bf16[5,128,128]{2,1,0:T(8,128)(2,1)S(1)} %get-tuple-element.23.nb_ref), channel_id=1, source_target_pairs={{0,31},{1,2},{2,1},{3,4},{4,3},{5,6},{6,5},{7,8},{8,7},{9,10},{10,... | collective-permute-start | bytes 491528 | tf_op jit(solution)/shard_map/ppermute | solution.py:273

commit v15 on v12

--- a/solution.py
+++ b/solution.py
@@ -222,10 +222,10 @@
     s = jnp.where(lane < TOTAL, gs[...] * scale, -jnp.inf)
     e = jnp.exp(s - jnp.max(s, axis=1, keepdims=True))
     w = e / jnp.sum(e, axis=1, keepdims=True)
-    row = lax.broadcasted_iota(jnp.int32, (MEM, 8, LAT), 1)
-    for m in range(OWN):
-        block = v1_ref[:, m].astype(F32)
-        o_ref[:, m] = jnp.where(row == USED - 8, w[m : m + 1][None], block).astype(BF16)
+    for m in range(OWN):
+        o_ref[:, m, USED - 8 : USED - 7, :] = jnp.broadcast_to(
+            w[m : m + 1].astype(BF16)[None], (MEM, 1, LAT)
+        )
 
 
 def mix_kernel(v0_ref, v1_ref, o_ref, vs, ms):

time: 99.2 us -> 99.2 us (level)
  no operation moved by 1% of the time
where the time goes in v15:
time: 99.2 us; the launch traced here: 98.8 us
  blocking collectives  85.4 us (86%)
  starting transfers between devices  6.9 us (7%)
  Pallas kernels  4.46 us (4%)
  local copies, waits for them, and re-layouts  1.1 us (1%)
    all_to_all x1, blocking collectives, shards(): qk = lax.all_to_all(qk, mem, 0, 0, tiled=True)  26.6 us
    all_to_all x1, blocking collectives, shards(): gram = lax.all_to_all(gram, lon, 0, 0, tiled=True)  16 us
    all_to_all x1, blocking collectives, shards(): v0 = lax.all_to_all(v0, mem, 0, 0, tiled=True)  13.6 us
    all_to_all x1, blocking collectives, shards(): mixed = lax.all_to_all(mixed, ('z', 'ylo'), 0, 0, tiled=True)  13.5 us
    all_to_all x1, blocking collectives, shards(): v1 = lax.all_to_all(v1, mem, 0, 0, tiled=True)  11.9 us
    ppermute x1, starting transfers between devices, shards(): got_nb = lax.ppermute(nb, ('yhi', 'x', 'core'), swaps)  6.9 us
    pallas_call x9, Pallas kernels, call(): pl.pallas_call(body, out_shape=outs, in_specs=[VMEM] * len(args), out_spe...  4.46 us
    all_gather x1, blocking collectives, shards(): got_sib = lax.all_gather(sib, 'core', axis=0, tiled=False)  2.04 us
  transfers between devices with their start and end apart: 1, of which 1 were waited for; matrix products, arithmetic and copies ran while one was open for 0% of the time, Pallas kernels for 1%

profile of v15, /device:TPU:8, one launch (start us, length us, event | category | flops | bytes accessed | tf_op | source)
XLA Modules:
  0.0 98.8 jit_solution(18005039248333826479)
XLA Ops:
  0.0 0.0 copy-start
  0.0 1.1 %copy-done = bf16[5,64,8,128]{3,2,1,0:T(8,128)(2,1)S(1)} copy-done((bf16[5,64,8,128]{3,2,1,0:T(8,128)(2,1)S(1)}, bf16[5,64,8,128]{3,2,1,0:T(8,128)(2,1)}, u32[]{:S(2)}) %copy-start) | copy-done | bytes 655384
  1.1 0.0 copy-start.1
  1.1 0.0 copy-start.2
  1.1 0.2 shard_map.56
  1.3 6.9 %collective-permute-start = (bf16[5,128,128]{2,1,0:T(8,128)(2,1)S(1)}, bf16[5,128,128]{2,1,0:T(8,128)(2,1)S(1)}, u32[]{:S(2)}, u32[]{:S(2)}) collective-permute-start(bf16[5,128,128]{2,1,0:T(8,128)(2,1)S(1)} %get-tuple-element.23.nb_ref), channel_id=1, source_target_pairs={{0,31},{1,2},{2,1},{3,4},{4,3},{5,6},{6,5},{7,8},{8,7},{9,10},{10,... | collective-permute-start | bytes 491528 | tf_op jit(solution)/shard_map/ppermute | solution.py:274
  8.2 0.0 copy-done.1
  8.2 0.0 copy-done.2
  8.2 0.0 copy-done.3
  8.2 0.0 copy-done.4
  8.2 1.1 %shard_map.55 = (bf16[16,5,24,128]{3,2,1,0:T(8,128)(2,1)S(1)}, bf16[16,48,128]{2,1,0:T(8,128)(2,1)S(1)}, bf16[16,5,8,128]{3,2,1,0:T(8,128)(2,1)S(1)}, f32[5,32,1...) custom-call(bf16[5,64,8,128]{3,2,1,0:T(8,128)(2,1)S(1)} %copy-done, ...), custom_call_target="tpu_custom_call" | custom-call | flops 450000000 | bytes 2000000 | tf_op jit(solution)/shard_map/pallas_call | solution.py:33
  9.4 2.0 %all-gather = bf16[10,128,128]{2,1,0:T(8,128)(2,1)S(1)} all-gather(bf16[5,128,128]{2,1,0:T(8,128)(2,1)S(1)} %get-tuple-element.22.sib_ref), channel_id=2, replica_groups=mesh['z'=8,'ylo'=2,'yhi'=4,'x'=4,'core'=2] {'core'}, dimensions={0}, use_global_device_ids=true | all-gather | bytes 491520 | tf_op jit(solution)/shard_map/all_gather | solution.py:275
  11.4 0.8 collective-permute-done.gn_ref
  12.2 0.6 shard_map.57
  12.9 26.6 %all_to_all.25.x_ref = bf16[16,5,24,128]{3,2,1,0:T(8,128)(2,1)S(1)} all-to-all(bf16[16,5,24,128]{3,2,1,0:T(8,128)(2,1)S(1)} %get-tuple-element.24), channel_id=1, replica_groups=mesh['z'=8,'ylo'=2,'yhi'=4,'x'=4,'core'=2] {'z','ylo'}, dimensions={0} | all-to-all | bytes 983040 | tf_op jit(solution)/shard_map/all_to_all | solution.py:318
  39.5 0.4 shard_map.58
  39.9 13.6 %all_to_all.26.x_ref.v0_ref = bf16[16,48,128]{2,1,0:T(8,128)(2,1)S(1)} all-to-all(bf16[16,48,128]{2,1,0:T(8,128)(2,1)S(1)} %shard_map.58), channel_id=1, replica_groups=mesh['z'=8,'ylo'=2,'yhi'=4,'x'=4,'core'=2] {'z','ylo'}, dimensions={0} | all-to-all | bytes 393216 | tf_op jit(solution)/shard_map/all_to_all | solution.py:333
  53.5 1.8 %all-gather.2.x_ref = f32[2,4,128]{2,1,0:T(4,128)S(1)} all-gather(f32[1,4,128]{2,1,0:T(4,128)S(1)} %bitcast.3), channel_id=3, replica_groups=mesh['z'=8,'ylo'=2,'yhi'=4,'x'=4,'core'=2] {'core'}, dimensions={0}, use_global_device_ids=true | all-gather | bytes 6144 | tf_op jit(solution)/shard_map/all_gather | solution.py:335
  55.3 16.0 %all_to_all.27.x_ref = f32[16,4,128]{2,1,0:T(4,128)S(1)} all-to-all(f32[16,4,128]{2,1,0:T(4,128)S(1)} %shard_map.60), channel_id=1, replica_groups=mesh['z'=8,'ylo'=2,'yhi'=4,'x'=4,'core'=2] {'yhi','x'}, dimensions={0} | all-to-all | bytes 65536 | tf_op jit(solution)/shard_map/all_to_all | solution.py:338
  71.3 0.3 shard_map.61
  71.6 11.9 %all_to_all.28.v1_ref = bf16[16,5,8,128]{3,2,1,0:T(8,128)(2,1)S(1)} all-to-all(bf16[16,5,8,128]{3,2,1,0:T(8,128)(2,1)S(1)} %shard_map.61), channel_id=1, replica_groups=mesh['z'=8,'ylo'=2,'yhi'=4,'x'=4,'core'=2] {'z','ylo'}, dimensions={0} | all-to-all | bytes 327680 | tf_op jit(solution)/shard_map/all_to_all | solution.py:350
  83.5 0.4 shard_map.62
  83.9 13.5 %all_to_all.29.x_ref = bf16[16,5,16,128]{3,2,1,0:T(8,128)(2,1)S(1)} all-to-all(bf16[16,5,16,128]{3,2,1,0:T(8,128)(2,1)S(1)} %shard_map.62), channel_id=1, replica_groups=mesh['z'=8,'ylo'=2,'yhi'=4,'x'=4,'core'=2] {'z','ylo'}, dimensions={0} | all-to-all | bytes 655360 | tf_op jit(solution)/shard_map/all_to_all | solution.py:360
  97.4 1.4 %shard_map.63 = bf16[5,64,8,128]{3,2,1,0:T(8,128)(2,1)} custom-call(bf16[16,5,16,128]{3,2,1,0:T(8,128)(2,1)S(1)} %all_to_all.29.x_ref, bf16[5,512,128]{2,1,0:T(8,128)(2,1)S(1)} %get-tuple-element.27.xt_ref, bf16[128,416]{1,0:T(8,128)(2,1)S(1)} %get-tuple-element.28.w_ref), custom_call_target="tpu_custom_call" | custom-call | flops 150000000 | bytes 1700000 | tf_op jit(solution)/shard_map/pallas_call | solution.py:33
  (4 shorter events, 0.0 us)
Async XLA Ops:
  0.0 1.1 %copy-start = (bf16[5,64,8,128]{3,2,1,0:T(8,128)(2,1)S(1)}, bf16[5,64,8,128]{3,2,1,0:T(8,128)(2,1)}, u32[]{:S(2)}) copy-start(bf16[5,64,8,128]{3,2,1,0:T(8,128)(2,1)} %f_ref.3) | copy-start | bytes 1966084
  1.1 7.1 %copy-start.1 = (bf16[64,216]{1,0:T(8,128)(2,1)S(1)}, bf16[64,216]{1,0:T(8,128)(2,1)}, u32[]{:S(2)}) copy-start(bf16[64,216]{1,0:T(8,128)(2,1)} %wo_ref.1) | copy-start | bytes 82948
  1.1 7.1 %copy-start.2 = (bf16[24,576]{1,0:T(8,128)(2,1)S(1)}, bf16[24,576]{1,0:T(8,128)(2,1)}, u32[]{:S(2)}) copy-start(bf16[24,576]{1,0:T(8,128)(2,1)} %wq_ref.1) | copy-start | bytes 82948
  1.1 7.1 %copy-start.3 = (bf16[24,576]{1,0:T(8,128)(2,1)S(1)}, bf16[24,576]{1,0:T(8,128)(2,1)}, u32[]{:S(2)}) copy-start(bf16[24,576]{1,0:T(8,128)(2,1)} %wk_ref.1) | copy-start | bytes 82948
  1.1 7.1 %copy-start.4 = (bf16[24,576]{1,0:T(8,128)(2,1)S(1)}, bf16[24,576]{1,0:T(8,128)(2,1)}, u32[]{:S(2)}) copy-start(bf16[24,576]{1,0:T(8,128)(2,1)} %wv_ref.1) | copy-start | bytes 82948
  1.3 11.0 %collective-permute-start = (bf16[5,128,128]{2,1,0:T(8,128)(2,1)S(1)}, bf16[5,128,128]{2,1,0:T(8,128)(2,1)S(1)}, u32[]{:S(2)}, u32[]{:S(2)}) collective-permute-start(bf16[5,128,128]{2,1,0:T(8,128)(2,1)S(1)} %get-tuple-element.23.nb_ref), channel_id=1, source_target_pairs={{0,31},{1,2},{2,1},{3,4},{4,3},{5,6},{6,5},{7,8},{8,7},{9,10},{10,... | collective-permute-start | bytes 491528 | tf_op jit(solution)/shard_map/ppermute | solution.py:274

commit v16 on v15

--- a/solution.py
+++ b/solution.py
@@ -19,6 +19,7 @@
 EXT = COLS + 2
 ROWS = 16
 USED = EXT * CQ // MEM
+EARLY = 3
 HEAD = 8
 F32, BF16 = jnp.float32, jnp.bfloat16
 VMEM = pl.BlockSpec(memory_space=pltpu.VMEM)
@@ -80,8 +81,12 @@
 
 
 def put_block(v0_ref, v1_ref, j, m, block):
-    v0_ref[j, HEAD + m * 8 : HEAD + m * 8 + 8] = block[:8].astype(BF16)
-    v1_ref[j, m] = block[8:].astype(BF16)
+    low = block[:8].astype(BF16)
+    if m < EARLY:
+        v0_ref[j, HEAD + m * 8 : HEAD + m * 8 + 8] = low
+    else:
+        v1_ref[j, (OWN + m - EARLY) * 8 : (OWN + m - EARLY + 1) * 8] = low
+    v1_ref[j, m * 8 : m * 8 + 8] = block[8:].astype(BF16)
 
 
 def put_pair(qk_ref, vs, m, p, outs):
@@ -223,14 +228,16 @@
     e = jnp.exp(s - jnp.max(s, axis=1, keepdims=True))
     w = e / jnp.sum(e, axis=1, keepdims=True)
     for m in range(OWN):
-        o_ref[:, m, USED - 8 : USED - 7, :] = jnp.broadcast_to(
+        row = m * 8 + USED - 8
+        o_ref[:, row : row + 1, :] = jnp.broadcast_to(
             w[m : m + 1].astype(BF16)[None], (MEM, 1, LAT)
         )
 
 
 def mix_kernel(v0_ref, v1_ref, o_ref, vs, ms):
-    vs[0] = v0_ref[:, HEAD:].astype(F32).reshape(TOTAL * 8, LAT)
-    vs[1] = v1_ref[...].astype(F32).reshape(TOTAL * 8, LAT)
+    low = [v0_ref[:, HEAD:].astype(F32), v1_ref[:, OWN * 8 :].astype(F32)]
+    vs[0] = jnp.concatenate(low, axis=1).reshape(TOTAL * 8, LAT)
+    vs[1] = v1_ref[:, : OWN * 8].astype(F32).reshape(TOTAL * 8, LAT)
     rows = [vs[r // 8, pl.ds(r % 8, TOTAL, stride=8), :].astype(BF16) for r in range(ROWS)]
     w = rows[USED][:, :TOTAL]
     v = jnp.concatenate(rows[:USED], axis=1)
@@ -274,8 +281,8 @@
     got_nb = lax.ppermute(nb, ("yhi", "x", "core"), swaps)
     got_sib = lax.all_gather(sib, "core", axis=0, tiled=False)
     qk_shape = jax.ShapeDtypeStruct((MEM, OWN, CQ, LAT), BF16)
-    v0_shape = jax.ShapeDtypeStruct((MEM, HEAD + OWN * 8, LAT), BF16)
-    v1_shape = jax.ShapeDtypeStruct((MEM, OWN, 8, LAT), BF16)
+    v0_shape = jax.ShapeDtypeStruct((MEM, HEAD + EARLY * 8, LAT), BF16)
+    v1_shape = jax.ShapeDtypeStruct((MEM, (2 * OWN - EARLY) * 8, LAT), BF16)
     ends = jax.ShapeDtypeStruct((OWN, 2 * ROWS, LAT), F32)
     pair = jax.ShapeDtypeStruct((18 * CQ, 4 * CH), BF16)
     pair_out = jax.ShapeDtypeStruct((2 * CH, 12 * CQ + 2 * CH), BF16)

time: 99.2 us -> 100 us (level)
    all_to_all x1, blocking collectives: 13.5 us -> 14.7 us  [shards(): mixed = lax.all_to_all(mixed, ('z', 'ylo'), 0, 0, tiled=True)]
    all_to_all x1, blocking collectives: 11.9 us -> 13.2 us  [shards(): v1 = lax.all_to_all(v1, mem, 0, 0, tiled=True)]
    all_to_all x1, blocking collectives: 13.6 us -> 12.4 us  [shards(): v0 = lax.all_to_all(v0, mem, 0, 0, tiled=True)]
where the time goes in v16:
time: 100 us; the launch traced here: 99.7 us
  blocking collectives  86.3 us (86%)
  starting transfers between devices  6.9 us (7%)
  Pallas kernels  4.46 us (4%)
  local copies, waits for them, and re-layouts  1.1 us (1%)
    all_to_all x1, blocking collectives, shards(): qk = lax.all_to_all(qk, mem, 0, 0, tiled=True)  26.6 us
    all_to_all x1, blocking collectives, shards(): gram = lax.all_to_all(gram, lon, 0, 0, tiled=True)  15.6 us
    all_to_all x1, blocking collectives, shards(): mixed = lax.all_to_all(mixed, ('z', 'ylo'), 0, 0, tiled=True)  14.7 us
    all_to_all x1, blocking collectives, shards(): v1 = lax.all_to_all(v1, mem, 0, 0, tiled=True)  13.2 us
    all_to_all x1, blocking collectives, shards(): v0 = lax.all_to_all(v0, mem, 0, 0, tiled=True)  12.4 us
    ppermute x1, starting transfers between devices, shards(): got_nb = lax.ppermute(nb, ('yhi', 'x', 'core'), swaps)  6.9 us
    pallas_call x9, Pallas kernels, call(): pl.pallas_call(body, out_shape=outs, in_specs=[VMEM] * len(args), out_spe...  4.46 us
    all_gather x1, blocking collectives, shards(): got_sib = lax.all_gather(sib, 'core', axis=0, tiled=False)  2.04 us
  transfers between devices with their start and end apart: 1, of which 1 were waited for; matrix products, arithmetic and copies ran while one was open for 0% of the time, Pallas kernels for 1%

profile of v16, /device:TPU:8, one launch (start us, length us, event | category | flops | bytes accessed | tf_op | source)
XLA Modules:
  0.0 99.7 jit_solution(10739834201686794414)
XLA Ops:
  0.0 0.0 copy-start
  0.0 1.1 %copy-done = bf16[5,64,8,128]{3,2,1,0:T(8,128)(2,1)S(1)} copy-done((bf16[5,64,8,128]{3,2,1,0:T(8,128)(2,1)S(1)}, bf16[5,64,8,128]{3,2,1,0:T(8,128)(2,1)}, u32[]{:S(2)}) %copy-start) | copy-done | bytes 655384
  1.1 0.0 copy-start.1
  1.1 0.0 copy-start.2
  1.1 0.2 shard_map.56
  1.3 6.9 %collective-permute-start = (bf16[5,128,128]{2,1,0:T(8,128)(2,1)S(1)}, bf16[5,128,128]{2,1,0:T(8,128)(2,1)S(1)}, u32[]{:S(2)}, u32[]{:S(2)}) collective-permute-start(bf16[5,128,128]{2,1,0:T(8,128)(2,1)S(1)} %get-tuple-element.23.nb_ref), channel_id=1, source_target_pairs={{0,31},{1,2},{2,1},{3,4},{4,3},{5,6},{6,5},{7,8},{8,7},{9,10},{10,... | collective-permute-start | bytes 491528 | tf_op jit(solution)/shard_map/ppermute | solution.py:281
  8.2 0.0 copy-done.1
  8.2 0.0 copy-done.2
  8.2 0.0 copy-done.3
  8.2 0.0 copy-done.4
  8.2 1.1 %shard_map.55 = (bf16[16,5,24,128]{3,2,1,0:T(8,128)(2,1)S(1)}, bf16[16,32,128]{2,1,0:T(8,128)(2,1)S(1)}, bf16[16,56,128]{2,1,0:T(8,128)(2,1)S(1)}, f32[5,32,128]...) custom-call(bf16[5,64,8,128]{3,2,1,0:T(8,128)(2,1)S(1)} %copy-done, ...), custom_call_target="tpu_custom_call" | custom-call | flops 450000000 | bytes 2000000 | tf_op jit(solution)/shard_map/pallas_call | solution.py:34
  9.4 2.0 %all-gather = bf16[10,128,128]{2,1,0:T(8,128)(2,1)S(1)} all-gather(bf16[5,128,128]{2,1,0:T(8,128)(2,1)S(1)} %get-tuple-element.22.sib_ref), channel_id=2, replica_groups=mesh['z'=8,'ylo'=2,'yhi'=4,'x'=4,'core'=2] {'core'}, dimensions={0}, use_global_device_ids=true | all-gather | bytes 491520 | tf_op jit(solution)/shard_map/all_gather | solution.py:282
  11.4 0.8 collective-permute-done.gn_ref
  12.2 0.6 shard_map.57
  12.9 26.6 %all_to_all.25.x_ref = bf16[16,5,24,128]{3,2,1,0:T(8,128)(2,1)S(1)} all-to-all(bf16[16,5,24,128]{3,2,1,0:T(8,128)(2,1)S(1)} %get-tuple-element.24), channel_id=1, replica_groups=mesh['z'=8,'ylo'=2,'yhi'=4,'x'=4,'core'=2] {'z','ylo'}, dimensions={0} | all-to-all | bytes 983040 | tf_op jit(solution)/shard_map/all_to_all | solution.py:325
  39.5 0.4 shard_map.58
  39.9 12.4 %all_to_all.26.x_ref.v0_ref = bf16[16,32,128]{2,1,0:T(8,128)(2,1)S(1)} all-to-all(bf16[16,32,128]{2,1,0:T(8,128)(2,1)S(1)} %shard_map.58), channel_id=1, replica_groups=mesh['z'=8,'ylo'=2,'yhi'=4,'x'=4,'core'=2] {'z','ylo'}, dimensions={0} | all-to-all | bytes 262144 | tf_op jit(solution)/shard_map/all_to_all | solution.py:340
  52.3 1.8 %all-gather.2.x_ref = f32[2,4,128]{2,1,0:T(4,128)S(1)} all-gather(f32[1,4,128]{2,1,0:T(4,128)S(1)} %bitcast.3), channel_id=3, replica_groups=mesh['z'=8,'ylo'=2,'yhi'=4,'x'=4,'core'=2] {'core'}, dimensions={0}, use_global_device_ids=true | all-gather | bytes 6144 | tf_op jit(solution)/shard_map/all_gather | solution.py:342
  54.1 15.6 %all_to_all.27.x_ref = f32[16,4,128]{2,1,0:T(4,128)S(1)} all-to-all(f32[16,4,128]{2,1,0:T(4,128)S(1)} %shard_map.60), channel_id=1, replica_groups=mesh['z'=8,'ylo'=2,'yhi'=4,'x'=4,'core'=2] {'yhi','x'}, dimensions={0} | all-to-all | bytes 65536 | tf_op jit(solution)/shard_map/all_to_all | solution.py:345
  69.7 0.3 shard_map.61
  70.0 13.2 %all_to_all.28.v1_ref = bf16[16,56,128]{2,1,0:T(8,128)(2,1)S(1)} all-to-all(bf16[16,56,128]{2,1,0:T(8,128)(2,1)S(1)} %shard_map.61), channel_id=1, replica_groups=mesh['z'=8,'ylo'=2,'yhi'=4,'x'=4,'core'=2] {'z','ylo'}, dimensions={0} | all-to-all | bytes 458752 | tf_op jit(solution)/shard_map/all_to_all | solution.py:357
  83.2 0.4 shard_map.62
  83.6 14.7 %all_to_all.29.x_ref = bf16[16,5,16,128]{3,2,1,0:T(8,128)(2,1)S(1)} all-to-all(bf16[16,5,16,128]{3,2,1,0:T(8,128)(2,1)S(1)} %shard_map.62), channel_id=1, replica_groups=mesh['z'=8,'ylo'=2,'yhi'=4,'x'=4,'core'=2] {'z','ylo'}, dimensions={0} | all-to-all | bytes 655360 | tf_op jit(solution)/shard_map/all_to_all | solution.py:367
  98.3 1.4 %shard_map.63 = bf16[5,64,8,128]{3,2,1,0:T(8,128)(2,1)} custom-call(bf16[16,5,16,128]{3,2,1,0:T(8,128)(2,1)S(1)} %all_to_all.29.x_ref, bf16[5,512,128]{2,1,0:T(8,128)(2,1)S(1)} %get-tuple-element.27.xt_ref, bf16[128,416]{1,0:T(8,128)(2,1)S(1)} %get-tuple-element.28.w_ref), custom_call_target="tpu_custom_call" | custom-call | flops 150000000 | bytes 1700000 | tf_op jit(solution)/shard_map/pallas_call | solution.py:34
  (4 shorter events, 0.0 us)
Async XLA Ops:
  0.0 1.1 %copy-start = (bf16[5,64,8,128]{3,2,1,0:T(8,128)(2,1)S(1)}, bf16[5,64,8,128]{3,2,1,0:T(8,128)(2,1)}, u32[]{:S(2)}) copy-start(bf16[5,64,8,128]{3,2,1,0:T(8,128)(2,1)} %f_ref.3) | copy-start | bytes 1966084
  1.1 7.1 %copy-start.1 = (bf16[64,216]{1,0:T(8,128)(2,1)S(1)}, bf16[64,216]{1,0:T(8,128)(2,1)}, u32[]{:S(2)}) copy-start(bf16[64,216]{1,0:T(8,128)(2,1)} %wo_ref.1) | copy-start | bytes 82948
  1.1 7.1 %copy-start.2 = (bf16[24,576]{1,0:T(8,128)(2,1)S(1)}, bf16[24,576]{1,0:T(8,128)(2,1)}, u32[]{:S(2)}) copy-start(bf16[24,576]{1,0:T(8,128)(2,1)} %wq_ref.1) | copy-start | bytes 82948
  1.1 7.1 %copy-start.3 = (bf16[24,576]{1,0:T(8,128)(2,1)S(1)}, bf16[24,576]{1,0:T(8,128)(2,1)}, u32[]{:S(2)}) copy-start(bf16[24,576]{1,0:T(8,128)(2,1)} %wk_ref.1) | copy-start | bytes 82948
  1.1 7.1 %copy-start.4 = (bf16[24,576]{1,0:T(8,128)(2,1)S(1)}, bf16[24,576]{1,0:T(8,128)(2,1)}, u32[]{:S(2)}) copy-start(bf16[24,576]{1,0:T(8,128)(2,1)} %wv_ref.1) | copy-start | bytes 82948
  1.3 11.0 %collective-permute-start = (bf16[5,128,128]{2,1,0:T(8,128)(2,1)S(1)}, bf16[5,128,128]{2,1,0:T(8,128)(2,1)S(1)}, u32[]{:S(2)}, u32[]{:S(2)}) collective-permute-start(bf16[5,128,128]{2,1,0:T(8,128)(2,1)S(1)} %get-tuple-element.23.nb_ref), channel_id=1, source_target_pairs={{0,31},{1,2},{2,1},{3,4},{4,3},{5,6},{6,5},{7,8},{8,7},{9,10},{10,... | collective-permute-start | bytes 491528 | tf_op jit(solution)/shard_map/ppermute | solution.py:281

commit v17 on v15

--- a/solution.py
+++ b/solution.py
@@ -19,6 +19,7 @@
 EXT = COLS + 2
 ROWS = 16
 USED = EXT * CQ // MEM
+LATE = 3
 HEAD = 8
 F32, BF16 = jnp.float32, jnp.bfloat16
 VMEM = pl.BlockSpec(memory_space=pltpu.VMEM)
@@ -81,7 +82,12 @@
 
 def put_block(v0_ref, v1_ref, j, m, block):
     v0_ref[j, HEAD + m * 8 : HEAD + m * 8 + 8] = block[:8].astype(BF16)
-    v1_ref[j, m] = block[8:].astype(BF16)
+    high = block[8:].astype(BF16)
+    if m < LATE:
+        v1_ref[j, m * 8 : m * 8 + 8] = high
+    else:
+        row = HEAD + (OWN + m - LATE) * 8
+        v0_ref[j, row : row + 8] = high
 
 
 def put_pair(qk_ref, vs, m, p, outs):
@@ -222,18 +228,18 @@
     s = jnp.where(lane < TOTAL, gs[...] * scale, -jnp.inf)
     e = jnp.exp(s - jnp.max(s, axis=1, keepdims=True))
     w = e / jnp.sum(e, axis=1, keepdims=True)
-    for m in range(OWN):
-        o_ref[:, m, USED - 8 : USED - 7, :] = jnp.broadcast_to(
-            w[m : m + 1].astype(BF16)[None], (MEM, 1, LAT)
-        )
-
-
-def mix_kernel(v0_ref, v1_ref, o_ref, vs, ms):
-    vs[0] = v0_ref[:, HEAD:].astype(F32).reshape(TOTAL * 8, LAT)
-    vs[1] = v1_ref[...].astype(F32).reshape(TOTAL * 8, LAT)
-    rows = [vs[r // 8, pl.ds(r % 8, TOTAL, stride=8), :].astype(BF16) for r in range(ROWS)]
-    w = rows[USED][:, :TOTAL]
-    v = jnp.concatenate(rows[:USED], axis=1)
+    o_ref[:, LATE * 8 :] = jnp.broadcast_to(w.astype(BF16)[None], (MEM, 8, LAT))
+
+
+def mix_kernel(v0_ref, v1_ref, o_ref, ws, vs, ms):
+    for s in range(MEM):
+        ws[s * OWN : (s + 1) * OWN] = v1_ref[s, LATE * 8 :].astype(F32)[:OWN]
+    w = ws[...].astype(BF16)[:, :TOTAL]
+    vs[0] = v0_ref[:, HEAD : HEAD + OWN * 8].astype(F32).reshape(TOTAL * 8, LAT)
+    high = [v1_ref[:, : LATE * 8].astype(F32), v0_ref[:, HEAD + OWN * 8 :].astype(F32)]
+    vs[1] = jnp.concatenate(high, axis=1).reshape(TOTAL * 8, LAT)
+    rows = [vs[r // 8, pl.ds(r % 8, TOTAL, stride=8), :].astype(BF16) for r in range(USED)]
+    v = jnp.concatenate(rows, axis=1)
     mixed = jnp.dot(w, v, preferred_element_type=F32)
     for r in range(USED):
         ms[pl.ds(r, TOTAL, stride=ROWS), :] = mixed[:, r * LAT : (r + 1) * LAT]
@@ -274,8 +280,8 @@
     got_nb = lax.ppermute(nb, ("yhi", "x", "core"), swaps)
     got_sib = lax.all_gather(sib, "core", axis=0, tiled=False)
     qk_shape = jax.ShapeDtypeStruct((MEM, OWN, CQ, LAT), BF16)
-    v0_shape = jax.ShapeDtypeStruct((MEM, HEAD + OWN * 8, LAT), BF16)
-    v1_shape = jax.ShapeDtypeStruct((MEM, OWN, 8, LAT), BF16)
+    v0_shape = jax.ShapeDtypeStruct((MEM, HEAD + (2 * OWN - LATE) * 8, LAT), BF16)
+    v1_shape = jax.ShapeDtypeStruct((MEM, LATE * 8 + 8, LAT), BF16)
     ends = jax.ShapeDtypeStruct((OWN, 2 * ROWS, LAT), F32)
     pair = jax.ShapeDtypeStruct((18 * CQ, 4 * CH), BF16)
     pair_out = jax.ShapeDtypeStruct((2 * CH, 12 * CQ + 2 * CH), BF16)
@@ -351,7 +357,11 @@
     mixed = call(
         mix_kernel,
         jax.ShapeDtypeStruct((MEM, OWN, ROWS, LAT), BF16),
-        [pltpu.VMEM((2, TOTAL * 8, LAT), F32), pltpu.VMEM((TOTAL * ROWS, LAT), F32)],
+        [
+            pltpu.VMEM((TOTAL, LAT), F32),
+            pltpu.VMEM((2, TOTAL * 8, LAT), F32),
+            pltpu.VMEM((TOTAL * ROWS, LAT), F32),
+        ],
         30_000_000,
         700_000,
         v0,

time: 99.2 us -> 101 us (1.018)
  blocking collectives: 85.4 us -> 86.8 us
where the time goes in v17:
time: 101 us; the launch traced here: 100 us
  blocking collectives  86.8 us (86%)
  starting transfers between devices  6.9 us (7%)
  Pallas kernels  4.45 us (4%)
  local copies, waits for them, and re-layouts  1.1 us (1%)
    all_to_all x1, blocking collectives, shards(): qk = lax.all_to_all(qk, mem, 0, 0, tiled=True)  26.6 us
    all_to_all x1, blocking collectives, shards(): gram = lax.all_to_all(gram, lon, 0, 0, tiled=True)  16 us
    all_to_all x1, blocking collectives, shards(): v0 = lax.all_to_all(v0, mem, 0, 0, tiled=True)  14.4 us
    all_to_all x1, blocking collectives, shards(): mixed = lax.all_to_all(mixed, ('z', 'ylo'), 0, 0, tiled=True)  13.9 us
    all_to_all x1, blocking collectives, shards(): v1 = lax.all_to_all(v1, mem, 0, 0, tiled=True)  12.2 us
    ppermute x1, starting transfers between devices, shards(): got_nb = lax.ppermute(nb, ('yhi', 'x', 'core'), swaps)  6.9 us
    pallas_call x9, Pallas kernels, call(): pl.pallas_call(body, out_shape=outs, in_specs=[VMEM] * len(args), out_spe...  4.45 us
    all_gather x1, blocking collectives, shards(): got_sib = lax.all_gather(sib, 'core', axis=0, tiled=False)  2.04 us
  transfers between devices with their start and end apart: 1, of which 1 were waited for; matrix products, arithmetic and copies ran while one was open for 0% of the time, Pallas kernels for 1%

profile of v17, /device:TPU:8, one launch (start us, length us, event | category | flops | bytes accessed | tf_op | source)
XLA Modules:
  0.0 100.2 jit_solution(7848814457865491749)
XLA Ops:
  0.0 0.0 copy-start
  0.0 1.1 %copy-done = bf16[5,64,8,128]{3,2,1,0:T(8,128)(2,1)S(1)} copy-done((bf16[5,64,8,128]{3,2,1,0:T(8,128)(2,1)S(1)}, bf16[5,64,8,128]{3,2,1,0:T(8,128)(2,1)}, u32[]{:S(2)}) %copy-start) | copy-done | bytes 655384
  1.1 0.0 copy-start.1
  1.1 0.0 copy-start.2
  1.1 0.2 shard_map.56
  1.3 6.9 %collective-permute-start = (bf16[5,128,128]{2,1,0:T(8,128)(2,1)S(1)}, bf16[5,128,128]{2,1,0:T(8,128)(2,1)S(1)}, u32[]{:S(2)}, u32[]{:S(2)}) collective-permute-start(bf16[5,128,128]{2,1,0:T(8,128)(2,1)S(1)} %get-tuple-element.23.nb_ref), channel_id=1, source_target_pairs={{0,31},{1,2},{2,1},{3,4},{4,3},{5,6},{6,5},{7,8},{8,7},{9,10},{10,... | collective-permute-start | bytes 491528 | tf_op jit(solution)/shard_map/ppermute | solution.py:280
  8.2 0.0 copy-done.1
  8.2 0.0 copy-done.2
  8.2 0.0 copy-done.3
  8.2 0.0 copy-done.4
  8.2 1.1 %shard_map.55 = (bf16[16,5,24,128]{3,2,1,0:T(8,128)(2,1)S(1)}, bf16[16,64,128]{2,1,0:T(8,128)(2,1)S(1)}, bf16[16,32,128]{2,1,0:T(8,128)(2,1)S(1)}, f32[5,32,128]...) custom-call(bf16[5,64,8,128]{3,2,1,0:T(8,128)(2,1)S(1)} %copy-done, ...), custom_call_target="tpu_custom_call" | custom-call | flops 450000000 | bytes 2000000 | tf_op jit(solution)/shard_map/pallas_call | solution.py:34
  9.4 2.0 %all-gather = bf16[10,128,128]{2,1,0:T(8,128)(2,1)S(1)} all-gather(bf16[5,128,128]{2,1,0:T(8,128)(2,1)S(1)} %get-tuple-element.22.sib_ref), channel_id=2, replica_groups=mesh['z'=8,'ylo'=2,'yhi'=4,'x'=4,'core'=2] {'core'}, dimensions={0}, use_global_device_ids=true | all-gather | bytes 491520 | tf_op jit(solution)/shard_map/all_gather | solution.py:281
  11.4 0.8 collective-permute-done.gn_ref
  12.2 0.6 shard_map.57
  12.9 26.6 %all_to_all.25.x_ref = bf16[16,5,24,128]{3,2,1,0:T(8,128)(2,1)S(1)} all-to-all(bf16[16,5,24,128]{3,2,1,0:T(8,128)(2,1)S(1)} %get-tuple-element.24), channel_id=1, replica_groups=mesh['z'=8,'ylo'=2,'yhi'=4,'x'=4,'core'=2] {'z','ylo'}, dimensions={0} | all-to-all | bytes 983040 | tf_op jit(solution)/shard_map/all_to_all | solution.py:324
  39.5 0.4 shard_map.58
  39.9 14.4 %all_to_all.26.x_ref.v0_ref = bf16[16,64,128]{2,1,0:T(8,128)(2,1)S(1)} all-to-all(bf16[16,64,128]{2,1,0:T(8,128)(2,1)S(1)} %shard_map.58), channel_id=1, replica_groups=mesh['z'=8,'ylo'=2,'yhi'=4,'x'=4,'core'=2] {'z','ylo'}, dimensions={0} | all-to-all | bytes 524288 | tf_op jit(solution)/shard_map/all_to_all | solution.py:339
  54.3 1.8 %all-gather.2.x_ref = f32[2,4,128]{2,1,0:T(4,128)S(1)} all-gather(f32[1,4,128]{2,1,0:T(4,128)S(1)} %bitcast.3), channel_id=3, replica_groups=mesh['z'=8,'ylo'=2,'yhi'=4,'x'=4,'core'=2] {'core'}, dimensions={0}, use_global_device_ids=true | all-gather | bytes 6144 | tf_op jit(solution)/shard_map/all_gather | solution.py:341
  56.1 16.0 %all_to_all.27.x_ref = f32[16,4,128]{2,1,0:T(4,128)S(1)} all-to-all(f32[16,4,128]{2,1,0:T(4,128)S(1)} %shard_map.60), channel_id=1, replica_groups=mesh['z'=8,'ylo'=2,'yhi'=4,'x'=4,'core'=2] {'yhi','x'}, dimensions={0} | all-to-all | bytes 65536 | tf_op jit(solution)/shard_map/all_to_all | solution.py:344
  72.0 0.3 shard_map.61
  72.3 12.2 %all_to_all.28.v1_ref = bf16[16,32,128]{2,1,0:T(8,128)(2,1)S(1)} all-to-all(bf16[16,32,128]{2,1,0:T(8,128)(2,1)S(1)} %shard_map.61), channel_id=1, replica_groups=mesh['z'=8,'ylo'=2,'yhi'=4,'x'=4,'core'=2] {'z','ylo'}, dimensions={0} | all-to-all | bytes 262144 | tf_op jit(solution)/shard_map/all_to_all | solution.py:356
  84.5 0.4 shard_map.62
  84.9 13.9 %all_to_all.29.x_ref = bf16[16,5,16,128]{3,2,1,0:T(8,128)(2,1)S(1)} all-to-all(bf16[16,5,16,128]{3,2,1,0:T(8,128)(2,1)S(1)} %shard_map.62), channel_id=1, replica_groups=mesh['z'=8,'ylo'=2,'yhi'=4,'x'=4,'core'=2] {'z','ylo'}, dimensions={0} | all-to-all | bytes 655360 | tf_op jit(solution)/shard_map/all_to_all | solution.py:370
  98.8 1.4 %shard_map.63 = bf16[5,64,8,128]{3,2,1,0:T(8,128)(2,1)} custom-call(bf16[16,5,16,128]{3,2,1,0:T(8,128)(2,1)S(1)} %all_to_all.29.x_ref, bf16[5,512,128]{2,1,0:T(8,128)(2,1)S(1)} %get-tuple-element.27.xt_ref, bf16[128,416]{1,0:T(8,128)(2,1)S(1)} %get-tuple-element.28.w_ref), custom_call_target="tpu_custom_call" | custom-call | flops 150000000 | bytes 1700000 | tf_op jit(solution)/shard_map/pallas_call | solution.py:34
  (4 shorter events, 0.0 us)
Async XLA Ops:
  0.0 1.1 %copy-start = (bf16[5,64,8,128]{3,2,1,0:T(8,128)(2,1)S(1)}, bf16[5,64,8,128]{3,2,1,0:T(8,128)(2,1)}, u32[]{:S(2)}) copy-start(bf16[5,64,8,128]{3,2,1,0:T(8,128)(2,1)} %f_ref.3) | copy-start | bytes 1966084
  1.1 7.1 %copy-start.1 = (bf16[64,216]{1,0:T(8,128)(2,1)S(1)}, bf16[64,216]{1,0:T(8,128)(2,1)}, u32[]{:S(2)}) copy-start(bf16[64,216]{1,0:T(8,128)(2,1)} %wo_ref.1) | copy-start | bytes 82948
  1.1 7.1 %copy-start.2 = (bf16[24,576]{1,0:T(8,128)(2,1)S(1)}, bf16[24,576]{1,0:T(8,128)(2,1)}, u32[]{:S(2)}) copy-start(bf16[24,576]{1,0:T(8,128)(2,1)} %wq_ref.1) | copy-start | bytes 82948
  1.1 7.1 %copy-start.3 = (bf16[24,576]{1,0:T(8,128)(2,1)S(1)}, bf16[24,576]{1,0:T(8,128)(2,1)}, u32[]{:S(2)}) copy-start(bf16[24,576]{1,0:T(8,128)(2,1)} %wk_ref.1) | copy-start | bytes 82948
  1.1 7.1 %copy-start.4 = (bf16[24,576]{1,0:T(8,128)(2,1)S(1)}, bf16[24,576]{1,0:T(8,128)(2,1)}, u32[]{:S(2)}) copy-start(bf16[24,576]{1,0:T(8,128)(2,1)} %wv_ref.1) | copy-start | bytes 82948
  1.3 11.0 %collective-permute-start = (bf16[5,128,128]{2,1,0:T(8,128)(2,1)S(1)}, bf16[5,128,128]{2,1,0:T(8,128)(2,1)S(1)}, u32[]{:S(2)}, u32[]{:S(2)}) collective-permute-start(bf16[5,128,128]{2,1,0:T(8,128)(2,1)S(1)} %get-tuple-element.23.nb_ref), channel_id=1, source_target_pairs={{0,31},{1,2},{2,1},{3,4},{4,3},{5,6},{6,5},{7,8},{8,7},{9,10},{10,... | collective-permute-start | bytes 491528 | tf_op jit(solution)/shard_map/ppermute | solution.py:280

commit v18 on v14

--- a/solution.py
+++ b/solution.py
@@ -221,10 +221,10 @@
     s = jnp.where(lane < TOTAL, gs[...] * scale, -jnp.inf)
     e = jnp.exp(s - jnp.max(s, axis=1, keepdims=True))
     w = e / jnp.sum(e, axis=1, keepdims=True)
-    row = lax.broadcasted_iota(jnp.int32, (MEM, 8, LAT), 1)
-    for m in range(OWN):
-        block = v1_ref[:, m].astype(F32)
-        o_ref[:, m] = jnp.where(row == USED - 8, w[m : m + 1][None], block).astype(BF16)
+    for m in range(OWN):
+        o_ref[:, m, USED - 8 : USED - 7, :] = jnp.broadcast_to(
+            w[m : m + 1].astype(BF16)[None], (MEM, 1, LAT)
+        )
 
 
 def mix_kernel(v0_ref, v1_ref, o_ref, vs, ms):

time: 99.2 us -> 99.2 us (level)
  no operation moved by 1% of the time
where the time goes in v18:
time: 99.2 us; the launch traced here: 98.8 us
  blocking collectives  85.4 us (86%)
  starting transfers between devices  6.9 us (7%)
  Pallas kernels  4.46 us (4%)
  local copies, waits for them, and re-layouts  1.1 us (1%)
    all_to_all x1, blocking collectives, shards(): qk = lax.all_to_all(qk, mem, 0, 0, tiled=True)  26.6 us
    all_to_all x1, blocking collectives, shards(): gram = lax.all_to_all(gram, lon, 0, 0, tiled=True)  15.8 us
    all_to_all x1, blocking collectives, shards(): v0 = lax.all_to_all(v0, mem, 0, 0, tiled=True)  13.8 us
    all_to_all x1, blocking collectives, shards(): mixed = lax.all_to_all(mixed, ('z', 'ylo'), 0, 0, tiled=True)  13.4 us
    all_to_all x1, blocking collectives, shards(): v1 = lax.all_to_all(v1, mem, 0, 0, tiled=True)  11.9 us
    ppermute x1, starting transfers between devices, shards(): got_nb = lax.ppermute(nb, ('yhi', 'x', 'core'), swaps)  6.9 us
    pallas_call x9, Pallas kernels, call(): pl.pallas_call(body, out_shape=outs, in_specs=[VMEM] * len(args), out_spe...  4.46 us
    all_gather x1, blocking collectives, shards(): got_sib = lax.all_gather(sib, 'core', axis=0, tiled=False)  2.04 us
  transfers between devices with their start and end apart: 1, of which 1 were waited for; matrix products, arithmetic and copies ran while one was open for 0% of the time, Pallas kernels for 1%

profile of v18, /device:TPU:8, one launch (start us, length us, event | category | flops | bytes accessed | tf_op | source)
XLA Modules:
  0.0 98.8 jit_solution(16268556580720878338)
XLA Ops:
  0.0 0.0 copy-start
  0.0 1.1 %copy-done = bf16[5,64,8,128]{3,2,1,0:T(8,128)(2,1)S(1)} copy-done((bf16[5,64,8,128]{3,2,1,0:T(8,128)(2,1)S(1)}, bf16[5,64,8,128]{3,2,1,0:T(8,128)(2,1)}, u32[]{:S(2)}) %copy-start) | copy-done | bytes 655384
  1.1 0.0 copy-start.1
  1.1 0.0 copy-start.2
  1.1 0.2 shard_map.56
  1.3 6.9 %collective-permute-start = (bf16[5,128,128]{2,1,0:T(8,128)(2,1)S(1)}, bf16[5,128,128]{2,1,0:T(8,128)(2,1)S(1)}, u32[]{:S(2)}, u32[]{:S(2)}) collective-permute-start(bf16[5,128,128]{2,1,0:T(8,128)(2,1)S(1)} %get-tuple-element.23.nb_ref), channel_id=1, source_target_pairs={{0,31},{1,2},{2,1},{3,4},{4,3},{5,6},{6,5},{7,8},{8,7},{9,10},{10,... | collective-permute-start | bytes 491528 | tf_op jit(solution)/shard_map/ppermute | solution.py:273
  8.2 0.0 copy-done.1
  8.2 0.0 copy-done.2
  8.2 0.0 copy-done.3
  8.2 0.0 copy-done.4
  8.2 1.1 %shard_map.55 = (bf16[16,5,24,128]{3,2,1,0:T(8,128)(2,1)S(1)}, bf16[16,48,128]{2,1,0:T(8,128)(2,1)S(1)}, bf16[16,5,8,128]{3,2,1,0:T(8,128)(2,1)S(1)}, f32[5,32,1...) custom-call(bf16[5,64,8,128]{3,2,1,0:T(8,128)(2,1)S(1)} %copy-done, ...), custom_call_target="tpu_custom_call" | custom-call | flops 450000000 | bytes 2000000 | tf_op jit(solution)/shard_map/pallas_call | solution.py:33
  9.4 2.0 %all-gather = bf16[10,128,128]{2,1,0:T(8,128)(2,1)S(1)} all-gather(bf16[5,128,128]{2,1,0:T(8,128)(2,1)S(1)} %get-tuple-element.22.sib_ref), channel_id=2, replica_groups=mesh['z'=8,'ylo'=2,'yhi'=4,'x'=4,'core'=2] {'core'}, dimensions={0}, use_global_device_ids=true | all-gather | bytes 491520 | tf_op jit(solution)/shard_map/all_gather | solution.py:274
  11.4 0.8 collective-permute-done.gn_ref
  12.2 0.6 shard_map.57
  12.9 26.6 %all_to_all.25.x_ref = bf16[16,5,24,128]{3,2,1,0:T(8,128)(2,1)S(1)} all-to-all(bf16[16,5,24,128]{3,2,1,0:T(8,128)(2,1)S(1)} %get-tuple-element.24), channel_id=1, replica_groups=mesh['z'=8,'ylo'=2,'yhi'=4,'x'=4,'core'=2] {'z','ylo'}, dimensions={0} | all-to-all | bytes 983040 | tf_op jit(solution)/shard_map/all_to_all | solution.py:317
  39.5 0.4 shard_map.58
  39.9 1.9 %all-gather.1 = f32[128,128]{1,0:T(8,128)S(1)} all-gather(f32[64,128]{1,0:T(8,128)S(1)} %shard_map.58), channel_id=3, replica_groups=mesh['z'=8,'ylo'=2,'yhi'=4,'x'=4,'core'=2] {'core'}, dimensions={0}, use_global_device_ids=true | all-gather | bytes 98304 | tf_op jit(solution)/shard_map/all_gather | solution.py:326
  41.7 13.8 %all_to_all.26.x_ref.v0_ref = bf16[16,48,128]{2,1,0:T(8,128)(2,1)S(1)} all-to-all(bf16[16,48,128]{2,1,0:T(8,128)(2,1)S(1)} %shard_map.59), channel_id=1, replica_groups=mesh['z'=8,'ylo'=2,'yhi'=4,'x'=4,'core'=2] {'z','ylo'}, dimensions={0} | all-to-all | bytes 393216 | tf_op jit(solution)/shard_map/all_to_all | solution.py:337
  55.6 15.8 %all_to_all.27.x_ref = f32[16,4,128]{2,1,0:T(4,128)S(1)} all-to-all(f32[16,4,128]{2,1,0:T(4,128)S(1)} %shard_map.60), channel_id=1, replica_groups=mesh['z'=8,'ylo'=2,'yhi'=4,'x'=4,'core'=2] {'yhi','x'}, dimensions={0} | all-to-all | bytes 65536 | tf_op jit(solution)/shard_map/all_to_all | solution.py:340
  71.4 0.3 shard_map.61
  71.7 11.9 %all_to_all.28.v1_ref = bf16[16,5,8,128]{3,2,1,0:T(8,128)(2,1)S(1)} all-to-all(bf16[16,5,8,128]{3,2,1,0:T(8,128)(2,1)S(1)} %shard_map.61), channel_id=1, replica_groups=mesh['z'=8,'ylo'=2,'yhi'=4,'x'=4,'core'=2] {'z','ylo'}, dimensions={0} | all-to-all | bytes 327680 | tf_op jit(solution)/shard_map/all_to_all | solution.py:352
  83.6 0.4 shard_map.62
  84.0 13.4 %all_to_all.29.x_ref = bf16[16,5,16,128]{3,2,1,0:T(8,128)(2,1)S(1)} all-to-all(bf16[16,5,16,128]{3,2,1,0:T(8,128)(2,1)S(1)} %shard_map.62), channel_id=1, replica_groups=mesh['z'=8,'ylo'=2,'yhi'=4,'x'=4,'core'=2] {'z','ylo'}, dimensions={0} | all-to-all | bytes 655360 | tf_op jit(solution)/shard_map/all_to_all | solution.py:362
  97.4 1.4 %shard_map.63 = bf16[5,64,8,128]{3,2,1,0:T(8,128)(2,1)} custom-call(bf16[16,5,16,128]{3,2,1,0:T(8,128)(2,1)S(1)} %all_to_all.29.x_ref, bf16[5,512,128]{2,1,0:T(8,128)(2,1)S(1)} %get-tuple-element.27.xt_ref, bf16[128,416]{1,0:T(8,128)(2,1)S(1)} %get-tuple-element.28.w_ref), custom_call_target="tpu_custom_call" | custom-call | flops 150000000 | bytes 1700000 | tf_op jit(solution)/shard_map/pallas_call | solution.py:33
  (4 shorter events, 0.1 us)
Async XLA Ops:
  0.0 1.1 %copy-start = (bf16[5,64,8,128]{3,2,1,0:T(8,128)(2,1)S(1)}, bf16[5,64,8,128]{3,2,1,0:T(8,128)(2,1)}, u32[]{:S(2)}) copy-start(bf16[5,64,8,128]{3,2,1,0:T(8,128)(2,1)} %f_ref.3) | copy-start | bytes 1966084
  1.1 7.1 %copy-start.1 = (bf16[64,216]{1,0:T(8,128)(2,1)S(1)}, bf16[64,216]{1,0:T(8,128)(2,1)}, u32[]{:S(2)}) copy-start(bf16[64,216]{1,0:T(8,128)(2,1)} %wo_ref.1) | copy-start | bytes 82948
  1.1 7.1 %copy-start.2 = (bf16[24,576]{1,0:T(8,128)(2,1)S(1)}, bf16[24,576]{1,0:T(8,128)(2,1)}, u32[]{:S(2)}) copy-start(bf16[24,576]{1,0:T(8,128)(2,1)} %wq_ref.1) | copy-start | bytes 82948
  1.1 7.1 %copy-start.3 = (bf16[24,576]{1,0:T(8,128)(2,1)S(1)}, bf16[24,576]{1,0:T(8,128)(2,1)}, u32[]{:S(2)}) copy-start(bf16[24,576]{1,0:T(8,128)(2,1)} %wk_ref.1) | copy-start | bytes 82948
  1.1 7.1 %copy-start.4 = (bf16[24,576]{1,0:T(8,128)(2,1)S(1)}, bf16[24,576]{1,0:T(8,128)(2,1)}, u32[]{:S(2)}) copy-start(bf16[24,576]{1,0:T(8,128)(2,1)} %wv_ref.1) | copy-start | bytes 82948
  1.3 11.0 %collective-permute-start = (bf16[5,128,128]{2,1,0:T(8,128)(2,1)S(1)}, bf16[5,128,128]{2,1,0:T(8,128)(2,1)S(1)}, u32[]{:S(2)}, u32[]{:S(2)}) collective-permute-start(bf16[5,128,128]{2,1,0:T(8,128)(2,1)S(1)} %get-tuple-element.23.nb_ref), channel_id=1, source_target_pairs={{0,31},{1,2},{2,1},{3,4},{4,3},{5,6},{6,5},{7,8},{8,7},{9,10},{10,... | collective-permute-start | bytes 491528 | tf_op jit(solution)/shard_map/ppermute | solution.py:273

commit v19 on v18

--- a/solution.py
+++ b/solution.py
@@ -236,7 +236,6 @@
     mixed = jnp.dot(w, v, preferred_element_type=F32)
     for r in range(USED):
         ms[pl.ds(r, TOTAL, stride=ROWS), :] = mixed[:, r * LAT : (r + 1) * LAT]
-    ms[pl.ds(USED, TOTAL, stride=ROWS), :] = jnp.zeros((TOTAL, LAT), F32)
     o_ref[...] = ms[...].astype(BF16).reshape(o_ref.shape)
 
 

time: 99.2 us -> 99.2 us (level)
  no operation moved by 1% of the time
where the time goes in v19:
time: 99.2 us; the launch traced here: 98.8 us
  blocking collectives  85.4 us (86%)
  starting transfers between devices  6.9 us (7%)
  Pallas kernels  4.44 us (4%)
  local copies, waits for them, and re-layouts  1.1 us (1%)
    all_to_all x1, blocking collectives, shards(): qk = lax.all_to_all(qk, mem, 0, 0, tiled=True)  26.6 us
    all_to_all x1, blocking collectives, shards(): gram = lax.all_to_all(gram, lon, 0, 0, tiled=True)  15.8 us
    all_to_all x1, blocking collectives, shards(): v0 = lax.all_to_all(v0, mem, 0, 0, tiled=True)  13.8 us
    all_to_all x1, blocking collectives, shards(): mixed = lax.all_to_all(mixed, ('z', 'ylo'), 0, 0, tiled=True)  13.4 us
    all_to_all x1, blocking collectives, shards(): v1 = lax.all_to_all(v1, mem, 0, 0, tiled=True)  11.9 us
    ppermute x1, starting transfers between devices, shards(): got_nb = lax.ppermute(nb, ('yhi', 'x', 'core'), swaps)  6.9 us
    pallas_call x9, Pallas kernels, call(): pl.pallas_call(body, out_shape=outs, in_specs=[VMEM] * len(args), out_spe...  4.44 us
    all_gather x1, blocking collectives, shards(): got_sib = lax.all_gather(sib, 'core', axis=0, tiled=False)  2.04 us
  transfers between devices with their start and end apart: 1, of which 1 were waited for; matrix products, arithmetic and copies ran while one was open for 0% of the time, Pallas kernels for 1%

profile of v19, /device:TPU:8, one launch (start us, length us, event | category | flops | bytes accessed | tf_op | source)
XLA Modules:
  0.0 98.8 jit_solution(13344903503106275073)
XLA Ops:
  0.0 0.0 copy-start
  0.0 1.1 %copy-done = bf16[5,64,8,128]{3,2,1,0:T(8,128)(2,1)S(1)} copy-done((bf16[5,64,8,128]{3,2,1,0:T(8,128)(2,1)S(1)}, bf16[5,64,8,128]{3,2,1,0:T(8,128)(2,1)}, u32[]{:S(2)}) %copy-start) | copy-done | bytes 655384
  1.1 0.0 copy-start.1
  1.1 0.0 copy-start.2
  1.1 0.2 shard_map.56
  1.3 6.9 %collective-permute-start = (bf16[5,128,128]{2,1,0:T(8,128)(2,1)S(1)}, bf16[5,128,128]{2,1,0:T(8,128)(2,1)S(1)}, u32[]{:S(2)}, u32[]{:S(2)}) collective-permute-start(bf16[5,128,128]{2,1,0:T(8,128)(2,1)S(1)} %get-tuple-element.23.nb_ref), channel_id=1, source_target_pairs={{0,31},{1,2},{2,1},{3,4},{4,3},{5,6},{6,5},{7,8},{8,7},{9,10},{10,... | collective-permute-start | bytes 491528 | tf_op jit(solution)/shard_map/ppermute | solution.py:272
  8.2 0.0 copy-done.1
  8.2 0.0 copy-done.2
  8.2 0.0 copy-done.3
  8.2 0.0 copy-done.4
  8.2 1.1 %shard_map.55 = (bf16[16,5,24,128]{3,2,1,0:T(8,128)(2,1)S(1)}, bf16[16,48,128]{2,1,0:T(8,128)(2,1)S(1)}, bf16[16,5,8,128]{3,2,1,0:T(8,128)(2,1)S(1)}, f32[5,32,1...) custom-call(bf16[5,64,8,128]{3,2,1,0:T(8,128)(2,1)S(1)} %copy-done, ...), custom_call_target="tpu_custom_call" | custom-call | flops 450000000 | bytes 2000000 | tf_op jit(solution)/shard_map/pallas_call | solution.py:33
  9.4 2.0 %all-gather = bf16[10,128,128]{2,1,0:T(8,128)(2,1)S(1)} all-gather(bf16[5,128,128]{2,1,0:T(8,128)(2,1)S(1)} %get-tuple-element.22.sib_ref), channel_id=2, replica_groups=mesh['z'=8,'ylo'=2,'yhi'=4,'x'=4,'core'=2] {'core'}, dimensions={0}, use_global_device_ids=true | all-gather | bytes 491520 | tf_op jit(solution)/shard_map/all_gather | solution.py:273
  11.4 0.8 collective-permute-done.gn_ref
  12.2 0.6 shard_map.57
  12.9 26.6 %all_to_all.25.x_ref = bf16[16,5,24,128]{3,2,1,0:T(8,128)(2,1)S(1)} all-to-all(bf16[16,5,24,128]{3,2,1,0:T(8,128)(2,1)S(1)} %get-tuple-element.24), channel_id=1, replica_groups=mesh['z'=8,'ylo'=2,'yhi'=4,'x'=4,'core'=2] {'z','ylo'}, dimensions={0} | all-to-all | bytes 983040 | tf_op jit(solution)/shard_map/all_to_all | solution.py:316
  39.5 0.4 shard_map.58
  39.9 1.9 %all-gather.1 = f32[128,128]{1,0:T(8,128)S(1)} all-gather(f32[64,128]{1,0:T(8,128)S(1)} %shard_map.58), channel_id=3, replica_groups=mesh['z'=8,'ylo'=2,'yhi'=4,'x'=4,'core'=2] {'core'}, dimensions={0}, use_global_device_ids=true | all-gather | bytes 98304 | tf_op jit(solution)/shard_map/all_gather | solution.py:325
  41.7 13.8 %all_to_all.26.x_ref.v0_ref = bf16[16,48,128]{2,1,0:T(8,128)(2,1)S(1)} all-to-all(bf16[16,48,128]{2,1,0:T(8,128)(2,1)S(1)} %shard_map.59), channel_id=1, replica_groups=mesh['z'=8,'ylo'=2,'yhi'=4,'x'=4,'core'=2] {'z','ylo'}, dimensions={0} | all-to-all | bytes 393216 | tf_op jit(solution)/shard_map/all_to_all | solution.py:336
  55.6 15.8 %all_to_all.27.x_ref = f32[16,4,128]{2,1,0:T(4,128)S(1)} all-to-all(f32[16,4,128]{2,1,0:T(4,128)S(1)} %shard_map.60), channel_id=1, replica_groups=mesh['z'=8,'ylo'=2,'yhi'=4,'x'=4,'core'=2] {'yhi','x'}, dimensions={0} | all-to-all | bytes 65536 | tf_op jit(solution)/shard_map/all_to_all | solution.py:339
  71.4 0.3 shard_map.61
  71.7 11.9 %all_to_all.28.v1_ref = bf16[16,5,8,128]{3,2,1,0:T(8,128)(2,1)S(1)} all-to-all(bf16[16,5,8,128]{3,2,1,0:T(8,128)(2,1)S(1)} %shard_map.61), channel_id=1, replica_groups=mesh['z'=8,'ylo'=2,'yhi'=4,'x'=4,'core'=2] {'z','ylo'}, dimensions={0} | all-to-all | bytes 327680 | tf_op jit(solution)/shard_map/all_to_all | solution.py:351
  83.6 0.4 shard_map.62
  84.0 13.4 %all_to_all.29.x_ref = bf16[16,5,16,128]{3,2,1,0:T(8,128)(2,1)S(1)} all-to-all(bf16[16,5,16,128]{3,2,1,0:T(8,128)(2,1)S(1)} %shard_map.62), channel_id=1, replica_groups=mesh['z'=8,'ylo'=2,'yhi'=4,'x'=4,'core'=2] {'z','ylo'}, dimensions={0} | all-to-all | bytes 655360 | tf_op jit(solution)/shard_map/all_to_all | solution.py:361
  97.4 1.4 %shard_map.63 = bf16[5,64,8,128]{3,2,1,0:T(8,128)(2,1)} custom-call(bf16[16,5,16,128]{3,2,1,0:T(8,128)(2,1)S(1)} %all_to_all.29.x_ref, bf16[5,512,128]{2,1,0:T(8,128)(2,1)S(1)} %get-tuple-element.27.xt_ref, bf16[128,416]{1,0:T(8,128)(2,1)S(1)} %get-tuple-element.28.w_ref), custom_call_target="tpu_custom_call" | custom-call | flops 150000000 | bytes 1700000 | tf_op jit(solution)/shard_map/pallas_call | solution.py:33
  (4 shorter events, 0.1 us)
Async XLA Ops:
  0.0 1.1 %copy-start = (bf16[5,64,8,128]{3,2,1,0:T(8,128)(2,1)S(1)}, bf16[5,64,8,128]{3,2,1,0:T(8,128)(2,1)}, u32[]{:S(2)}) copy-start(bf16[5,64,8,128]{3,2,1,0:T(8,128)(2,1)} %f_ref.3) | copy-start | bytes 1966084
  1.1 7.1 %copy-start.1 = (bf16[64,216]{1,0:T(8,128)(2,1)S(1)}, bf16[64,216]{1,0:T(8,128)(2,1)}, u32[]{:S(2)}) copy-start(bf16[64,216]{1,0:T(8,128)(2,1)} %wo_ref.1) | copy-start | bytes 82948
  1.1 7.1 %copy-start.2 = (bf16[24,576]{1,0:T(8,128)(2,1)S(1)}, bf16[24,576]{1,0:T(8,128)(2,1)}, u32[]{:S(2)}) copy-start(bf16[24,576]{1,0:T(8,128)(2,1)} %wq_ref.1) | copy-start | bytes 82948
  1.1 7.1 %copy-start.3 = (bf16[24,576]{1,0:T(8,128)(2,1)S(1)}, bf16[24,576]{1,0:T(8,128)(2,1)}, u32[]{:S(2)}) copy-start(bf16[24,576]{1,0:T(8,128)(2,1)} %wk_ref.1) | copy-start | bytes 82948
  1.1 7.1 %copy-start.4 = (bf16[24,576]{1,0:T(8,128)(2,1)S(1)}, bf16[24,576]{1,0:T(8,128)(2,1)}, u32[]{:S(2)}) copy-start(bf16[24,576]{1,0:T(8,128)(2,1)} %wv_ref.1) | copy-start | bytes 82948
  1.3 11.0 %collective-permute-start = (bf16[5,128,128]{2,1,0:T(8,128)(2,1)S(1)}, bf16[5,128,128]{2,1,0:T(8,128)(2,1)S(1)}, u32[]{:S(2)}, u32[]{:S(2)}) collective-permute-start(bf16[5,128,128]{2,1,0:T(8,128)(2,1)S(1)} %get-tuple-element.23.nb_ref), channel_id=1, source_target_pairs={{0,31},{1,2},{2,1},{3,4},{4,3},{5,6},{6,5},{7,8},{8,7},{9,10},{10,... | collective-permute-start | bytes 491528 | tf_op jit(solution)/shard_map/ppermute | solution.py:272
